TPU v7x, 128 devices: a whole 4x4x4 slice. The times are simulated.
128 devices in a mesh: rows: 64 (over z, y, x), sub: 2 (over core).
Axes of the slice: x: 4, y: 4, z: 4, core: 2. Of those that a mesh axis runs over, the one named last changes fastest.
Arguments:
- points: bfloat16 [262144, 1024], P(('rows', 'sub')), may hold values from -192 to 192
- assign: int32 [262144], P(('rows', 'sub')), may hold values from 0 to 65535, as said below
- cluster_counts: int32 [65536], P(('rows', 'sub')), may hold values from 0 to 512, as said below
- centroids: float32 [65536, 1024], P(('rows', 'sub')), may hold values from -6 to 6
- codebook: float32 [8, 256, 128], P('sub'), may hold values from -8 to 8
Outputs:
- rebuilt: bfloat16 [262144, 1024], P(('rows', 'sub'))
- moved_centroids: float32 [65536, 1024], P(('rows', 'sub'))
- moved_codebook: float32 [8, 256, 128], P('sub')
Inputs may be any that keep to these rules, and one draw needn't show every extreme that they name: Within each device block (rows b * 2048 to (b + 1) * 2048 - 1) assign does not fall. The rows of device block b name clusters of centroid block b (clusters b * 512 to (b + 1) * 512 - 1), or of the top 64 clusters of block b - 1, or of the bottom 64 clusters of block b + 1; every device block except the first has 1 to 512 rows in the block below, every one except the last has 1 to 512 rows in the block above, and some device block has exactly 512 in the block below and some exactly 512 in the block above. cluster_counts[k] is the number of rows with assign = k; some cluster holds exactly 512 rows.
All inputs are finite; a program needn't handle non-finite values.
Results may differ from a plain program's by a relative error of at most 0.001.
The roundings to bfloat16 on the way count: a program that leaves them out, or rounds other values in their place, can miss the bound.
Values may be sent and summed in bfloat16 or wider, within the bound.
No kernel may reach another device: no remote copies, remote signals or barrier semaphores. Data moves between devices by JAX's collectives and lax.ppermute only.
A program may use at most 128 MiB of HBM per device.

v0:
```python
import math

import jax
import jax.numpy as jnp
from jax import lax
from jax.sharding import PartitionSpec as P

RIM = 64


def with_halo(cells, sides, width):
    for axis, dim in sides:
        count = lax.axis_size(axis)
        ends = count - 1
        head = lax.slice_in_dim(cells, 0, width, axis=dim)
        tail = lax.slice_in_dim(cells, cells.shape[dim] - width, cells.shape[dim], axis=dim)
        cells = jnp.concatenate(
            [
                lax.ppermute(tail, axis, [(i, (i + 1) % count) for i in range(ends)]),
                cells,
                lax.ppermute(head, axis, [((i + 1) % count, i) for i in range(ends)]),
            ],
            axis=dim,
        )
    return cells


def quantize(flat_rows, code_books):
    row_count, row_width = flat_rows.shape
    sub_count, code_count, subdim = code_books.shape
    grouped = flat_rows.reshape(row_count, sub_count, subdim)
    books_low = code_books.astype(jnp.bfloat16)
    dot_terms = jnp.einsum("gjd,jcd->gjc", grouped, books_low, preferred_element_type=jnp.float32)
    code_norm = jnp.sum(code_books * code_books, axis=-1)
    logits = (2.0 * dot_terms - code_norm[None, :, :]) / math.sqrt(subdim)
    weights = jax.nn.softmax(logits, axis=-1)
    weights_low = weights.astype(jnp.bfloat16)
    rebuilt = jnp.einsum("gjc,jcd->gjd", weights_low, books_low, preferred_element_type=jnp.float32)
    rebuilt = rebuilt.astype(jnp.bfloat16).reshape(row_count, row_width)
    totals = jnp.einsum("gjc,gjd->jcd", weights_low, grouped, preferred_element_type=jnp.float32)
    code_mass = jnp.sum(weights, axis=0)
    return (rebuilt, totals, code_mass)


def body(points, assign, cluster_counts, centroids, codebook):
    shard_len = centroids.shape[0]
    rows_here = points.shape[0]
    position = lax.axis_index(("rows", "sub"))
    window = with_halo(centroids, ((("rows", "sub"), 0),), RIM)
    local_ids = assign - (position * shard_len - RIM)
    cent_rows = jnp.take(window, local_ids, axis=0)
    residual = (points.astype(jnp.float32) - cent_rows).astype(jnp.bfloat16)
    slot_count = shard_len + 2 * RIM
    onehot = (
        lax.broadcasted_iota(jnp.int32, (slot_count, rows_here), 0) == local_ids[None, :]
    ).astype(jnp.bfloat16)
    part_sums = jnp.dot(onehot, points, preferred_element_type=jnp.float32)
    spread = with_halo(part_sums.astype(jnp.bfloat16), ((("rows", "sub"), 0),), RIM).astype(
        part_sums.dtype
    )
    own_sums = part_sums[RIM : RIM + shard_len]
    own_sums = own_sums.at[:RIM].add(spread[:RIM])
    own_sums = own_sums.at[shard_len - RIM :].add(spread[spread.shape[0] - RIM :])
    counts_real = cluster_counts.astype(jnp.float32)
    moved_centroids = (own_sums + 2.0 * centroids) / (counts_real + 2.0)[:, None]
    rows_all = rows_here * lax.axis_size("rows") * lax.axis_size("sub")
    prior_mass = rows_all / codebook.shape[1]
    grouped_rows = lax.all_to_all(residual, "sub", split_axis=1, concat_axis=0, tiled=True)
    rebuilt_group, totals, code_mass = quantize(grouped_rows, codebook)
    totals, code_mass = lax.psum((totals, code_mass), "rows")
    moved_codebook = (totals + prior_mass * codebook) / (code_mass + prior_mass)[:, :, None]
    rebuilt = lax.all_to_all(rebuilt_group, "sub", split_axis=0, concat_axis=1, tiled=True)
    return (rebuilt, moved_centroids, moved_codebook)


def solution(mesh):
    placed = (
        P(("rows", "sub"), None),
        P(("rows", "sub")),
        P(("rows", "sub")),
        P(("rows", "sub"), None),
        P("sub", None, None),
    )
    return jax.shard_map(
        body,
        mesh=mesh,
        in_specs=placed,
        out_specs=(P(("rows", "sub"), None), P(("rows", "sub"), None), P("sub", None, None)),
        check_vma=False,
    )
```

profile of v0, /device:TPU:0, one launch (start us, length us, event | category | flops | bytes accessed | tf_op | source)
XLA Modules:
  0.0 353.9 jit_solution(3689900348104379707)
XLA Ops:
  7.2 0.0 all-reduce.2.cloned.1.call-start
  7.2 1.1 fusion.24
  8.3 1.3 collective-permute-start.1
  9.6 3.7 %collective-permute-start = (f32[64,1024]{1,0:T(8,128)S(1)}, f32[64,1024]{1,0:T(8,128)}, u32[]{:S(2)}, u32[]{:S(2)}) collective-permute-start(f32[64,1024]{1,0:T(8,128)S(1)} %get-tuple-element.34), channel_id=1, source_target_pairs={{0,1},{1,2},{2,3},{3,4},{4,5},{5,6},{6,7},{7,8},{8,9},{9,10},{10,1... | collective-permute-start | bytes 786440 | tf_op jit(solution)/shard_map/ppermute | solution.py:19
  13.3 0.7 compare_and_fusion
  14.0 4.7 %fusion.27 = (bf16[640,1024]{1,0:T(8,128)(2,1)S(1)}, f32[640,1024]{1,0:T(8,128)S(1)}) fusion(bf16[2048,1024]{1,0:T(8,128)(2,1)} %param.9, s32[2048]{0:T(1024)S(1)} %get-tuple-element.31), kind=kOutput, calls=%fused_computation.47 | convolution fusion | flops 2686320640 | bytes 8134656 | tf_op jit(solution)/shard_map/dot_general | solution.py:57
  18.7 0.0 copy-start.4
  18.7 0.0 copy-start.3
  18.7 1.4 collective-permute-start.3
  20.2 3.1 collective-permute-start.2
  23.3 0.0 copy-start.2
  23.3 0.2 slice.71
  23.5 0.0 copy-done.4
  23.5 0.0 copy-done.3
  23.5 0.2 multiply_reduce_fusion
  23.8 0.0 collective-permute-done.3
  23.8 0.4 collective-permute-done.2
  24.2 0.1 fusion.17
  24.3 0.5 copy-done.2
  24.9 1.8 add_divide_fusion
  26.7 0.0 collective-permute-done.1
  26.7 0.0 collective-permute-done
  26.7 1.2 pad_maximum_fusion
  27.8 9.8 %gather_fusion = f32[2048,1024]{1,0:T(8,128)} fusion(f32[640,1024]{1,0:T(8,128)S(1)} %pad_maximum_fusion, s32[2048]{0:T(1024)S(1)} %fusion.21), kind=kCustom, calls=%fused_computation | custom fusion | bytes 16785408 | tf_op jit(solution)/shard_map/jit(_take)/gather | solution.py:51
  37.7 5.3 %subtract_convert_fusion = bf16[2048,1024]{1,0:T(8,128)(2,1)S(1)} fusion(f32[2048,1024]{1,0:T(8,128)} %gather_fusion, bf16[2048,1024]{1,0:T(8,128)(2,1)} %param.9, pred[2048]{0:T(1024)(128)(4,1)S(1)} %get-tuple-element.30), kind=kLoop, calls=%fused_computation.11 | loop fusion | flops 8388608 | bytes 16779264 | tf_op jit(solution)/shard_map/convert_element_type | solution.py:52
  42.9 0.3 copy.28
  43.3 9.8 %all_to_all.35 = bf16[2048,2,512]{2,0,1:T(8,128)(2,1)} all-to-all(bf16[2048,2,512]{2,0,1:T(8,128)(2,1)S(1)} %bitcast.24), channel_id=1, replica_groups=mesh['rows'=64,'sub'=2] {'sub'}, dimensions={1} | all-to-all | bytes 8388608 | tf_op jit(solution)/shard_map/all_to_all | solution.py:68
  53.0 6.9 %reshape.78 = bf16[4096,4,128]{2,1,0:T(4,128)(2,1)} reshape(bf16[2,2048,512]{2,1,0:T(8,128)(2,1)} %bitcast.25) | data formatting | bytes 8388608 | tf_op jit(solution)/shard_map/reshape | solution.py:31
  59.9 10.3 %fusion.14 = f32[4,4096,256]{1,2,0:T(8,128)} fusion(bf16[4096,4,128]{2,1,0:T(4,128)(2,1)} %reshape.78, f32[4,256,128]{2,1,0:T(8,128)S(1)} %copy-done.3), kind=kOutput, calls=%fused_computation.21 | convolution fusion | flops 1073872896 | bytes 21495808 | tf_op jit(solution)/shard_map/gjd,jcd->gjc/dot_general | solution.py:33
  70.2 20.0 %fusion.26 = (f32[4096,4]{0,1:T(4,128)S(1)}, f32[4096,4,256]{0,2,1:T(8,128)}) fusion(f32[4,4096,256]{1,2,0:T(8,128)} %fusion.14, f32[4,256]{1,0:T(4,128)S(1)} %multiply_reduce_fusion), kind=kOutput, calls=%fused_computation.46 | output fusion | flops 33554688 | bytes 33624064 | tf_op jit(solution)/shard_map/sub | solution.py:36
  90.2 0.0 copy-start.1
  90.2 7.5 %fusion.8 = (f32[4,256]{1,0:T(4,128)S(1)}, bf16[4096,4,256]{0,2,1:T(8,128)(2,1)S(1)}) fusion(f32[4096,4,256]{0,2,1:T(8,128)} %get-tuple-element.39, f32[4096,4]{0,1:T(4,128)S(1)} %get-tuple-element.38), kind=kLoop, calls=%fused_computation.12 | loop fusion | flops 12581888 | bytes 25235456 | tf_op jit(solution)/shard_map/reduce_sum | solution.py:41
  97.8 0.0 copy-start
  97.8 3.2 copy-done
  101.0 0.0 copy-done.1
  101.0 3.3 fusion.12
  104.3 0.0 all-reduce.2.cloned.1.call-update
  104.3 6.5 %fusion.10 = bf16[4096,4,128]{2,0,1:T(8,128)(2,1)S(1)} fusion(bf16[4096,4,256]{0,2,1:T(8,128)(2,1)} %copy-done, f32[4,256,128]{2,1,0:T(8,128)S(1)} %copy-done.3), kind=kOutput, calls=%fused_computation.15 | convolution fusion | flops 1075970048 | bytes 13107200 | tf_op jit(solution)/shard_map/gjc,jcd->gjd/dot_general | solution.py:38
  110.8 20.4 %copy.17 = bf16[4096,4,128]{2,1,0:T(4,128)(2,1)} copy(bf16[4096,4,128]{2,0,1:T(8,128)(2,1)S(1)} %fusion.10) | data formatting | bytes 8388608 | tf_op jit(solution)/shard_map/convert_element_type | solution.py:39
  131.3 7.2 %all_to_all.29 = bf16[2,2048,512]{2,1,0:T(8,128)(2,1)} reshape(bf16[4096,4,128]{2,1,0:T(4,128)(2,1)} %copy.17) | data formatting | bytes 8388608 | tf_op jit(solution)/shard_map/all_to_all | solution.py:72
  138.5 11.8 %all_to_all.36 = bf16[2,2048,512]{2,1,0:T(8,128)(2,1)} all-to-all(bf16[2,2048,512]{2,1,0:T(8,128)(2,1)} %all_to_all.29), channel_id=1, replica_groups=mesh['rows'=64,'sub'=2] {'sub'}, dimensions={0} | all-to-all | bytes 8388608 | tf_op jit(solution)/shard_map/all_to_all | solution.py:72
  150.3 6.3 %copy.18 = bf16[2048,2,512]{0,2,1:T(8,128)(2,1)} copy(bf16[2048,2,512]{2,0,1:T(8,128)(2,1)} %bitcast.26) | data formatting | bytes 8388608 | tf_op jit(solution)/shard_map/all_to_all | solution.py:72
  156.6 6.4 %copy.20 = bf16[2048,1024]{1,0:T(8,128)(2,1)} copy(bf16[2048,1024]{0,1:T(8,128)(2,1)} %bitcast.27) | data formatting | bytes 8388608
  163.0 182.0 %psum.15 = f32[4,256]{1,0:T(4,128)S(1)} all-reduce(f32[4,256]{1,0:T(4,128)S(1)} %get-tuple-element.32), channel_id=1, replica_groups=mesh['rows'=64,'sub'=2] {'rows'}, use_global_device_ids=true, to_apply=%region_5.6 | all-reduce | flops 1024 | bytes 8192 | tf_op jit(solution)/shard_map/psum | solution.py:70
  345.0 0.0 all-reduce.2.cloned.1.call-done
  345.0 2.0 add_divide_fusion.1
  (5 shorter events, 0.1 us)
Async XLA Ops:
  7.2 337.9 %all-reduce.2.cloned.1.call-start = ((), (), s32[]{:S(2)}) async-start(), calls=%async_computation.2 | async-start | bytes 1048576 | tf_op jit(solution)/shard_map/psum | solution.py:70
  8.3 18.4 %collective-permute-start.1 = (f32[64,1024]{1,0:T(8,128)S(1)}, f32[64,1024]{1,0:T(8,128)S(1)}, u32[]{:S(2)}, u32[]{:S(2)}) collective-permute-start(f32[64,1024]{1,0:T(8,128)S(1)} %get-tuple-element.35), channel_id=1, source_target_pairs={{1,0},{2,1},{3,2},{4,3},{5,4},{6,5},{7,6},{8,7},{9,8},{10,9},{11,1... | collective-permute-start | bytes 786440 | tf_op jit(solution)/shard_map/ppermute | solution.py:21
  9.6 17.1 %collective-permute-start = (f32[64,1024]{1,0:T(8,128)S(1)}, f32[64,1024]{1,0:T(8,128)}, u32[]{:S(2)}, u32[]{:S(2)}) collective-permute-start(f32[64,1024]{1,0:T(8,128)S(1)} %get-tuple-element.34), channel_id=1, source_target_pairs={{0,1},{1,2},{2,3},{3,4},{4,5},{5,6},{6,7},{7,8},{8,9},{9,10},{10,1... | collective-permute-start | bytes 786440 | tf_op jit(solution)/shard_map/ppermute | solution.py:19
  18.7 4.8 %copy-start.4 = (s32[512]{0:T(512)S(1)}, s32[512]{0:T(512)}, u32[]{:S(2)}) copy-start(s32[512]{0:T(512)} %param.11) | copy-start | bytes 6148
  18.7 4.8 %copy-start.3 = (f32[4,256,128]{2,1,0:T(8,128)S(1)}, f32[4,256,128]{2,1,0:T(8,128)}, u32[]{:S(2)}) copy-start(f32[4,256,128]{2,1,0:T(8,128)} %param.13) | copy-start | bytes 1572868
  18.7 5.0 %collective-permute-start.3 = (bf16[64,1024]{1,0:T(8,128)(2,1)S(1)}, bf16[64,1024]{1,0:T(8,128)(2,1)S(1)}, u32[]{:S(2)}, u32[]{:S(2)}) collective-permute-start(bf16[64,1024]{1,0:T(8,128)(2,1)S(1)} %get-tuple-element.37), channel_id=1, source_target_pairs={{1,0},{2,1},{3,2},{4,3},{5,4},{6,5},{7,6},{8,7},{9,8},{10,9},{11,1... | collective-permute-start | bytes 393224 | tf_op jit(solution)/shard_map/ppermute | solution.py:21
  20.2 4.0 %collective-permute-start.2 = (bf16[64,1024]{1,0:T(8,128)(2,1)S(1)}, bf16[64,1024]{1,0:T(8,128)(2,1)S(1)}, u32[]{:S(2)}, u32[]{:S(2)}) collective-permute-start(bf16[64,1024]{1,0:T(8,128)(2,1)S(1)} %get-tuple-element.36), channel_id=1, source_target_pairs={{0,1},{1,2},{2,3},{3,4},{4,5},{5,6},{6,7},{7,8},{8,9},{9,10},{10,1... | collective-permute-start | bytes 393224 | tf_op jit(solution)/shard_map/ppermute | solution.py:19
  23.3 1.6 copy-start.2
  90.2 10.8 %copy-start.1 = (bf16[4096,4,128]{2,1,0:T(4,128)(2,1)S(1)}, bf16[4096,4,128]{2,1,0:T(4,128)(2,1)}, u32[]{:S(2)}) copy-start(bf16[4096,4,128]{2,1,0:T(4,128)(2,1)} %reshape.78) | copy-start | bytes 12582916
  97.8 3.2 copy-start
Sparse Core Ops, SparseCore 0:
  104.4 138.7 all-reduce.1
where the time goes:
time: 355 us; the launch traced here: 354 us
  blocking collectives  204 us (57%)
  local copies, waits for them, and re-layouts  62.4 us (18%)
  other arithmetic  38.8 us (11%)
  matrix products  24.8 us (7%)
  between operations  14.2 us (4%)
  starting transfers between devices  9.55 us (3%)
    psum x1, blocking collectives, body(): totals, code_mass = lax.psum((totals, code_mass), 'rows')  182 us
    convert_element_type x1, local copies, waits for them, and re-layouts, quantize(): rebuilt = rebuilt.astype(jnp.bfloat16).reshape(row_count, row_width)  20.4 us
    sub x1, other arithmetic, quantize(): weights = jax.nn.softmax(logits, axis=-1)  20 us
    all_to_all x2, local copies, waits for them, and re-layouts, body(): lax.all_to_all(rebuilt_group, 'sub', split_axis=0, concat_axis=1, tiled=T...  13.5 us
    all_to_all x1, blocking collectives, body(): lax.all_to_all(rebuilt_group, 'sub', split_axis=0, concat_axis=1, tiled=T...  11.8 us
    dot_general x1, matrix products, quantize(): jnp.einsum('gjd,jcd->gjc', grouped, books_low, preferred_element_type=jnp...  10.3 us
    unnamed x11, local copies, waits for them, and re-layouts  10.2 us
    gather x1, local copies, waits for them, and re-layouts, body(): cent_rows = jnp.take(window, local_ids, axis=0)  9.81 us
  transfers between devices with their start and end apart: 5, of which 1 were waited for; matrix products, arithmetic and copies ran while one was open for 13% of the time, Pallas kernels for 0%

commit v1 on v0

v1 whole, which is shorter than its diff:
```python
import math

import jax
import jax.numpy as jnp
from jax import lax
from jax.experimental import pallas as pl
from jax.experimental.pallas import tpu as pltpu
from jax.sharding import PartitionSpec as P

RIM = 64
TILE = 128
STEP = 256
MESH_AXES = ("rows", "sub")
NN = (((1,), (0,)), ((), ()))
NT = (((1,), (1,)), ((), ()))
TN = (((0,), (0,)), ((), ()))


def row_of_ids(ids_ref, first, count, base):
    parts = [ids_ref[pl.ds(first + k, 1), :] for k in range(count)]
    return jnp.concatenate(parts, axis=1) - base


def picks(ids_row, tile):
    slots = lax.broadcasted_iota(jnp.int32, (TILE, ids_row.shape[1]), 0) + tile * TILE
    return (slots == ids_row).astype(jnp.float32).astype(jnp.bfloat16)


def tile_range(ids_smem, base, step):
    first = (ids_smem[step * STEP] - base) // TILE
    last = (ids_smem[step * STEP + STEP - 1] - base) // TILE
    return first, last


def sums_kernel(ids_smem, base_smem, ids_ref, points_ref, counts_ref, cent_ref, moved_ref, down_ref, up_ref, acc):
    step = pl.program_id(0)
    base = base_smem[0]

    @pl.when(step == 0)
    def _():
        acc[...] = jnp.zeros_like(acc)

    first, last = tile_range(ids_smem, base, step)
    ids_row = row_of_ids(ids_ref, step * (STEP // 128), STEP // 128, base)

    def add(tile, carry):
        at = pl.ds(pl.multiple_of(tile * TILE, TILE), TILE)
        acc[at, :] += lax.dot_general(picks(ids_row, tile), points_ref[...], NN, preferred_element_type=jnp.float32)
        return carry

    lax.fori_loop(first, last + 1, add, 0)

    @pl.when(step == pl.num_programs(0) - 1)
    def _():
        own = cent_ref.shape[0]
        down_ref[...] = acc[:RIM].astype(jnp.bfloat16)
        up_ref[...] = acc[RIM + own :].astype(jnp.bfloat16)
        for part in range(own // 128):
            count = jnp.broadcast_to(counts_ref[part : part + 1, :], (128, 128)).astype(jnp.float32)
            inverse = (1.0 / (count + 2.0)).T
            lo = 64 if part == 0 else 0
            hi = 64 if part == own // 128 - 1 else 128
            at = slice(part * 128 + lo, part * 128 + hi)
            for col in range(cent_ref.shape[1] // 128):
                cols = slice(col * 128, col * 128 + 128)
                moved_ref[at, cols] = (
                    acc[RIM + part * 128 + lo : RIM + part * 128 + hi, cols] + 2.0 * cent_ref[at, cols]
                ) * inverse[lo:hi]
        moved_ref[:RIM, :] = acc[RIM : 2 * RIM]
        moved_ref[own - RIM :, :] = acc[own : own + RIM]


def edge_kernel(moved_in, low_in, high_in, counts_ref, cent_ref, moved_ref):
    which = pl.program_id(0)
    row = jnp.where(which == 0, 0, counts_ref.shape[0] - 1)
    count = jnp.broadcast_to(counts_ref[pl.ds(row, 1), :], (128, 128)).astype(jnp.float32)
    inverse = (1.0 / (count + 2.0)).T
    inverse = jnp.where(which == 0, inverse[:RIM], inverse[RIM:])
    spread = jnp.where(which == 0, low_in[...].astype(jnp.float32), high_in[...].astype(jnp.float32))
    for col in range(cent_ref.shape[1] // 128):
        cols = slice(col * 128, col * 128 + 128)
        moved_ref[:, cols] = (moved_in[:, cols] + spread[:, cols] + 2.0 * cent_ref[:, cols]) * inverse


def quant_kernel(
    ids_smem, base_smem, ids_ref, points_ref, cent_ref, low_ref, high_ref, books_ref,
    rebuilt_ref, payload_ref, window3, gathered, resid, books_low, books_t, norms, totals, mass,
):
    step = pl.program_id(0)
    base = base_smem[0]
    subs, codes, subdim = books_ref.shape
    rate = 1.0 / (math.sqrt(subdim) * math.log(2.0))
    own = cent_ref.shape[0]

    @pl.when(step == 0)
    def _():
        def split(value, tile, at):
            hi = value.astype(jnp.bfloat16)
            rest = value - hi.astype(jnp.float32)
            mid = rest.astype(jnp.bfloat16)
            lo = (rest - mid.astype(jnp.float32)).astype(jnp.bfloat16)
            count = value.shape[0]
            for k, piece in enumerate((hi, mid, lo)):
                window3[tile, k * TILE + at : k * TILE + at + count, :] = piece

        split(low_ref[...], 0, 0)
        split(high_ref[...], window3.shape[0] - 1, RIM)
        for part in range(own // RIM):
            tile, at = divmod(part + 1, TILE // RIM)
            split(cent_ref[part * RIM : part * RIM + RIM, :], tile, at * RIM)
        for j in range(subs):
            words = books_ref[j]
            low = words.astype(jnp.bfloat16)
            books_low[j] = low
            books_t[j] = words.T.astype(jnp.bfloat16)
            norm = jnp.sum(words * words, axis=1, keepdims=True) * rate
            norms[j] = jnp.broadcast_to(norm, (codes, 128))
        totals[...] = jnp.zeros_like(totals)
        mass[...] = jnp.zeros_like(mass)

    first, last = tile_range(ids_smem, base, step)
    ids_row = row_of_ids(ids_ref, step * (STEP // 128), STEP // 128, base)

    def fetch(tile):
        pick = picks(ids_row, tile)
        pick3 = jnp.concatenate([pick, pick, pick], axis=0)
        return lax.dot_general(pick3, window3[tile], TN, preferred_element_type=jnp.float32)

    gathered[...] = fetch(first)

    def more(tile, carry):
        gathered[...] += fetch(tile)
        return carry

    lax.fori_loop(first + 1, last + 1, more, 0)
    resid[...] = (points_ref[...].astype(jnp.float32) - gathered[...]).astype(jnp.bfloat16)

    for j in range(subs):
        cols = slice(j * subdim, (j + 1) * subdim)
        rows_j = resid[:, cols]
        dots = lax.dot_general(books_low[j], rows_j, NT, preferred_element_type=jnp.float32)
        weights_low = []
        for part in range(STEP // 128):
            lanes = slice(part * 128, part * 128 + 128)
            logits = dots[:, lanes] * (2.0 * rate) - norms[j]
            top = jnp.max(logits, axis=0, keepdims=True)
            raised = jnp.exp2(logits - top)
            weights = raised * (1.0 / jnp.sum(raised, axis=0, keepdims=True))
            mass[j] += weights
            weights_low.append(weights.astype(jnp.bfloat16))
        weights_low = jnp.concatenate(weights_low, axis=1)
        totals[j] += lax.dot_general(weights_low, rows_j, NN, preferred_element_type=jnp.float32)
        rebuilt_t = lax.dot_general(books_t[j], weights_low, NN, preferred_element_type=jnp.float32)
        rebuilt_ref[:, cols] = rebuilt_t.T.astype(jnp.bfloat16)

    @pl.when(step == pl.num_programs(0) - 1)
    def _():
        half = subs // 2
        group = codes * half // payload_ref.shape[1]
        left = lax.broadcasted_iota(jnp.int32, (8, 128), 1) < 64
        for j in range(subs):
            for g in range(codes // group):
                at = slice(g * group, g * group + group)
                slot = (j % half) * (codes // group) + g
                payload_ref[j // half, slot, :group, :] = totals[j, at, :]
                part = mass[j, at, :]
                part = part + pltpu.roll(part, 64, 1)
                payload_ref[j // half, slot, group:, :] = jnp.where(left, part[:8], part[8:])


def reduce_kernel(prior, parts_ref, book_ref, out_ref):
    total = jnp.sum(parts_ref[...], axis=0)
    group = book_ref.shape[0]
    left = lax.broadcasted_iota(jnp.int32, (8, 128), 1) < 64
    packed = total[group:]
    mass = jnp.concatenate(
        [
            jnp.sum(jnp.where(left, packed, 0.0), axis=1, keepdims=True),
            jnp.sum(jnp.where(left, 0.0, packed), axis=1, keepdims=True),
        ],
        axis=0,
    )
    moved = (total[:group] + prior * book_ref[...]) / (mass + prior)
    out_ref[...] = jnp.broadcast_to(moved[None], out_ref.shape)


def whole(shape):
    return pl.BlockSpec(shape, lambda *_: (0,) * len(shape))


def body(points, assign, cluster_counts, centroids, codebook):
    own, width = centroids.shape
    rows_here = points.shape[0]
    half, codes, subdim = codebook.shape
    rows_axis, sub_axis = MESH_AXES
    owners = lax.axis_size(rows_axis)
    places = owners * lax.axis_size(sub_axis)
    sub = lax.axis_index(sub_axis)
    position = lax.axis_index(rows_axis) * lax.axis_size(sub_axis) + sub
    base = jnp.reshape(position * own - RIM, (1,)).astype(jnp.int32)
    up = [(i, i + 1) for i in range(places - 1)]
    down = [(i + 1, i) for i in range(places - 1)]
    swap = [(0, 1), (1, 0)]
    low = lax.ppermute(centroids[own - RIM :], MESH_AXES, up)
    high = lax.ppermute(centroids[:RIM], MESH_AXES, down)
    other_book = lax.ppermute(codebook, sub_axis, swap)
    ids = assign.reshape(rows_here // 128, 128)
    counts = cluster_counts.reshape(own // 128, 128)
    steps = rows_here // STEP
    slots = own + 2 * RIM
    tile_rows = pl.BlockSpec((STEP, width), lambda i, *_: (i, 0))
    params = pltpu.CompilerParams(vmem_limit_bytes=56 * 1024 * 1024)

    sums, sum_down, sum_up = pl.pallas_call(
        sums_kernel,
        grid_spec=pltpu.PrefetchScalarGridSpec(
            num_scalar_prefetch=2,
            grid=(steps,),
            in_specs=[whole(ids.shape), tile_rows, whole(counts.shape), whole(centroids.shape)],
            out_specs=[whole(centroids.shape), whole((RIM, width)), whole((RIM, width))],
            scratch_shapes=[pltpu.VMEM((slots, width), jnp.float32)],
        ),
        out_shape=[
            jax.ShapeDtypeStruct(centroids.shape, jnp.float32),
            jax.ShapeDtypeStruct((RIM, width), jnp.bfloat16),
            jax.ShapeDtypeStruct((RIM, width), jnp.bfloat16),
        ],
        compiler_params=params,
        cost_estimate=pl.CostEstimate(flops=2 * 10**9, bytes_accessed=8 * 10**6, transcendentals=0),
        name="cluster_sums",
    )(assign, base, ids, points, counts, centroids)

    sum_low = lax.ppermute(sum_up, MESH_AXES, up)
    sum_high = lax.ppermute(sum_down, MESH_AXES, down)

    books = jnp.where(
        sub == 0,
        jnp.concatenate([codebook, other_book], axis=0),
        jnp.concatenate([other_book, codebook], axis=0),
    )
    subs = 2 * half
    group = half * codes // owners
    rebuilt, payload = pl.pallas_call(
        quant_kernel,
        grid_spec=pltpu.PrefetchScalarGridSpec(
            num_scalar_prefetch=2,
            grid=(steps,),
            in_specs=[
                whole(ids.shape), tile_rows, whole(centroids.shape),
                whole((RIM, width)), whole((RIM, width)), whole(books.shape),
            ],
            out_specs=[tile_rows, whole((2, owners, group + 8, subdim))],
            scratch_shapes=[
                pltpu.VMEM((slots // TILE, 3 * TILE, width), jnp.bfloat16),
                pltpu.VMEM((STEP, width), jnp.float32),
                pltpu.VMEM((STEP, width), jnp.bfloat16),
                pltpu.VMEM((subs, codes, subdim), jnp.bfloat16),
                pltpu.VMEM((subs, subdim, codes), jnp.bfloat16),
                pltpu.VMEM((subs, codes, 128), jnp.float32),
                pltpu.VMEM((subs, codes, subdim), jnp.float32),
                pltpu.VMEM((subs, codes, 128), jnp.float32),
            ],
        ),
        out_shape=[
            jax.ShapeDtypeStruct(points.shape, jnp.bfloat16),
            jax.ShapeDtypeStruct((2, owners, group + 8, subdim), jnp.float32),
        ],
        compiler_params=params,
        cost_estimate=pl.CostEstimate(flops=8 * 10**9, bytes_accessed=12 * 10**6, transcendentals=4 * 10**6),
        name="quantize",
    )(assign, base, ids, points, centroids, low, high, books)

    edge = pl.BlockSpec((RIM, width), lambda i: (i * (own // RIM - 1), 0))
    moved_centroids = pl.pallas_call(
        edge_kernel,
        grid=(2,),
        in_specs=[edge, whole((RIM, width)), whole((RIM, width)), whole(counts.shape), edge],
        out_specs=edge,
        out_shape=jax.ShapeDtypeStruct(centroids.shape, jnp.float32),
        input_output_aliases={0: 0},
        name="edge_clusters",
    )(sums, sum_low, sum_high, counts, centroids)

    mine = lax.dynamic_index_in_dim(payload, sub, 0, keepdims=False)
    theirs = lax.dynamic_index_in_dim(payload, 1 - sub, 0, keepdims=False)
    chip = mine + lax.ppermute(theirs, sub_axis, swap)
    parts = lax.all_to_all(chip, rows_axis, 0, 0, tiled=True)
    book_rows = lax.dynamic_slice_in_dim(
        codebook.reshape(half * codes, subdim), lax.axis_index(rows_axis) * group, group, 0
    )
    prior = rows_here * places / codes
    moved = pl.pallas_call(
        lambda *refs: reduce_kernel(prior, *refs),
        out_shape=jax.ShapeDtypeStruct((owners, group, subdim), jnp.float32),
        name="moved_codes",
    )(parts, book_rows)
    moved = lax.all_to_all(moved, rows_axis, 0, 0, tiled=True)
    return (rebuilt, moved_centroids, moved.reshape(codebook.shape))


def solution(mesh):
    both = P(("rows", "sub"), None)
    flat = P(("rows", "sub"))
    books = P("sub", None, None)
    return jax.shard_map(
        body,
        mesh=mesh,
        in_specs=(both, flat, flat, both, books),
        out_specs=(both, both, books),
        check_vma=False,
    )
```

time: 355 us -> 119 us (0.34)
  the two profiles are of different devices: /device:TPU:0 before, /device:TPU:31 now
where the time goes in v1:
time: 119 us
  Pallas kernels  48.1 us (40%)
  starting transfers between devices  30.8 us (26%)
  waiting for transfers between devices  28.9 us (24%)
  local copies, waits for them, and re-layouts  6.72 us (6%)
  other arithmetic  3.23 us (3%)
    pallas_call x1, Pallas kernels, body(): pl.pallas_call(quant_kernel, grid_spec=pltpu.PrefetchScalarGridSpec(num_s...  33.9 us
    all_to_all x1, waiting for transfers between devices, body(): parts = lax.all_to_all(chip, rows_axis, 0, 0, tiled=True)  10.2 us
    pallas_call x1, Pallas kernels, body(): pl.pallas_call(sums_kernel, grid_spec=pltpu.PrefetchScalarGridSpec(num_sc...  9.93 us
    all_to_all x1, starting transfers between devices, body(): parts = lax.all_to_all(chip, rows_axis, 0, 0, tiled=True)  9.64 us
    all_to_all x1, starting transfers between devices, body(): moved = lax.all_to_all(moved, rows_axis, 0, 0, tiled=True)  8.6 us
    ppermute x1, waiting for transfers between devices, body(): sum_high = lax.ppermute(sum_down, MESH_AXES, down)  8.47 us
    ppermute x1, waiting for transfers between devices, body(): high = lax.ppermute(centroids[:RIM], MESH_AXES, down)  7.68 us
    ppermute x1, starting transfers between devices, body(): sum_low = lax.ppermute(sum_up, MESH_AXES, up)  4.89 us
  transfers between devices with their start and end apart: 8, of which 5 were waited for; matrix products, arithmetic and copies ran while one was open for 4% of the time, Pallas kernels for 10%

profile of v1, /device:TPU:31, one launch (start us, length us, event | category | flops | bytes accessed | tf_op | source)
XLA Modules:
  0.0 118.6 jit_solution(16631606892429341647)
XLA Ops:
  0.6 0.8 collective-permute-start.2
  1.4 1.1 fusion
  2.5 3.0 %collective-permute-start = (f32[64,1024]{1,0:T(8,128)S(1)}, f32[64,1024]{1,0:T(8,128)S(1)}, u32[]{:S(2)}, u32[]{:S(2)}) collective-permute-start(f32[64,1024]{1,0:T(8,128)S(1)} %get-tuple-element.14), channel_id=1, source_target_pairs={{0,1},{1,2},{2,3},{3,4},{4,5},{5,6},{6,7},{7,8},{8,9},{9,10},{10,1... | collective-permute-start | bytes 786440 | tf_op jit(solution)/shard_map/ppermute | solution.py:204
  5.5 1.9 %collective-permute-start.1 = (f32[64,1024]{1,0:T(8,128)S(1)}, f32[64,1024]{1,0:T(8,128)S(1)}, u32[]{:S(2)}, u32[]{:S(2)}) collective-permute-start(f32[64,1024]{1,0:T(8,128)S(1)} %get-tuple-element.13), channel_id=1, source_target_pairs={{1,0},{2,1},{3,2},{4,3},{5,4},{6,5},{7,6},{8,7},{9,8},{10,9},{11,1... | collective-permute-start | bytes 786440 | tf_op jit(solution)/shard_map/ppermute | solution.py:205
  7.4 0.0 collective-permute-done.2
  7.4 2.3 %maximum_select_fusion.books_ref = f32[8,256,128]{2,1,0:T(8,128)} fusion(f32[4,256,128]{2,1,0:T(8,128)S(1)} %collective-permute-done.2, f32[4,256,128]{2,1,0:T(8,128)} %param.9, pred[]{:T(512)S(6)} %eq.3), kind=kLoop, calls=%fused_computation | loop fusion | flops 786432 | bytes 2097153 | tf_op jit(solution)/shard_map/jit(_where)/select_n | solution.py:236
  9.7 0.0 collective-permute-done.low_ref
  9.7 0.0 copy-start.4
  9.7 7.7 %collective-permute-done.1.high_ref = f32[64,1024]{1,0:T(8,128)S(1)} collective-permute-done((f32[64,1024]{1,0:T(8,128)S(1)}, f32[64,1024]{1,0:T(8,128)S(1)}, u32[]{:S(2)}, u32[]{:S(2)}) %collective-permute-start.1) | collective-permute-done | bytes 262176 | tf_op jit(solution)/shard_map/ppermute | solution.py:205
  17.4 0.0 copy-start.5
  17.4 0.0 copy-done.4
  17.4 0.7 copy-done.5
  18.1 33.9 %quantize.1 = (bf16[2048,1024]{1,0:T(8,128)(2,1)}, f32[2,64,24,128]{3,2,1,0:T(8,128)}) custom-call(s32[2048]{0:T(1024)} %ids_smem.3, s32[1]{0:T(128)} %bitcast.base_smem, s32[16,128]{1,0:T(8,128)} %bitcast.13, bf16[2048,1024]{1,0:T(8,128)(2,1)} %points_ref.3, f32[512,1024]{1,0:T(8,128)} %cent_ref.5, f32[64,1024]{1,0:T(8,128)} %copy-done.4, ...), custom_call_target="tpu_custom_call" | custom-call | flops 8000000000 | bytes 12000000 | tf_op jit(solution)/shard_map/quantize/pallas_call | solution.py:243
  52.0 0.0 copy-start.1
  52.0 1.3 %dynamic-slice_bitcast_fusion = f32[64,24,128]{2,1,0:T(8,128)S(1)} fusion(f32[2,64,24,128]{3,2,1,0:T(8,128)} %get-tuple-element.12, s32[]{:T(128)S(6)} %select_n.21), kind=kLoop, calls=%fused_computation.2 | loop fusion | bytes 1572868 | tf_op jit(solution)/shard_map/jit(dynamic_index_in_dim)/squeeze | solution.py:285
  53.3 0.1 collective-permute-start.5
  53.4 2.3 %collective-permute-done.5 = f32[64,24,128]{2,1,0:T(8,128)S(1)} collective-permute-done((f32[64,24,128]{2,1,0:T(8,128)S(1)}, f32[64,24,128]{2,1,0:T(8,128)S(1)}, u32[]{:S(2)}, u32[]{:S(2)}) %collective-permute-start.5) | collective-permute-done | bytes 786464 | tf_op jit(solution)/shard_map/ppermute | solution.py:286
  55.7 0.0 copy-done.1
  55.7 1.0 bitcast_add_fusion
  56.7 9.6 %all-to-all-start = ((f32[64,24,128]{2,1,0:T(8,128)}), f32[64,24,128]{2,1,0:T(8,128)S(1)}, u32[]{:S(2)}, u32[]{:S(2)}) async-start(f32[64,24,128]{2,1,0:T(8,128)} %bitcast_add_fusion), calls=%async_computation | async-start | bytes 1572864 | tf_op jit(solution)/shard_map/all_to_all | solution.py:287
  66.3 1.3 %constant_dynamic-slice_fusion.refs_1_ = f32[16,128]{1,0:T(8,128)} fusion(f32[1024,128]{1,0:T(8,128)} %bitcast.10, s32[]{:T(128)S(6)} %select_n.22), kind=kLoop, calls=%fused_computation.3 | loop fusion | bytes 16388 | tf_op jit(solution)/shard_map/dynamic_slice | solution.py:288
  67.6 10.2 %all-to-all-done.refs_0_ = f32[64,24,128]{2,1,0:T(8,128)S(1)} async-done(((f32[64,24,128]{2,1,0:T(8,128)}), f32[64,24,128]{2,1,0:T(8,128)S(1)}, u32[]{:S(2)}, u32[]{:S(2)}) %all-to-all-start) | async-done | bytes 786464 | tf_op jit(solution)/shard_map/all_to_all | solution.py:287
  77.8 0.0 copy-start
  77.8 0.9 copy-done
  78.7 2.2 %moved_codes.1 = f32[64,16,128]{2,1,0:T(8,128)} custom-call(f32[64,24,128]{2,1,0:T(8,128)} %copy-done, f32[16,128]{1,0:T(8,128)} %constant_dynamic-slice_fusion.refs_1_), custom_call_target="tpu_custom_call" | custom-call | tf_op jit(solution)/shard_map/moved_codes/pallas_call | solution.py:292
  80.8 8.6 %all-to-all-start.1 = ((f32[64,16,128]{2,1,0:T(8,128)}), f32[64,16,128]{2,1,0:T(8,128)S(1)}, u32[]{:S(2)}, u32[]{:S(2)}) async-start(f32[64,16,128]{2,1,0:T(8,128)} %moved_codes.1), calls=%async_computation.1 | async-start | bytes 1048576 | tf_op jit(solution)/shard_map/all_to_all | solution.py:297
  89.5 9.9 %cluster_sums.1 = (f32[512,1024]{1,0:T(8,128)}, bf16[64,1024]{1,0:T(8,128)(2,1)}, bf16[64,1024]{1,0:T(8,128)(2,1)}) custom-call(s32[2048]{0:T(1024)} %ids_smem.3, s32[1]{0:T(128)} %bitcast.base_smem, s32[16,128]{1,0:T(8,128)} %bitcast.14, bf16[2048,1024]{1,0:T(8,128)(2,1)} %points_ref.3, s32[4,128]{1,0:T(4,128)} %bitcast.11, f32[512,1024]{1,0:T(8,128)} %cent_ref.5), custom_call_target="tpu_custom_call" | custom-call | flops 2000000000 | bytes 8000000 | tf_op jit(solution)/shard_map/cluster_sums/pallas_call | solution.py:214
  99.4 4.9 %collective-permute-start.3 = (bf16[64,1024]{1,0:T(8,128)(2,1)}, bf16[64,1024]{1,0:T(8,128)(2,1)S(1)}, u32[]{:S(2)}, u32[]{:S(2)}) collective-permute-start(bf16[64,1024]{1,0:T(8,128)(2,1)} %get-tuple-element.10), channel_id=1, source_target_pairs={{0,1},{1,2},{2,3},{3,4},{4,5},{5,6},{6,7},{7,8},{8,9},{9,10},{10,1... | collective-permute-start | bytes 393224 | tf_op jit(solution)/shard_map/ppermute | solution.py:233
  104.3 1.9 %collective-permute-start.4 = (bf16[64,1024]{1,0:T(8,128)(2,1)}, bf16[64,1024]{1,0:T(8,128)(2,1)S(1)}, u32[]{:S(2)}, u32[]{:S(2)}) collective-permute-start(bf16[64,1024]{1,0:T(8,128)(2,1)} %get-tuple-element.11), channel_id=1, source_target_pairs={{1,0},{2,1},{3,2},{4,3},{5,4},{6,5},{7,6},{8,7},{9,8},{10,9},{11,1... | collective-permute-start | bytes 393224 | tf_op jit(solution)/shard_map/ppermute | solution.py:234
  106.2 0.3 collective-permute-done.3.low_in
  106.5 0.0 copy-start.2
  106.5 8.5 %collective-permute-done.4.high_in = bf16[64,1024]{1,0:T(8,128)(2,1)S(1)} collective-permute-done((bf16[64,1024]{1,0:T(8,128)(2,1)}, bf16[64,1024]{1,0:T(8,128)(2,1)S(1)}, u32[]{:S(2)}, u32[]{:S(2)}) %collective-permute-start.4) | collective-permute-done | bytes 131104 | tf_op jit(solution)/shard_map/ppermute | solution.py:234
  115.0 0.0 copy-start.3
  115.0 0.0 copy-done.2
  115.0 0.7 copy-done.3
  115.7 2.1 %edge_clusters.1 = f32[512,1024]{1,0:T(8,128)} custom-call(f32[512,1024]{1,0:T(8,128)} %get-tuple-element.9.moved_in, bf16[64,1024]{1,0:T(8,128)(2,1)} %copy-done.2, bf16[64,1024]{1,0:T(8,128)(2,1)} %copy-done.3, s32[4,128]{1,0:T(4,128)} %bitcast.12, f32[512,1024]{1,0:T(8,128)} %cent_ref.5), custom_call_target="tpu_custom_call", output_to_operand_aliasing={{}: (0, {})} | custom-call | tf_op jit(solution)/shard_map/edge_clusters/pallas_call | solution.py:274
  117.8 0.0 all-to-all-done.1
  117.8 0.8 copy.11
Async XLA Ops:
  0.6 6.8 %collective-permute-start.2 = (f32[4,256,128]{2,1,0:T(8,128)}, f32[4,256,128]{2,1,0:T(8,128)S(1)}, u32[]{:S(2)}, u32[]{:S(2)}) collective-permute-start(f32[4,256,128]{2,1,0:T(8,128)} %param.9), channel_id=1, source_target_pairs={{0,1},{1,0},{2,3},{3,2},{4,5},{5,4},{6,7},{7,6},{8,9},{9,8},{10,11... | collective-permute-start | bytes 1572872 | tf_op jit(solution)/shard_map/ppermute | solution.py:206
  2.5 7.3 %collective-permute-start = (f32[64,1024]{1,0:T(8,128)S(1)}, f32[64,1024]{1,0:T(8,128)S(1)}, u32[]{:S(2)}, u32[]{:S(2)}) collective-permute-start(f32[64,1024]{1,0:T(8,128)S(1)} %get-tuple-element.14), channel_id=1, source_target_pairs={{0,1},{1,2},{2,3},{3,4},{4,5},{5,6},{6,7},{7,8},{8,9},{9,10},{10,1... | collective-permute-start | bytes 786440 | tf_op jit(solution)/shard_map/ppermute | solution.py:204
  5.5 11.9 %collective-permute-start.1 = (f32[64,1024]{1,0:T(8,128)S(1)}, f32[64,1024]{1,0:T(8,128)S(1)}, u32[]{:S(2)}, u32[]{:S(2)}) collective-permute-start(f32[64,1024]{1,0:T(8,128)S(1)} %get-tuple-element.13), channel_id=1, source_target_pairs={{1,0},{2,1},{3,2},{4,3},{5,4},{6,5},{7,6},{8,7},{9,8},{10,9},{11,1... | collective-permute-start | bytes 786440 | tf_op jit(solution)/shard_map/ppermute | solution.py:205
  9.7 7.7 %copy-start.4 = (f32[64,1024]{1,0:T(8,128)}, f32[64,1024]{1,0:T(8,128)S(1)}, u32[]{:S(2)}) copy-start(f32[64,1024]{1,0:T(8,128)S(1)} %collective-permute-done.low_ref) | copy-start | bytes 786436
  17.4 0.7 copy-start.5
  52.0 3.7 %copy-start.1 = (f32[2,64,24,128]{3,2,1,0:T(8,128)S(1)}, f32[2,64,24,128]{3,2,1,0:T(8,128)}, u32[]{:S(2)}) copy-start(f32[2,64,24,128]{3,2,1,0:T(8,128)} %get-tuple-element.12) | copy-start | bytes 4718596
  53.3 2.4 %collective-permute-start.5 = (f32[64,24,128]{2,1,0:T(8,128)S(1)}, f32[64,24,128]{2,1,0:T(8,128)S(1)}, u32[]{:S(2)}, u32[]{:S(2)}) collective-permute-start(f32[64,24,128]{2,1,0:T(8,128)S(1)} %dynamic-slice_bitcast_fusion), channel_id=1, source_target_pairs={{0,1},{1,0},{2,3},{3,2},{4,5},{5,4},{6,7},{7,6},{8,9},{9,8},{10,11... | collective-permute-start | bytes 2359304 | tf_op jit(solution)/shard_map/ppermute | solution.py:286
  56.7 21.1 %all-to-all-start = ((f32[64,24,128]{2,1,0:T(8,128)}), f32[64,24,128]{2,1,0:T(8,128)S(1)}, u32[]{:S(2)}, u32[]{:S(2)}) async-start(f32[64,24,128]{2,1,0:T(8,128)} %bitcast_add_fusion), calls=%async_computation | async-start | bytes 1572864 | tf_op jit(solution)/shard_map/all_to_all | solution.py:287
  77.8 0.9 copy-start
  80.8 36.9 %all-to-all-start.1 = ((f32[64,16,128]{2,1,0:T(8,128)}), f32[64,16,128]{2,1,0:T(8,128)S(1)}, u32[]{:S(2)}, u32[]{:S(2)}) async-start(f32[64,16,128]{2,1,0:T(8,128)} %moved_codes.1), calls=%async_computation.1 | async-start | bytes 1048576 | tf_op jit(solution)/shard_map/all_to_all | solution.py:297
  99.4 7.1 %collective-permute-start.3 = (bf16[64,1024]{1,0:T(8,128)(2,1)}, bf16[64,1024]{1,0:T(8,128)(2,1)S(1)}, u32[]{:S(2)}, u32[]{:S(2)}) collective-permute-start(bf16[64,1024]{1,0:T(8,128)(2,1)} %get-tuple-element.10), channel_id=1, source_target_pairs={{0,1},{1,2},{2,3},{3,4},{4,5},{5,6},{6,7},{7,8},{8,9},{9,10},{10,1... | collective-permute-start | bytes 393224 | tf_op jit(solution)/shard_map/ppermute | solution.py:233
  104.3 10.7 %collective-permute-start.4 = (bf16[64,1024]{1,0:T(8,128)(2,1)}, bf16[64,1024]{1,0:T(8,128)(2,1)S(1)}, u32[]{:S(2)}, u32[]{:S(2)}) collective-permute-start(bf16[64,1024]{1,0:T(8,128)(2,1)} %get-tuple-element.11), channel_id=1, source_target_pairs={{1,0},{2,1},{3,2},{4,3},{5,4},{6,5},{7,6},{8,7},{9,8},{10,9},{11,1... | collective-permute-start | bytes 393224 | tf_op jit(solution)/shard_map/ppermute | solution.py:234
  106.5 8.5 %copy-start.2 = (bf16[64,1024]{1,0:T(8,128)(2,1)}, bf16[64,1024]{1,0:T(8,128)(2,1)S(1)}, u32[]{:S(2)}) copy-start(bf16[64,1024]{1,0:T(8,128)(2,1)S(1)} %collective-permute-done.3.low_in) | copy-start | bytes 393220
  115.0 0.7 copy-start.3

commit v2 on v0

v2 whole, which is shorter than its diff:
```python
import functools
import math

import jax
import jax.numpy as jnp
from jax import lax
from jax.experimental import pallas as pl
from jax.experimental.pallas import tpu as pltpu
from jax.sharding import PartitionSpec as P

RIM = 64
TILE = 256
CHUNK = 512
COLS = 256
SPAN = 80
PIECES = 3
DEPTH = 256
MESH_AXES = ("rows", "sub")
NT = (((1,), (1,)), ((), ()))
TN = (((0,), (0,)), ((), ()))


def window_starts(ids_smem, base, tile, slots):
    first = ids_smem[tile * TILE] - base
    last = ids_smem[tile * TILE + TILE - 1] - base
    head = jnp.minimum((first // 16) * 16, slots - SPAN)
    tail = jnp.clip((last // 16) * 16 - (SPAN - 16), 0, slots - SPAN)
    return pl.multiple_of(head, 16), pl.multiple_of(tail, 16), last


def note_gaps(ids_smem, ids_ref, base, slots, gaps):
    per = TILE // 128
    missed = jnp.zeros((per, 128), jnp.float32)
    for tile in range(ids_ref.shape[0] // per):
        head, tail, _ = window_starts(ids_smem, base, tile, slots)
        ids = ids_ref[tile * per : tile * per + per, :] - base
        missed = jnp.where((ids >= head + SPAN) & (ids < tail), 1.0, missed)
    gaps[0] = jnp.max(missed).astype(jnp.int32)


def later_windows(ids_smem, base, tile, slots, gaps, use):
    head, tail, last = window_starts(ids_smem, base, tile, slots)

    @pl.when(last >= head + SPAN)
    def _():
        use(tail, jnp.maximum(tail, head + SPAN), tail + SPAN)

        @pl.when(gaps[0] > 0)
        def _():
            def step(n, carry):
                at = pl.multiple_of(head + (n + 1) * SPAN, 16)
                use(jnp.minimum(at, slots - SPAN), at, jnp.minimum(at + SPAN, tail))
                return carry

            count = (jnp.maximum(tail - head - SPAN, 0) + SPAN - 1) // SPAN
            lax.fori_loop(0, count, step, 0)


def sums_kernel(ids_smem, base_smem, ids_ref, points_ref, counts_ref, cent_ref, moved_ref, down_ref, up_ref, acc, gaps):
    base = base_smem[0]
    own = cent_ref.shape[0]
    slots = own + 2 * RIM
    per = TILE // 128

    @pl.when(pl.program_id(0) == 0)
    def _():
        note_gaps(ids_smem, ids_ref, base, slots, gaps)

    acc[...] = jnp.zeros_like(acc)

    for tile in range(points_ref.shape[0] // TILE):
        rows = slice(tile * TILE, tile * TILE + TILE)
        ids = jnp.concatenate([ids_ref[tile * per + k : tile * per + k + 1, :] for k in range(per)], axis=1) - base

        def add(start, low, high):
            start = pl.multiple_of(start, 16)
            slot = lax.broadcasted_iota(jnp.int32, (SPAN, TILE), 0) + start
            pick = ((slot == ids) & (ids >= low) & (ids < high)).astype(jnp.float32).astype(jnp.bfloat16)
            acc[pl.ds(start, SPAN), :] += jnp.dot(pick, points_ref[rows, :], preferred_element_type=jnp.float32)

        head, _, _ = window_starts(ids_smem, base, tile, slots)
        add(head, head, head + SPAN)
        later_windows(ids_smem, base, tile, slots, gaps, add)

    down_ref[...] = acc[:RIM].astype(jnp.bfloat16)
    up_ref[...] = acc[RIM + own :].astype(jnp.bfloat16)
    for part in range(own // 128):
        count = jnp.broadcast_to(counts_ref[part : part + 1, :], (128, 128)).astype(jnp.float32)
        inverse = (1.0 / (count + 2.0)).T
        lo = RIM if part == 0 else 0
        hi = 128 - RIM if part == own // 128 - 1 else 128
        at = slice(part * 128 + lo, part * 128 + hi)
        for col in range(COLS // 128):
            cols = slice(col * 128, col * 128 + 128)
            moved_ref[at, cols] = (
                acc[RIM + part * 128 + lo : RIM + part * 128 + hi, cols] + 2.0 * cent_ref[at, cols]
            ) * inverse[lo:hi]
    moved_ref[:RIM, :] = acc[RIM : 2 * RIM]
    moved_ref[own - RIM :, :] = acc[own : own + RIM]


def edge_kernel(moved_in, low_in, high_in, counts_ref, cent_ref, moved_ref):
    which = pl.program_id(0)
    row = jnp.where(which == 0, 0, counts_ref.shape[0] - 1)
    count = jnp.broadcast_to(counts_ref[pl.ds(row, 1), :], (128, 128)).astype(jnp.float32)
    inverse = (1.0 / (count + 2.0)).T
    inverse = jnp.where(which == 0, inverse[:RIM], inverse[RIM:])
    spread = jnp.where(which == 0, low_in[...].astype(jnp.float32), high_in[...].astype(jnp.float32))
    for col in range(cent_ref.shape[1] // 128):
        cols = slice(col * 128, col * 128 + 128)
        moved_ref[:, cols] = (moved_in[:, cols] + spread[:, cols] + 2.0 * cent_ref[:, cols]) * inverse


def quant_kernel(
    ids_smem, place_smem, ids_ref, points_ref, cent_ref, low_ref, high_ref, books_ref, *refs
):
    rebuilt_ref, payload_ref, hi_win, mid_win, lo_win, picks, ids_col, resid, books_low, norms, totals, mass, gaps = refs[-13:]
    base = place_smem[0]
    subs, codes, subdim = books_ref.shape
    rate = 1.0 / (math.sqrt(subdim) * math.log(2.0))
    own = cent_ref.shape[0]
    slots = own + 2 * RIM
    rows = points_ref.shape[0]
    tiles = rows // TILE
    lane = lax.broadcasted_iota(jnp.int32, (1, DEPTH), 1)
    pattern = jnp.where(lane < PIECES * SPAN, lax.rem(lane, SPAN), -1)

    def pick_rows(tile, start, low, high):
        ids = ids_col[tile * TILE : tile * TILE + TILE, :]
        ids = jnp.where((ids >= low) & (ids < high), ids - start, -2)
        parts = [(ids == pattern[:, k * 128 : k * 128 + 128]).astype(jnp.float32) for k in range(DEPTH // 128)]
        return jnp.concatenate(parts, axis=1).astype(jnp.bfloat16)

    def split(value, at):
        at = slice(at, at + value.shape[0])
        hi = value.astype(jnp.bfloat16)
        rest = value - hi.astype(jnp.float32)
        mid = rest.astype(jnp.bfloat16)
        hi_win[at] = hi
        mid_win[at] = mid
        lo_win[at] = (rest - mid.astype(jnp.float32)).astype(jnp.bfloat16)

    @pl.when(pl.program_id(0) == 0)
    def _():
        note_gaps(ids_smem, ids_ref, base, slots, gaps)
        for k in range(rows // 128):
            ids_col[k * 128 : k * 128 + 128, :] = jnp.broadcast_to(ids_ref[k : k + 1, :] - base, (128, 128)).T
        for tile in range(tiles):
            head, _, _ = window_starts(ids_smem, base, tile, slots)
            picks[tile] = pick_rows(tile, head, head, head + SPAN)

    split(low_ref[...], 0)
    split(cent_ref[...], RIM)
    split(high_ref[...], RIM + own)
    for j in range(subs):
        words = books_ref[j]
        books_low[j] = words.astype(jnp.bfloat16)
        norms[j] = jnp.broadcast_to(jnp.sum(words * words, axis=1, keepdims=True) * rate, (codes, 128))

    def fetch(pick, start):
        at = pl.ds(pl.multiple_of(start, 16), SPAN)
        rest = jnp.zeros((DEPTH - PIECES * SPAN, COLS), jnp.bfloat16)
        window = jnp.concatenate([hi_win[at, :], mid_win[at, :], lo_win[at, :], rest], axis=0)
        return jnp.dot(pick, window, preferred_element_type=jnp.float32)

    for tile in range(tiles):
        at = slice(tile * TILE, tile * TILE + TILE)
        head, _, _ = window_starts(ids_smem, base, tile, slots)
        resid[at, :] = (points_ref[at, :].astype(jnp.float32) - fetch(picks[tile], head)).astype(jnp.bfloat16)

    for tile in range(tiles):
        at = slice(tile * TILE, tile * TILE + TILE)

        def redo(start, low, high):
            got = fetch(pick_rows(tile, start, low, high), start)
            fresh = points_ref[at, :].astype(jnp.float32) - got
            ids = ids_col[at, :]
            new = (ids >= low) & (ids < high)
            for k in range(COLS // 128):
                cols = slice(k * 128, k * 128 + 128)
                resid[at, cols] = jnp.where(new, fresh[:, cols], resid[at, cols].astype(jnp.float32)).astype(jnp.bfloat16)

        later_windows(ids_smem, base, tile, slots, gaps, redo)

    units = [(j, c) for j in range(subs) for c in range(rows // CHUNK)]

    def place(unit):
        j, c = unit
        return slice(c * CHUNK, c * CHUNK + CHUNK), slice(j * subdim, j * subdim + subdim)

    def dots_of(unit):
        return lax.dot_general(books_low[unit[0]], resid[place(unit)], NT, preferred_element_type=jnp.float32)

    def weigh(unit, dots):
        j, c = unit
        low, over_rows = [], None
        for part in range(CHUNK // 128):
            logits = dots[:, part * 128 : part * 128 + 128] * (2.0 * rate) - norms[j]
            top = jnp.max(logits, axis=0, keepdims=True)
            raised = jnp.exp2(logits - top)
            weights = raised * (1.0 / jnp.sum(raised, axis=0, keepdims=True))
            low.append(weights.astype(jnp.bfloat16))
            over_rows = weights if over_rows is None else over_rows + weights
        mass[j] = over_rows if c == 0 else mass[j] + over_rows
        return jnp.concatenate(low, axis=1)

    def products(unit, weights_low):
        j, c = unit
        got = jnp.dot(weights_low, resid[place(unit)], preferred_element_type=jnp.float32)
        totals[j] = got if c == 0 else totals[j] + got
        rebuilt = lax.dot_general(weights_low, books_low[j], TN, preferred_element_type=jnp.float32)
        rebuilt_ref[place(unit)] = rebuilt.astype(jnp.bfloat16)

    dots, weights_low = dots_of(units[0]), None
    for n, unit in enumerate(units):
        ahead = dots_of(units[n + 1]) if n + 1 < len(units) else None
        fresh = weigh(unit, dots)
        if n > 0:
            products(units[n - 1], weights_low)
        dots, weights_low = ahead, fresh
    products(units[-1], weights_low)

    group = payload_ref.shape[1] - 8
    left = lax.broadcasted_iota(jnp.int32, (8, 128), 1) < 64
    for j in range(subs):
        for g in range(codes // group):
            at = slice(g * group, g * group + group)
            slot = j * (codes // group) + g
            payload_ref[slot, :group, :] = totals[j, at, :]
            part = mass[j, at, :]
            part = part + pltpu.roll(part, 64, 1)
            payload_ref[slot, group:, :] = jnp.where(left, part[:8], part[8:])


def reduce_kernel(prior, parts_ref, book_ref, out_ref):
    total = jnp.sum(parts_ref[...], axis=0)
    group = book_ref.shape[0]
    left = lax.broadcasted_iota(jnp.int32, (8, 128), 1) < 64
    packed = total[group:]
    mass = jnp.concatenate(
        [
            jnp.sum(jnp.where(left, packed, 0.0), axis=1, keepdims=True),
            jnp.sum(jnp.where(left, 0.0, packed), axis=1, keepdims=True),
        ],
        axis=0,
    )
    moved = (total[:group] + prior * book_ref[...]) / (mass + prior)
    out_ref[...] = jnp.broadcast_to(moved[None], out_ref.shape)


def whole(shape):
    return pl.BlockSpec(shape, lambda *_: (0,) * len(shape))


def quantize(assign, place, ids, points, centroids, low, high, books, owners, rebuilt):
    rows_here, width = points.shape
    half, codes, subdim = books.shape
    own = centroids.shape[0]
    subs = COLS // subdim
    steps = half // subs
    group = half * codes // owners
    slots = own + 2 * RIM

    def columns(count):
        return pl.BlockSpec((count, COLS), lambda i, ids, place: (0, place[1] + i))

    in_specs = [
        whole(ids.shape), columns(rows_here), columns(own), columns(RIM), columns(RIM),
        pl.BlockSpec((subs, codes, subdim), lambda i, *_: (i, 0, 0)),
    ]
    inputs = [assign, place, ids, points, centroids, low, high, books]
    aliases = {}
    if rebuilt is not None:
        aliases = {len(inputs): 0}
        in_specs.append(pl.BlockSpec(memory_space=pl.ANY))
        inputs.append(rebuilt)
    return pl.pallas_call(
        quant_kernel,
        grid_spec=pltpu.PrefetchScalarGridSpec(
            num_scalar_prefetch=2,
            grid=(steps,),
            in_specs=in_specs,
            out_specs=[columns(rows_here), pl.BlockSpec((owners // steps, group + 8, subdim), lambda i, *_: (i, 0, 0))],
            scratch_shapes=[pltpu.VMEM((slots, COLS), jnp.bfloat16)] * 3
            + [
                pltpu.VMEM((rows_here // TILE, TILE, DEPTH), jnp.bfloat16),
                pltpu.VMEM((rows_here, 128), jnp.int32),
                pltpu.VMEM((rows_here, COLS), jnp.bfloat16),
                pltpu.VMEM((subs, codes, subdim), jnp.bfloat16),
                pltpu.VMEM((subs, codes, 128), jnp.float32),
                pltpu.VMEM((subs, codes, subdim), jnp.float32),
                pltpu.VMEM((subs, codes, 128), jnp.float32),
                pltpu.SMEM((1,), jnp.int32),
            ],
        ),
        out_shape=[
            jax.ShapeDtypeStruct(points.shape, jnp.bfloat16),
            jax.ShapeDtypeStruct((owners, group + 8, subdim), jnp.float32),
        ],
        input_output_aliases=aliases,
        compiler_params=pltpu.CompilerParams(vmem_limit_bytes=58 * 1024 * 1024),
        cost_estimate=pl.CostEstimate(flops=4 * 10**9, bytes_accessed=6 * 10**6, transcendentals=2 * 10**6),
        name="quantize",
    )(*inputs)


def cluster_sums(assign, place, ids, points, counts, centroids):
    rows_here, width = points.shape
    own = centroids.shape[0]

    def columns(count):
        return pl.BlockSpec((count, COLS), lambda i, *_: (0, i))

    return pl.pallas_call(
        sums_kernel,
        grid_spec=pltpu.PrefetchScalarGridSpec(
            num_scalar_prefetch=2,
            grid=(width // COLS,),
            in_specs=[whole(ids.shape), columns(rows_here), whole(counts.shape), columns(own)],
            out_specs=[columns(own), columns(RIM), columns(RIM)],
            scratch_shapes=[pltpu.VMEM((own + 2 * RIM, COLS), jnp.float32), pltpu.SMEM((1,), jnp.int32)],
        ),
        out_shape=[
            jax.ShapeDtypeStruct(centroids.shape, jnp.float32),
            jax.ShapeDtypeStruct((RIM, width), jnp.bfloat16),
            jax.ShapeDtypeStruct((RIM, width), jnp.bfloat16),
        ],
        compiler_params=pltpu.CompilerParams(vmem_limit_bytes=58 * 1024 * 1024),
        cost_estimate=pl.CostEstimate(flops=2 * 10**9, bytes_accessed=8 * 10**6, transcendentals=0),
        name="cluster_sums",
    )(assign, place, ids, points, counts, centroids)


def body(points, assign, cluster_counts, centroids, codebook):
    own, width = centroids.shape
    rows_here = points.shape[0]
    half, codes, subdim = codebook.shape
    rows_axis, sub_axis = MESH_AXES
    owners = lax.axis_size(rows_axis)
    places = owners * lax.axis_size(sub_axis)
    sub = lax.axis_index(sub_axis)
    position = lax.axis_index(rows_axis) * lax.axis_size(sub_axis) + sub
    base = position * own - RIM
    blocks = half * subdim // COLS
    up = [(i, i + 1) for i in range(places - 1)]
    down = [(i + 1, i) for i in range(places - 1)]
    swap = [(0, 1), (1, 0)]
    other_book = lax.ppermute(codebook, sub_axis, swap)
    low = lax.ppermute(centroids[own - RIM :], MESH_AXES, up)
    high = lax.ppermute(centroids[:RIM], MESH_AXES, down)
    ids = assign.reshape(rows_here // 128, 128)
    counts = cluster_counts.reshape(own // 128, 128)
    group = half * codes // owners

    theirs = jnp.stack([base, (1 - sub) * blocks]).astype(jnp.int32)
    mine = jnp.stack([base, sub * blocks]).astype(jnp.int32)
    rebuilt, away = quantize(assign, theirs, ids, points, centroids, low, high, other_book, owners, None)
    arrived = lax.ppermute(away, sub_axis, swap)
    rebuilt, kept = quantize(assign, mine, ids, points, centroids, low, high, codebook, owners, rebuilt)

    parts = lax.all_to_all(kept + arrived, rows_axis, 0, 0, tiled=True)
    later = lax.optimization_barrier((mine, kept))[0]
    sums, sum_down, sum_up = cluster_sums(assign, later, ids, points, counts, centroids)
    parts, sum_down, sum_up = lax.optimization_barrier((parts, sum_down, sum_up))
    sum_low = lax.ppermute(sum_up, MESH_AXES, up)
    sum_high = lax.ppermute(sum_down, MESH_AXES, down)

    book_rows = lax.dynamic_slice_in_dim(
        codebook.reshape(half * codes, subdim), lax.axis_index(rows_axis) * group, group, 0
    )
    prior = rows_here * places / codes
    moved = pl.pallas_call(
        functools.partial(reduce_kernel, prior),
        out_shape=jax.ShapeDtypeStruct((owners, group, subdim), jnp.float32),
        compiler_params=pltpu.CompilerParams(vmem_limit_bytes=8 * 1024 * 1024),
        name="moved_codes",
    )(parts, book_rows)
    moved = lax.all_to_all(moved, rows_axis, 0, 0, tiled=True)

    edge = pl.BlockSpec((RIM, width), lambda i: (i * (own // RIM - 1), 0))
    moved_centroids = pl.pallas_call(
        edge_kernel,
        grid=(2,),
        in_specs=[edge, whole((RIM, width)), whole((RIM, width)), whole(counts.shape), edge],
        out_specs=edge,
        out_shape=jax.ShapeDtypeStruct(centroids.shape, jnp.float32),
        input_output_aliases={0: 0},
        compiler_params=pltpu.CompilerParams(vmem_limit_bytes=8 * 1024 * 1024),
        name="edge_clusters",
    )(sums, sum_low, sum_high, counts, centroids)
    return (rebuilt, moved_centroids, moved.reshape(codebook.shape))


def solution(mesh):
    both = P(("rows", "sub"), None)
    flat = P(("rows", "sub"))
    books = P("sub", None, None)
    return jax.shard_map(
        body,
        mesh=mesh,
        in_specs=(both, flat, flat, both, books),
        out_specs=(both, both, books),
        check_vma=False,
    )
```

time: 355 us -> 92.5 us (0.26)
  the two profiles are of different devices: /device:TPU:0 before, /device:TPU:31 now
where the time goes in v2:
time: 92.5 us; the launch traced here: 91.9 us
  Pallas kernels  35.5 us (38%)
  starting transfers between devices  31.3 us (34%)
  waiting for transfers between devices  18.2 us (20%)
  local copies, waits for them, and re-layouts  3.45 us (4%)
  other arithmetic  2.69 us (3%)
    pallas_call x2, Pallas kernels, quantize(): pl.pallas_call(quant_kernel, grid_spec=pltpu.PrefetchScalarGridSpec(num_s...  22.4 us
    pallas_call x1, Pallas kernels, cluster_sums(): pl.pallas_call(sums_kernel, grid_spec=pltpu.PrefetchScalarGridSpec(num_sc...  10.1 us
    all_to_all x1, starting transfers between devices, body(): parts = lax.all_to_all(kept + arrived, rows_axis, 0, 0, tiled=True)  9.64 us
    all_to_all x1, starting transfers between devices, body(): moved = lax.all_to_all(moved, rows_axis, 0, 0, tiled=True)  9.55 us
    ppermute x1, waiting for transfers between devices, body(): high = lax.ppermute(centroids[:RIM], MESH_AXES, down)  8.61 us
    ppermute x1, waiting for transfers between devices, body(): sum_high = lax.ppermute(sum_down, MESH_AXES, down)  7.72 us
    ppermute x1, starting transfers between devices, body(): sum_low = lax.ppermute(sum_up, MESH_AXES, up)  4.52 us
    ppermute x1, starting transfers between devices, body(): low = lax.ppermute(centroids[own - RIM:], MESH_AXES, up)  3.02 us
  transfers between devices with their start and end apart: 8, of which 5 were waited for; matrix products, arithmetic and copies ran while one was open for 3% of the time, Pallas kernels for 25%

profile of v2, /device:TPU:31, one launch (start us, length us, event | category | flops | bytes accessed | tf_op | source)
XLA Modules:
  0.0 91.9 jit_solution(11748387892373441740)
XLA Ops:
  0.6 0.8 collective-permute-start.2
  1.4 1.1 %fusion = (f32[64,1024]{1,0:T(8,128)S(1)}, f32[64,1024]{1,0:T(8,128)S(1)}) fusion(f32[512,1024]{1,0:T(8,128)} %cent_ref.7), kind=kLoop, calls=%fused_computation.3 | loop fusion | bytes 1048576 | tf_op jit(solution)/shard_map/slice | solution.py:350
  2.5 3.0 %collective-permute-start = (f32[64,1024]{1,0:T(8,128)S(1)}, f32[64,1024]{1,0:T(8,128)S(1)}, u32[]{:S(2)}, u32[]{:S(2)}) collective-permute-start(f32[64,1024]{1,0:T(8,128)S(1)} %get-tuple-element.26), channel_id=1, source_target_pairs={{0,1},{1,2},{2,3},{3,4},{4,5},{5,6},{6,7},{7,8},{8,9},{9,10},{10,1... | collective-permute-start | bytes 786440 | tf_op jit(solution)/shard_map/ppermute | solution.py:349
  5.5 1.9 %collective-permute-start.1 = (f32[64,1024]{1,0:T(8,128)S(1)}, f32[64,1024]{1,0:T(8,128)S(1)}, u32[]{:S(2)}, u32[]{:S(2)}) collective-permute-start(f32[64,1024]{1,0:T(8,128)S(1)} %get-tuple-element.25), channel_id=1, source_target_pairs={{1,0},{2,1},{3,2},{4,3},{5,4},{6,5},{7,6},{8,7},{9,8},{10,9},{11,1... | collective-permute-start | bytes 786440 | tf_op jit(solution)/shard_map/ppermute | solution.py:350
  7.4 0.6 pad_add_fusion
  8.0 0.8 collective-permute-done.low_ref
  8.8 0.0 copy-start.3
  8.8 8.6 %collective-permute-done.1.high_ref = f32[64,1024]{1,0:T(8,128)S(1)} collective-permute-done((f32[64,1024]{1,0:T(8,128)S(1)}, f32[64,1024]{1,0:T(8,128)S(1)}, u32[]{:S(2)}, u32[]{:S(2)}) %collective-permute-start.1) | collective-permute-done | bytes 262176 | tf_op jit(solution)/shard_map/ppermute | solution.py:350
  17.4 0.0 copy-start.4
  17.4 0.0 collective-permute-done.2.books_ref
  17.4 0.0 copy-start.2
  17.4 0.0 copy-done.3
  17.4 0.7 copy-done.4
  18.1 0.2 copy-done.2
  18.3 11.2 %quantize.2 = (bf16[2048,1024]{1,0:T(8,128)(2,1)}, f32[64,24,128]{2,1,0:T(8,128)}) custom-call(s32[2048]{0:T(1024)} %ids_smem.5, s32[2]{0:T(128)} %get-tuple-element.28.place_smem, s32[16,128]{1,0:T(8,128)} %bitcast.11, bf16[2048,1024]{1,0:T(8,128)(2,1)} %points_ref.5, f32[512,1024]{1,0:T(8,128)} %cent_ref.7, f32[64,1024]{1,0:T(8,128)} %copy-done.3, ...), custom_call_target="tpu_custom_call" | custom-call | flops 4000000000 | bytes 6000000 | tf_op jit(solution)/shard_map/quantize/pallas_call | solution.py:277
  29.4 0.0 collective-permute-start.3
  29.4 11.2 %quantize.3 = (bf16[2048,1024]{1,0:T(8,128)(2,1)}, f32[64,24,128]{2,1,0:T(8,128)}) custom-call(s32[2048]{0:T(1024)} %ids_smem.5, s32[2]{0:T(128)} %get-tuple-element.17.place_smem.base_smem, s32[16,128]{1,0:T(8,128)} %bitcast.12, bf16[2048,1024]{1,0:T(8,128)(2,1)} %points_ref.5, f32[512,1024]{1,0:T(8,128)} %cent_ref.7, ...), custom_call_target="tpu_custom_call", output_to_operand_aliasing={{0}: (8, {})} | custom-call | flops 4000000000 | bytes 6000000 | tf_op jit(solution)/shard_map/quantize/pallas_call | solution.py:277
  40.6 0.0 collective-permute-done.3
  40.7 2.1 %add.11 = f32[64,24,128]{2,1,0:T(8,128)} add(f32[64,24,128]{2,1,0:T(8,128)} %get-tuple-element.16, f32[64,24,128]{2,1,0:T(8,128)S(1)} %collective-permute-done.3) | non-fusion elementwise | flops 196608 | bytes 2359296 | tf_op jit(solution)/shard_map/add | solution.py:361
  42.7 9.6 %all-to-all-start = ((f32[64,24,128]{2,1,0:T(8,128)}), f32[64,24,128]{2,1,0:T(8,128)S(1)}, u32[]{:S(2)}, u32[]{:S(2)}) async-start(f32[64,24,128]{2,1,0:T(8,128)} %add.11), calls=%async_computation | async-start | bytes 1572864 | tf_op jit(solution)/shard_map/all_to_all | solution.py:361
  52.4 0.7 constant_dynamic-slice_fusion.book_ref
  53.1 10.1 %cluster_sums.1 = (f32[512,1024]{1,0:T(8,128)}, bf16[64,1024]{1,0:T(8,128)(2,1)}, bf16[64,1024]{1,0:T(8,128)(2,1)}) custom-call(s32[2048]{0:T(1024)} %ids_smem.5, s32[2]{0:T(128)} %get-tuple-element.17.place_smem.base_smem, s32[16,128]{1,0:T(8,128)} %bitcast.13, bf16[2048,1024]{1,0:T(8,128)(2,1)} %points_ref.5, s32[4,128]{1,0:T(4,128)} %bitcast.7, ...), custom_call_target="tpu_custom_call" | custom-call | flops 2000000000 | bytes 8000000 | tf_op jit(solution)/shard_map/cluster_sums/pallas_call | solution.py:314
  63.2 0.0 copy-start.6
  63.2 0.0 copy-start.5
  63.3 0.0 copy-start
  63.3 0.0 copy-start.1
  63.3 0.2 all-to-all-done.parts_ref
  63.5 1.0 %moved_codes.1 = f32[64,16,128]{2,1,0:T(8,128)} custom-call(f32[64,24,128]{2,1,0:T(8,128)S(1)} %all-to-all-done.parts_ref, f32[16,128]{1,0:T(8,128)S(1)} %constant_dynamic-slice_fusion.book_ref), custom_call_target="tpu_custom_call" | custom-call | tf_op jit(solution)/shard_map/moved_codes/pallas_call | solution.py:372
  64.6 9.6 %all-to-all-start.1 = ((f32[64,16,128]{2,1,0:T(8,128)}), f32[64,16,128]{2,1,0:T(8,128)S(1)}, u32[]{:S(2)}, u32[]{:S(2)}) async-start(f32[64,16,128]{2,1,0:T(8,128)} %moved_codes.1), calls=%async_computation.1 | async-start | bytes 1048576 | tf_op jit(solution)/shard_map/all_to_all | solution.py:378
  74.1 0.0 copy-done.6
  74.1 4.5 %collective-permute-start.4 = (bf16[64,1024]{1,0:T(8,128)(2,1)S(1)}, bf16[64,1024]{1,0:T(8,128)(2,1)S(1)}, u32[]{:S(2)}, u32[]{:S(2)}) collective-permute-start(bf16[64,1024]{1,0:T(8,128)(2,1)S(1)} %copy-done.6), channel_id=1, source_target_pairs={{0,1},{1,2},{2,3},{3,4},{4,5},{5,6},{6,7},{7,8},{8,9},{9,10},{10,1... | collective-permute-start | bytes 393224 | tf_op jit(solution)/shard_map/ppermute | solution.py:365
  78.7 0.0 copy-done.5
  78.7 1.9 %collective-permute-start.5 = (bf16[64,1024]{1,0:T(8,128)(2,1)S(1)}, bf16[64,1024]{1,0:T(8,128)(2,1)S(1)}, u32[]{:S(2)}, u32[]{:S(2)}) collective-permute-start(bf16[64,1024]{1,0:T(8,128)(2,1)S(1)} %copy-done.5), channel_id=1, source_target_pairs={{1,0},{2,1},{3,2},{4,3},{5,4},{6,5},{7,6},{8,7},{9,8},{10,9},{11,1... | collective-permute-start | bytes 393224 | tf_op jit(solution)/shard_map/ppermute | solution.py:366
  80.6 0.9 collective-permute-done.4.low_in
  81.5 7.7 %collective-permute-done.5.high_in = bf16[64,1024]{1,0:T(8,128)(2,1)S(1)} collective-permute-done((bf16[64,1024]{1,0:T(8,128)(2,1)S(1)}, bf16[64,1024]{1,0:T(8,128)(2,1)S(1)}, u32[]{:S(2)}, u32[]{:S(2)}) %collective-permute-start.5) | collective-permute-done | bytes 131104 | tf_op jit(solution)/shard_map/ppermute | solution.py:366
  89.2 0.0 copy-done
  89.2 0.0 copy-done.1
  89.2 1.9 %edge_clusters.1 = f32[512,1024]{1,0:T(8,128)} custom-call(f32[512,1024]{1,0:T(8,128)} %get-tuple-element.18.moved_in, bf16[64,1024]{1,0:T(8,128)(2,1)S(1)} %collective-permute-done.4.low_in, bf16[64,1024]{1,0:T(8,128)(2,1)S(1)} %collective-permute-done.5.high_in, s32[4,128]{1,0:T(4,128)S(1)} %bitcast.8, ...), custom_call_target="tpu_custom_call", output_to_operand_aliasing={{}: (0, {})} | custom-call | tf_op jit(solution)/shard_map/edge_clusters/pallas_call | solution.py:381
  91.1 0.0 all-to-all-done.1
  91.1 0.8 copy.13
Async XLA Ops:
  0.6 16.8 %collective-permute-start.2 = (f32[4,256,128]{2,1,0:T(8,128)}, f32[4,256,128]{2,1,0:T(8,128)S(1)}, u32[]{:S(2)}, u32[]{:S(2)}) collective-permute-start(f32[4,256,128]{2,1,0:T(8,128)} %books_ref.1), channel_id=1, source_target_pairs={{0,1},{1,0},{2,3},{3,2},{4,5},{5,4},{6,7},{7,6},{8,9},{9,8},{10,11... | collective-permute-start | bytes 1572872 | tf_op jit(solution)/shard_map/ppermute | solution.py:348
  2.5 6.3 %collective-permute-start = (f32[64,1024]{1,0:T(8,128)S(1)}, f32[64,1024]{1,0:T(8,128)S(1)}, u32[]{:S(2)}, u32[]{:S(2)}) collective-permute-start(f32[64,1024]{1,0:T(8,128)S(1)} %get-tuple-element.26), channel_id=1, source_target_pairs={{0,1},{1,2},{2,3},{3,4},{4,5},{5,6},{6,7},{7,8},{8,9},{9,10},{10,1... | collective-permute-start | bytes 786440 | tf_op jit(solution)/shard_map/ppermute | solution.py:349
  5.5 11.9 %collective-permute-start.1 = (f32[64,1024]{1,0:T(8,128)S(1)}, f32[64,1024]{1,0:T(8,128)S(1)}, u32[]{:S(2)}, u32[]{:S(2)}) collective-permute-start(f32[64,1024]{1,0:T(8,128)S(1)} %get-tuple-element.25), channel_id=1, source_target_pairs={{1,0},{2,1},{3,2},{4,3},{5,4},{6,5},{7,6},{8,7},{9,8},{10,9},{11,1... | collective-permute-start | bytes 786440 | tf_op jit(solution)/shard_map/ppermute | solution.py:350
  8.8 8.6 %copy-start.3 = (f32[64,1024]{1,0:T(8,128)}, f32[64,1024]{1,0:T(8,128)S(1)}, u32[]{:S(2)}) copy-start(f32[64,1024]{1,0:T(8,128)S(1)} %collective-permute-done.low_ref) | copy-start | bytes 786436
  17.4 0.7 copy-start.4
  17.4 0.9 copy-start.2
  29.4 11.2 %collective-permute-start.3 = (f32[64,24,128]{2,1,0:T(8,128)}, f32[64,24,128]{2,1,0:T(8,128)S(1)}, u32[]{:S(2)}, u32[]{:S(2)}) collective-permute-start(f32[64,24,128]{2,1,0:T(8,128)} %get-tuple-element.19), channel_id=1, source_target_pairs={{0,1},{1,0},{2,3},{3,2},{4,5},{5,4},{6,7},{7,6},{8,9},{9,8},{10,11... | collective-permute-start | bytes 2359304 | tf_op jit(solution)/shard_map/ppermute | solution.py:358
  42.7 20.8 %all-to-all-start = ((f32[64,24,128]{2,1,0:T(8,128)}), f32[64,24,128]{2,1,0:T(8,128)S(1)}, u32[]{:S(2)}, u32[]{:S(2)}) async-start(f32[64,24,128]{2,1,0:T(8,128)} %add.11), calls=%async_computation | async-start | bytes 1572864 | tf_op jit(solution)/shard_map/all_to_all | solution.py:361
  63.2 10.9 %copy-start.6 = (bf16[64,1024]{1,0:T(8,128)(2,1)S(1)}, bf16[64,1024]{1,0:T(8,128)(2,1)}, u32[]{:S(2)}) copy-start(bf16[64,1024]{1,0:T(8,128)(2,1)} %get-tuple-element.22) | copy-start | bytes 393220
  63.2 15.4 %copy-start.5 = (bf16[64,1024]{1,0:T(8,128)(2,1)S(1)}, bf16[64,1024]{1,0:T(8,128)(2,1)}, u32[]{:S(2)}) copy-start(bf16[64,1024]{1,0:T(8,128)(2,1)} %get-tuple-element.23) | copy-start | bytes 393220
  63.3 25.9 %copy-start = (f32[512,1024]{1,0:T(8,128)S(1)}, f32[512,1024]{1,0:T(8,128)}, u32[]{:S(2)}) copy-start(f32[512,1024]{1,0:T(8,128)} %cent_ref.7) | copy-start | bytes 6291460
  63.3 25.9 %copy-start.1 = (s32[512]{0:T(512)S(1)}, s32[512]{0:T(512)}, u32[]{:S(2)}) copy-start(s32[512]{0:T(512)} %param.7) | copy-start | bytes 6148
  64.6 26.5 %all-to-all-start.1 = ((f32[64,16,128]{2,1,0:T(8,128)}), f32[64,16,128]{2,1,0:T(8,128)S(1)}, u32[]{:S(2)}, u32[]{:S(2)}) async-start(f32[64,16,128]{2,1,0:T(8,128)} %moved_codes.1), calls=%async_computation.1 | async-start | bytes 1048576 | tf_op jit(solution)/shard_map/all_to_all | solution.py:378
  74.1 7.3 %collective-permute-start.4 = (bf16[64,1024]{1,0:T(8,128)(2,1)S(1)}, bf16[64,1024]{1,0:T(8,128)(2,1)S(1)}, u32[]{:S(2)}, u32[]{:S(2)}) collective-permute-start(bf16[64,1024]{1,0:T(8,128)(2,1)S(1)} %copy-done.6), channel_id=1, source_target_pairs={{0,1},{1,2},{2,3},{3,4},{4,5},{5,6},{6,7},{7,8},{8,9},{9,10},{10,1... | collective-permute-start | bytes 393224 | tf_op jit(solution)/shard_map/ppermute | solution.py:365
  78.7 10.5 %collective-permute-start.5 = (bf16[64,1024]{1,0:T(8,128)(2,1)S(1)}, bf16[64,1024]{1,0:T(8,128)(2,1)S(1)}, u32[]{:S(2)}, u32[]{:S(2)}) collective-permute-start(bf16[64,1024]{1,0:T(8,128)(2,1)S(1)} %copy-done.5), channel_id=1, source_target_pairs={{1,0},{2,1},{3,2},{4,3},{5,4},{6,5},{7,6},{8,7},{9,8},{10,9},{11,1... | collective-permute-start | bytes 393224 | tf_op jit(solution)/shard_map/ppermute | solution.py:366

commit v3 on v2

--- a/solution.py
+++ b/solution.py
@@ -38,52 +38,68 @@
     gaps[0] = jnp.max(missed).astype(jnp.int32)
 
 
-def later_windows(ids_smem, base, tile, slots, gaps, use):
-    head, tail, last = window_starts(ids_smem, base, tile, slots)
-
-    @pl.when(last >= head + SPAN)
-    def _():
-        use(tail, jnp.maximum(tail, head + SPAN), tail + SPAN)
-
-        @pl.when(gaps[0] > 0)
-        def _():
-            def step(n, carry):
-                at = pl.multiple_of(head + (n + 1) * SPAN, 16)
-                use(jnp.minimum(at, slots - SPAN), at, jnp.minimum(at + SPAN, tail))
-                return carry
-
-            count = (jnp.maximum(tail - head - SPAN, 0) + SPAN - 1) // SPAN
-            lax.fori_loop(0, count, step, 0)
-
-
-def sums_kernel(ids_smem, base_smem, ids_ref, points_ref, counts_ref, cent_ref, moved_ref, down_ref, up_ref, acc, gaps):
-    base = base_smem[0]
+def middle_windows(ids_smem, base, tile, slots, use):
+    head, tail, _ = window_starts(ids_smem, base, tile, slots)
+
+    def step(n, carry):
+        at = pl.multiple_of(head + (n + 1) * SPAN, 16)
+        use(jnp.minimum(at, slots - SPAN), at, jnp.minimum(at + SPAN, tail))
+        return carry
+
+    count = (jnp.maximum(tail - head - SPAN, 0) + SPAN - 1) // SPAN
+    lax.fori_loop(0, count, step, 0)
+
+
+def sums_kernel(
+    ids_smem, place_smem, ids_ref, points_ref, counts_ref, cent_ref, moved_ref, inner_ref, outer_ref, acc, picks, gaps
+):
+    base = place_smem[0]
     own = cent_ref.shape[0]
     slots = own + 2 * RIM
     per = TILE // 128
+    tiles = points_ref.shape[0] // TILE
+
+    def pick_slots(tile, start, low, high):
+        ids = jnp.concatenate([ids_ref[tile * per + k : tile * per + k + 1, :] for k in range(per)], axis=1) - base
+        ids = jnp.where((ids >= low) & (ids < high), ids - start, -1)
+        slot = lax.broadcasted_iota(jnp.int32, (SPAN, TILE), 0)
+        return (slot == ids).astype(jnp.float32).astype(jnp.bfloat16)
 
     @pl.when(pl.program_id(0) == 0)
     def _():
         note_gaps(ids_smem, ids_ref, base, slots, gaps)
+        for tile in range(tiles):
+            head, tail, _ = window_starts(ids_smem, base, tile, slots)
+            picks[tile, :SPAN] = pick_slots(tile, head, head, head + SPAN)
+            picks[tile, SPAN:] = pick_slots(tile, tail, jnp.maximum(tail, head + SPAN), tail + SPAN)
 
     acc[...] = jnp.zeros_like(acc)
-
-    for tile in range(points_ref.shape[0] // TILE):
-        rows = slice(tile * TILE, tile * TILE + TILE)
-        ids = jnp.concatenate([ids_ref[tile * per + k : tile * per + k + 1, :] for k in range(per)], axis=1) - base
-
-        def add(start, low, high):
-            start = pl.multiple_of(start, 16)
-            slot = lax.broadcasted_iota(jnp.int32, (SPAN, TILE), 0) + start
-            pick = ((slot == ids) & (ids >= low) & (ids < high)).astype(jnp.float32).astype(jnp.bfloat16)
-            acc[pl.ds(start, SPAN), :] += jnp.dot(pick, points_ref[rows, :], preferred_element_type=jnp.float32)
-
-        head, _, _ = window_starts(ids_smem, base, tile, slots)
-        add(head, head, head + SPAN)
-        later_windows(ids_smem, base, tile, slots, gaps, add)
-
-    down_ref[...] = acc[:RIM].astype(jnp.bfloat16)
-    up_ref[...] = acc[RIM + own :].astype(jnp.bfloat16)
+    sums = [
+        jnp.dot(picks[tile], points_ref[tile * TILE : tile * TILE + TILE, :], preferred_element_type=jnp.float32)
+        for tile in range(tiles)
+    ]
+    for tile in range(tiles):
+        head, tail, _ = window_starts(ids_smem, base, tile, slots)
+        acc[pl.ds(head, SPAN), :] += sums[tile][:SPAN]
+        acc[pl.ds(tail, SPAN), :] += sums[tile][SPAN:]
+
+    @pl.when(gaps[0] > 0)
+    def _():
+        for tile in range(tiles):
+            rows = slice(tile * TILE, tile * TILE + TILE)
+
+            def add(start, low, high):
+                start = pl.multiple_of(start, 16)
+                pick = pick_slots(tile, start, low, high)
+                acc[pl.ds(start, SPAN), :] += jnp.dot(pick, points_ref[rows, :], preferred_element_type=jnp.float32)
+
+            middle_windows(ids_smem, base, tile, slots, add)
+
+    down = acc[:RIM].astype(jnp.bfloat16)
+    up = acc[RIM + own :].astype(jnp.bfloat16)
+    first = place_smem[2] == 0
+    inner_ref[...] = jnp.where(first, up, down)
+    outer_ref[...] = jnp.where(first, down, up)
     for part in range(own // 128):
         count = jnp.broadcast_to(counts_ref[part : part + 1, :], (128, 128)).astype(jnp.float32)
         inverse = (1.0 / (count + 2.0)).T
@@ -99,20 +115,21 @@
     moved_ref[own - RIM :, :] = acc[own : own + RIM]
 
 
-def edge_kernel(moved_in, low_in, high_in, counts_ref, cent_ref, moved_ref):
+def edge_kernel(place_smem, moved_in, inner_in, outer_in, counts_ref, cent_ref, moved_ref):
     which = pl.program_id(0)
     row = jnp.where(which == 0, 0, counts_ref.shape[0] - 1)
     count = jnp.broadcast_to(counts_ref[pl.ds(row, 1), :], (128, 128)).astype(jnp.float32)
     inverse = (1.0 / (count + 2.0)).T
     inverse = jnp.where(which == 0, inverse[:RIM], inverse[RIM:])
-    spread = jnp.where(which == 0, low_in[...].astype(jnp.float32), high_in[...].astype(jnp.float32))
+    outer = which == place_smem[2]
+    spread = jnp.where(outer, outer_in[...].astype(jnp.float32), inner_in[...].astype(jnp.float32))
     for col in range(cent_ref.shape[1] // 128):
         cols = slice(col * 128, col * 128 + 128)
         moved_ref[:, cols] = (moved_in[:, cols] + spread[:, cols] + 2.0 * cent_ref[:, cols]) * inverse
 
 
 def quant_kernel(
-    ids_smem, place_smem, ids_ref, points_ref, cent_ref, low_ref, high_ref, books_ref, *refs
+    ids_smem, place_smem, ids_ref, points_ref, cent_ref, inner_ref, outer_ref, books_ref, *refs
 ):
     rebuilt_ref, payload_ref, hi_win, mid_win, lo_win, picks, ids_col, resid, books_low, norms, totals, mass, gaps = refs[-13:]
     base = place_smem[0]
@@ -146,41 +163,51 @@
         for k in range(rows // 128):
             ids_col[k * 128 : k * 128 + 128, :] = jnp.broadcast_to(ids_ref[k : k + 1, :] - base, (128, 128)).T
         for tile in range(tiles):
-            head, _, _ = window_starts(ids_smem, base, tile, slots)
-            picks[tile] = pick_rows(tile, head, head, head + SPAN)
-
-    split(low_ref[...], 0)
+            head, tail, _ = window_starts(ids_smem, base, tile, slots)
+            picks[tile, :, :DEPTH] = pick_rows(tile, head, head, head + SPAN)
+            picks[tile, :, DEPTH:] = pick_rows(tile, tail, jnp.maximum(tail, head + SPAN), tail + SPAN)
+
+    first = place_smem[2] == 0
+    split(jnp.where(first, outer_ref[...], inner_ref[...]), 0)
     split(cent_ref[...], RIM)
-    split(high_ref[...], RIM + own)
+    split(jnp.where(first, inner_ref[...], outer_ref[...]), RIM + own)
     for j in range(subs):
         words = books_ref[j]
         books_low[j] = words.astype(jnp.bfloat16)
         norms[j] = jnp.broadcast_to(jnp.sum(words * words, axis=1, keepdims=True) * rate, (codes, 128))
 
-    def fetch(pick, start):
+    def window(start):
         at = pl.ds(pl.multiple_of(start, 16), SPAN)
         rest = jnp.zeros((DEPTH - PIECES * SPAN, COLS), jnp.bfloat16)
-        window = jnp.concatenate([hi_win[at, :], mid_win[at, :], lo_win[at, :], rest], axis=0)
-        return jnp.dot(pick, window, preferred_element_type=jnp.float32)
+        return [hi_win[at, :], mid_win[at, :], lo_win[at, :], rest]
+
+    def subtract(tile):
+        at = slice(tile * TILE, tile * TILE + TILE)
+        head, tail, _ = window_starts(ids_smem, base, tile, slots)
+        both = jnp.concatenate(window(head) + window(tail), axis=0)
+        got = jnp.dot(picks[tile], both, preferred_element_type=jnp.float32)
+        resid[at, :] = (points_ref[at, :].astype(jnp.float32) - got).astype(jnp.bfloat16)
 
     for tile in range(tiles):
-        at = slice(tile * TILE, tile * TILE + TILE)
-        head, _, _ = window_starts(ids_smem, base, tile, slots)
-        resid[at, :] = (points_ref[at, :].astype(jnp.float32) - fetch(picks[tile], head)).astype(jnp.bfloat16)
-
-    for tile in range(tiles):
-        at = slice(tile * TILE, tile * TILE + TILE)
-
-        def redo(start, low, high):
-            got = fetch(pick_rows(tile, start, low, high), start)
-            fresh = points_ref[at, :].astype(jnp.float32) - got
-            ids = ids_col[at, :]
-            new = (ids >= low) & (ids < high)
-            for k in range(COLS // 128):
-                cols = slice(k * 128, k * 128 + 128)
-                resid[at, cols] = jnp.where(new, fresh[:, cols], resid[at, cols].astype(jnp.float32)).astype(jnp.bfloat16)
-
-        later_windows(ids_smem, base, tile, slots, gaps, redo)
+        subtract(tile)
+
+    @pl.when(gaps[0] > 0)
+    def _():
+        for tile in range(tiles):
+            at = slice(tile * TILE, tile * TILE + TILE)
+
+            def redo(start, low, high):
+                pick = pick_rows(tile, start, low, high)
+                got = jnp.dot(pick, jnp.concatenate(window(start), axis=0), preferred_element_type=jnp.float32)
+                fresh = points_ref[at, :].astype(jnp.float32) - got
+                ids = ids_col[at, :]
+                new = (ids >= low) & (ids < high)
+                for k in range(COLS // 128):
+                    cols = slice(k * 128, k * 128 + 128)
+                    kept = resid[at, cols].astype(jnp.float32)
+                    resid[at, cols] = jnp.where(new, fresh[:, cols], kept).astype(jnp.bfloat16)
+
+            middle_windows(ids_smem, base, tile, slots, redo)
 
     units = [(j, c) for j in range(subs) for c in range(rows // CHUNK)]
 
@@ -252,7 +279,7 @@
     return pl.BlockSpec(shape, lambda *_: (0,) * len(shape))
 
 
-def quantize(assign, place, ids, points, centroids, low, high, books, owners, rebuilt):
+def quantize(assign, place, ids, points, centroids, inner, outer, books, owners, rebuilt):
     rows_here, width = points.shape
     half, codes, subdim = books.shape
     own = centroids.shape[0]
@@ -268,7 +295,7 @@
         whole(ids.shape), columns(rows_here), columns(own), columns(RIM), columns(RIM),
         pl.BlockSpec((subs, codes, subdim), lambda i, *_: (i, 0, 0)),
     ]
-    inputs = [assign, place, ids, points, centroids, low, high, books]
+    inputs = [assign, place, ids, points, centroids, inner, outer, books]
     aliases = {}
     if rebuilt is not None:
         aliases = {len(inputs): 0}
@@ -283,7 +310,7 @@
             out_specs=[columns(rows_here), pl.BlockSpec((owners // steps, group + 8, subdim), lambda i, *_: (i, 0, 0))],
             scratch_shapes=[pltpu.VMEM((slots, COLS), jnp.bfloat16)] * 3
             + [
-                pltpu.VMEM((rows_here // TILE, TILE, DEPTH), jnp.bfloat16),
+                pltpu.VMEM((rows_here // TILE, TILE, 2 * DEPTH), jnp.bfloat16),
                 pltpu.VMEM((rows_here, 128), jnp.int32),
                 pltpu.VMEM((rows_here, COLS), jnp.bfloat16),
                 pltpu.VMEM((subs, codes, subdim), jnp.bfloat16),
@@ -318,7 +345,11 @@
             grid=(width // COLS,),
             in_specs=[whole(ids.shape), columns(rows_here), whole(counts.shape), columns(own)],
             out_specs=[columns(own), columns(RIM), columns(RIM)],
-            scratch_shapes=[pltpu.VMEM((own + 2 * RIM, COLS), jnp.float32), pltpu.SMEM((1,), jnp.int32)],
+            scratch_shapes=[
+                pltpu.VMEM((own + 2 * RIM, COLS), jnp.float32),
+                pltpu.VMEM((rows_here // TILE, 2 * SPAN, TILE), jnp.bfloat16),
+                pltpu.SMEM((1,), jnp.int32),
+            ],
         ),
         out_shape=[
             jax.ShapeDtypeStruct(centroids.shape, jnp.float32),
@@ -342,28 +373,30 @@
     position = lax.axis_index(rows_axis) * lax.axis_size(sub_axis) + sub
     base = position * own - RIM
     blocks = half * subdim // COLS
-    up = [(i, i + 1) for i in range(places - 1)]
-    down = [(i + 1, i) for i in range(places - 1)]
     swap = [(0, 1), (1, 0)]
+    pairs = [(i, i + 1) for i in range(1, places - 1, 2)]
+    across = pairs + [(j, i) for i, j in pairs]
     other_book = lax.ppermute(codebook, sub_axis, swap)
-    low = lax.ppermute(centroids[own - RIM :], MESH_AXES, up)
-    high = lax.ppermute(centroids[:RIM], MESH_AXES, down)
+    outer = lax.dynamic_slice_in_dim(centroids, sub * (own - RIM), RIM, 0)
+    inner = lax.dynamic_slice_in_dim(centroids, (1 - sub) * (own - RIM), RIM, 0)
+    outer = lax.ppermute(outer, MESH_AXES, across)
+    inner = lax.ppermute(inner, sub_axis, swap)
     ids = assign.reshape(rows_here // 128, 128)
     counts = cluster_counts.reshape(own // 128, 128)
     group = half * codes // owners
 
-    theirs = jnp.stack([base, (1 - sub) * blocks]).astype(jnp.int32)
-    mine = jnp.stack([base, sub * blocks]).astype(jnp.int32)
-    rebuilt, away = quantize(assign, theirs, ids, points, centroids, low, high, other_book, owners, None)
+    theirs = jnp.stack([base, (1 - sub) * blocks, sub]).astype(jnp.int32)
+    mine = jnp.stack([base, sub * blocks, sub]).astype(jnp.int32)
+    rebuilt, away = quantize(assign, theirs, ids, points, centroids, inner, outer, other_book, owners, None)
     arrived = lax.ppermute(away, sub_axis, swap)
-    rebuilt, kept = quantize(assign, mine, ids, points, centroids, low, high, codebook, owners, rebuilt)
+    rebuilt, kept = quantize(assign, mine, ids, points, centroids, inner, outer, codebook, owners, rebuilt)
 
     parts = lax.all_to_all(kept + arrived, rows_axis, 0, 0, tiled=True)
     later = lax.optimization_barrier((mine, kept))[0]
-    sums, sum_down, sum_up = cluster_sums(assign, later, ids, points, counts, centroids)
-    parts, sum_down, sum_up = lax.optimization_barrier((parts, sum_down, sum_up))
-    sum_low = lax.ppermute(sum_up, MESH_AXES, up)
-    sum_high = lax.ppermute(sum_down, MESH_AXES, down)
+    sums, sum_inner, sum_outer = cluster_sums(assign, later, ids, points, counts, centroids)
+    sum_outer = lax.ppermute(sum_outer, MESH_AXES, across)
+    sum_inner = lax.ppermute(sum_inner, sub_axis, swap)
+    parts, sum_inner, sum_outer = lax.optimization_barrier((parts, sum_inner, sum_outer))
 
     book_rows = lax.dynamic_slice_in_dim(
         codebook.reshape(half * codes, subdim), lax.axis_index(rows_axis) * group, group, 0
@@ -377,17 +410,20 @@
     )(parts, book_rows)
     moved = lax.all_to_all(moved, rows_axis, 0, 0, tiled=True)
 
-    edge = pl.BlockSpec((RIM, width), lambda i: (i * (own // RIM - 1), 0))
+    edge = pl.BlockSpec((RIM, width), lambda i, *_: (i * (own // RIM - 1), 0))
     moved_centroids = pl.pallas_call(
         edge_kernel,
-        grid=(2,),
-        in_specs=[edge, whole((RIM, width)), whole((RIM, width)), whole(counts.shape), edge],
-        out_specs=edge,
+        grid_spec=pltpu.PrefetchScalarGridSpec(
+            num_scalar_prefetch=1,
+            grid=(2,),
+            in_specs=[edge, whole((RIM, width)), whole((RIM, width)), whole(counts.shape), edge],
+            out_specs=edge,
+        ),
         out_shape=jax.ShapeDtypeStruct(centroids.shape, jnp.float32),
-        input_output_aliases={0: 0},
+        input_output_aliases={1: 0},
         compiler_params=pltpu.CompilerParams(vmem_limit_bytes=8 * 1024 * 1024),
         name="edge_clusters",
-    )(sums, sum_low, sum_high, counts, centroids)
+    )(mine, sums, sum_inner, sum_outer, counts, centroids)
     return (rebuilt, moved_centroids, moved.reshape(codebook.shape))
 
 

time: 92.5 us -> 92 us (level)
  the two profiles are of different devices: /device:TPU:31 before, /device:TPU:1 now
where the time goes in v3:
time: 92 us; the launch traced here: 91.3 us
  starting transfers between devices  36.6 us (40%)
  Pallas kernels  32.2 us (35%)
  waiting for transfers between devices  15.6 us (17%)
  local copies, waits for them, and re-layouts  3.45 us (4%)
  other arithmetic  2.81 us (3%)
    pallas_call x2, Pallas kernels, quantize(): pl.pallas_call(quant_kernel, grid_spec=pltpu.PrefetchScalarGridSpec(num_s...  22 us
    all_to_all x1, starting transfers between devices, body(): parts = lax.all_to_all(kept + arrived, rows_axis, 0, 0, tiled=True)  15 us
    all_to_all x1, starting transfers between devices, body(): moved = lax.all_to_all(moved, rows_axis, 0, 0, tiled=True)  12.5 us
    all_to_all x1, waiting for transfers between devices, body(): moved = lax.all_to_all(moved, rows_axis, 0, 0, tiled=True)  8.36 us
    pallas_call x1, Pallas kernels, cluster_sums(): pl.pallas_call(sums_kernel, grid_spec=pltpu.PrefetchScalarGridSpec(num_sc...  6.62 us
    ppermute x1, starting transfers between devices, body(): outer = lax.ppermute(outer, MESH_AXES, across)  3.56 us
    ppermute x1, waiting for transfers between devices, body(): outer = lax.ppermute(outer, MESH_AXES, across)  3.42 us
    ppermute x1, starting transfers between devices, body(): sum_outer = lax.ppermute(sum_outer, MESH_AXES, across)  3.22 us
  transfers between devices with their start and end apart: 8, of which 4 were waited for; matrix products, arithmetic and copies ran while one was open for 3% of the time, Pallas kernels for 22%

profile of v3, /device:TPU:1, one launch (start us, length us, event | category | flops | bytes accessed | tf_op | source)
XLA Modules:
  0.0 91.3 jit_solution(13336549404312616404)
XLA Ops:
  0.6 1.5 %collective-permute-start.2 = (f32[4,256,128]{2,1,0:T(8,128)}, f32[4,256,128]{2,1,0:T(8,128)S(1)}, u32[]{:S(2)}, u32[]{:S(2)}) collective-permute-start(f32[4,256,128]{2,1,0:T(8,128)} %books_ref.1), channel_id=1, source_target_pairs={{0,1},{1,0},{2,3},{3,2},{4,5},{5,4},{6,7},{7,6},{8,9},{9,8},{10,11... | collective-permute-start | bytes 1572872 | tf_op jit(solution)/shard_map/ppermute | solution.py:379
  2.1 1.1 %constant_dynamic-slice_fusion.1 = (f32[64,1024]{1,0:T(8,128)S(1)}, f32[64,1024]{1,0:T(8,128)S(1)}) fusion(f32[512,1024]{1,0:T(8,128)} %cent_ref.7, s32[]{:T(128)S(6)} %select_n.10, s32[]{:T(128)S(6)} %select_n.9), kind=kLoop, calls=%fused_computation.1 | loop fusion | bytes 1048584 | tf_op jit(solution)/shard_map/dynamic_slice | solution.py:380
  3.2 0.1 collective-permute-start
  3.3 3.6 %collective-permute-start.1 = (f32[64,1024]{1,0:T(8,128)S(1)}, f32[64,1024]{1,0:T(8,128)S(1)}, u32[]{:S(2)}, u32[]{:S(2)}) collective-permute-start(f32[64,1024]{1,0:T(8,128)S(1)} %get-tuple-element.25), channel_id=1, source_target_pairs={{1,2},{3,4},{5,6},{7,8},{9,10},{11,12},{13,14},{15,16},{17,18},{19... | collective-permute-start | bytes 786440 | tf_op jit(solution)/shard_map/ppermute | solution.py:382
  6.9 0.7 add_add_fusion
  7.6 0.0 collective-permute-done.inner_ref
  7.6 0.0 copy-start.4
  7.6 3.4 %collective-permute-done.1.outer_ref = f32[64,1024]{1,0:T(8,128)S(1)} collective-permute-done((f32[64,1024]{1,0:T(8,128)S(1)}, f32[64,1024]{1,0:T(8,128)S(1)}, u32[]{:S(2)}, u32[]{:S(2)}) %collective-permute-start.1) | collective-permute-done | bytes 262176 | tf_op jit(solution)/shard_map/ppermute | solution.py:382
  11.0 0.0 copy-start.5
  11.0 0.0 collective-permute-done.2.books_ref
  11.0 0.0 copy-start.3
  11.0 0.0 copy-done.4
  11.0 0.7 copy-done.5
  11.7 0.2 copy-done.3
  11.9 11.0 %quantize.2 = (bf16[2048,1024]{1,0:T(8,128)(2,1)}, f32[64,24,128]{2,1,0:T(8,128)}) custom-call(s32[2048]{0:T(1024)} %ids_smem.5, s32[3]{0:T(128)} %get-tuple-element.28.place_smem, s32[16,128]{1,0:T(8,128)} %bitcast.12, bf16[2048,1024]{1,0:T(8,128)(2,1)} %points_ref.5, f32[512,1024]{1,0:T(8,128)} %cent_ref.7, f32[64,1024]{1,0:T(8,128)} %copy-done.4, ...), custom_call_target="tpu_custom_call" | custom-call | flops 4000000000 | bytes 6000000 | tf_op jit(solution)/shard_map/quantize/pallas_call | solution.py:304
  22.8 0.0 collective-permute-start.3
  22.8 11.1 %quantize.3 = (bf16[2048,1024]{1,0:T(8,128)(2,1)}, f32[64,24,128]{2,1,0:T(8,128)}) custom-call(s32[2048]{0:T(1024)} %ids_smem.5, s32[3]{0:T(128)} %get-tuple-element.17.place_smem, s32[16,128]{1,0:T(8,128)} %bitcast.13, bf16[2048,1024]{1,0:T(8,128)(2,1)} %points_ref.5, f32[512,1024]{1,0:T(8,128)} %cent_ref.7, ...), custom_call_target="tpu_custom_call", output_to_operand_aliasing={{0}: (8, {})} | custom-call | flops 4000000000 | bytes 6000000 | tf_op jit(solution)/shard_map/quantize/pallas_call | solution.py:304
  33.9 0.0 collective-permute-done.3
  33.9 2.1 %add.19 = f32[64,24,128]{2,1,0:T(8,128)} add(f32[64,24,128]{2,1,0:T(8,128)} %get-tuple-element.16, f32[64,24,128]{2,1,0:T(8,128)S(1)} %collective-permute-done.3) | non-fusion elementwise | flops 196608 | bytes 2359296 | tf_op jit(solution)/shard_map/add | solution.py:394
  36.0 15.0 %all-to-all-start = ((f32[64,24,128]{2,1,0:T(8,128)}), f32[64,24,128]{2,1,0:T(8,128)S(1)}, u32[]{:S(2)}, u32[]{:S(2)}) async-start(f32[64,24,128]{2,1,0:T(8,128)} %add.19), calls=%async_computation | async-start | bytes 1572864 | tf_op jit(solution)/shard_map/all_to_all | solution.py:394
  51.0 6.6 %cluster_sums.1 = (f32[512,1024]{1,0:T(8,128)}, bf16[64,1024]{1,0:T(8,128)(2,1)}, bf16[64,1024]{1,0:T(8,128)(2,1)}) custom-call(s32[2048]{0:T(1024)} %ids_smem.5, s32[3]{0:T(128)} %get-tuple-element.17.place_smem, s32[16,128]{1,0:T(8,128)} %bitcast.14, bf16[2048,1024]{1,0:T(8,128)(2,1)} %points_ref.5, s32[4,128]{1,0:T(4,128)} %bitcast.8, f32[512,1024]{1,0:T(8,128)} %cent_ref.7), custom_call_target="tpu_custom_call" | custom-call | flops 2000000000 | bytes 8000000 | tf_op jit(solution)/shard_map/cluster_sums/pallas_call | solution.py:341
  57.6 0.0 copy-start
  57.6 0.0 copy-start.1
  57.7 0.0 copy-start.2
  57.7 0.8 collective-permute-start.4
  58.4 3.2 %collective-permute-start.5 = (bf16[64,1024]{1,0:T(8,128)(2,1)}, bf16[64,1024]{1,0:T(8,128)(2,1)S(1)}, u32[]{:S(2)}, u32[]{:S(2)}) collective-permute-start(bf16[64,1024]{1,0:T(8,128)(2,1)} %get-tuple-element.21), channel_id=1, source_target_pairs={{1,2},{3,4},{5,6},{7,8},{9,10},{11,12},{13,14},{15,16},{17,18},{19... | collective-permute-start | bytes 393224 | tf_op jit(solution)/shard_map/ppermute | solution.py:397
  61.7 0.7 constant_dynamic-slice_fusion.book_ref
  62.4 0.0 collective-permute-done.4.inner_in
  62.4 2.8 %collective-permute-done.5.outer_in = bf16[64,1024]{1,0:T(8,128)(2,1)S(1)} collective-permute-done((bf16[64,1024]{1,0:T(8,128)(2,1)}, bf16[64,1024]{1,0:T(8,128)(2,1)S(1)}, u32[]{:S(2)}, u32[]{:S(2)}) %collective-permute-start.5) | collective-permute-done | bytes 131104 | tf_op jit(solution)/shard_map/ppermute | solution.py:397
  65.2 0.9 %all-to-all-done.parts_ref = f32[64,24,128]{2,1,0:T(8,128)S(1)} async-done(((f32[64,24,128]{2,1,0:T(8,128)}), f32[64,24,128]{2,1,0:T(8,128)S(1)}, u32[]{:S(2)}, u32[]{:S(2)}) %all-to-all-start) | async-done | bytes 786464 | tf_op jit(solution)/shard_map/all_to_all | solution.py:394
  66.2 1.0 %moved_codes.1 = f32[64,16,128]{2,1,0:T(8,128)} custom-call(f32[64,24,128]{2,1,0:T(8,128)S(1)} %all-to-all-done.parts_ref, f32[16,128]{1,0:T(8,128)S(1)} %constant_dynamic-slice_fusion.book_ref), custom_call_target="tpu_custom_call" | custom-call | tf_op jit(solution)/shard_map/moved_codes/pallas_call | solution.py:405
  67.2 12.5 %all-to-all-start.1 = ((f32[64,16,128]{2,1,0:T(8,128)}), f32[64,16,128]{2,1,0:T(8,128)S(1)}, u32[]{:S(2)}, u32[]{:S(2)}) async-start(f32[64,16,128]{2,1,0:T(8,128)} %moved_codes.1), calls=%async_computation.1 | async-start | bytes 1048576 | tf_op jit(solution)/shard_map/all_to_all | solution.py:411
  79.7 0.0 copy-done
  79.7 0.0 copy-done.1
  79.7 0.0 copy-done.2
  79.7 2.5 %edge_clusters.1 = f32[512,1024]{1,0:T(8,128)} custom-call(s32[3]{0:T(128)S(1)} %copy-done.2, f32[512,1024]{1,0:T(8,128)} %get-tuple-element.18.moved_in, bf16[64,1024]{1,0:T(8,128)(2,1)S(1)} %collective-permute-done.4.inner_in, bf16[64,1024]{1,0:T(8,128)(2,1)S(1)} %collective-permute-done.5.outer_in, ...), custom_call_target="tpu_custom_call", output_to_operand_aliasing={{}: (1, {})} | custom-call | tf_op jit(solution)/shard_map/edge_clusters/pallas_call | solution.py:414
  82.2 8.4 %all-to-all-done.1 = f32[64,16,128]{2,1,0:T(8,128)S(1)} async-done(((f32[64,16,128]{2,1,0:T(8,128)}), f32[64,16,128]{2,1,0:T(8,128)S(1)}, u32[]{:S(2)}, u32[]{:S(2)}) %all-to-all-start.1) | async-done | bytes 524320 | tf_op jit(solution)/shard_map/all_to_all | solution.py:411
  90.6 0.8 copy.13
Async XLA Ops:
  0.6 10.4 %collective-permute-start.2 = (f32[4,256,128]{2,1,0:T(8,128)}, f32[4,256,128]{2,1,0:T(8,128)S(1)}, u32[]{:S(2)}, u32[]{:S(2)}) collective-permute-start(f32[4,256,128]{2,1,0:T(8,128)} %books_ref.1), channel_id=1, source_target_pairs={{0,1},{1,0},{2,3},{3,2},{4,5},{5,4},{6,7},{7,6},{8,9},{9,8},{10,11... | collective-permute-start | bytes 1572872 | tf_op jit(solution)/shard_map/ppermute | solution.py:379
  3.2 4.4 %collective-permute-start = (f32[64,1024]{1,0:T(8,128)S(1)}, f32[64,1024]{1,0:T(8,128)S(1)}, u32[]{:S(2)}, u32[]{:S(2)}) collective-permute-start(f32[64,1024]{1,0:T(8,128)S(1)} %get-tuple-element.26), channel_id=1, source_target_pairs={{0,1},{1,0},{2,3},{3,2},{4,5},{5,4},{6,7},{7,6},{8,9},{9,8},{10,11... | collective-permute-start | bytes 786440 | tf_op jit(solution)/shard_map/ppermute | solution.py:383
  3.3 7.7 %collective-permute-start.1 = (f32[64,1024]{1,0:T(8,128)S(1)}, f32[64,1024]{1,0:T(8,128)S(1)}, u32[]{:S(2)}, u32[]{:S(2)}) collective-permute-start(f32[64,1024]{1,0:T(8,128)S(1)} %get-tuple-element.25), channel_id=1, source_target_pairs={{1,2},{3,4},{5,6},{7,8},{9,10},{11,12},{13,14},{15,16},{17,18},{19... | collective-permute-start | bytes 786440 | tf_op jit(solution)/shard_map/ppermute | solution.py:382
  7.6 3.4 %copy-start.4 = (f32[64,1024]{1,0:T(8,128)}, f32[64,1024]{1,0:T(8,128)S(1)}, u32[]{:S(2)}) copy-start(f32[64,1024]{1,0:T(8,128)S(1)} %collective-permute-done.inner_ref) | copy-start | bytes 786436
  11.0 0.7 copy-start.5
  11.0 0.9 copy-start.3
  22.8 11.1 %collective-permute-start.3 = (f32[64,24,128]{2,1,0:T(8,128)}, f32[64,24,128]{2,1,0:T(8,128)S(1)}, u32[]{:S(2)}, u32[]{:S(2)}) collective-permute-start(f32[64,24,128]{2,1,0:T(8,128)} %get-tuple-element.19), channel_id=1, source_target_pairs={{0,1},{1,0},{2,3},{3,2},{4,5},{5,4},{6,7},{7,6},{8,9},{9,8},{10,11... | collective-permute-start | bytes 2359304 | tf_op jit(solution)/shard_map/ppermute | solution.py:391
  36.0 30.1 %all-to-all-start = ((f32[64,24,128]{2,1,0:T(8,128)}), f32[64,24,128]{2,1,0:T(8,128)S(1)}, u32[]{:S(2)}, u32[]{:S(2)}) async-start(f32[64,24,128]{2,1,0:T(8,128)} %add.19), calls=%async_computation | async-start | bytes 1572864 | tf_op jit(solution)/shard_map/all_to_all | solution.py:394
  57.6 22.1 %copy-start = (f32[512,1024]{1,0:T(8,128)S(1)}, f32[512,1024]{1,0:T(8,128)}, u32[]{:S(2)}) copy-start(f32[512,1024]{1,0:T(8,128)} %cent_ref.7) | copy-start | bytes 6291460
  57.6 22.1 %copy-start.1 = (s32[512]{0:T(512)S(1)}, s32[512]{0:T(512)}, u32[]{:S(2)}) copy-start(s32[512]{0:T(512)} %param.7) | copy-start | bytes 6148
  57.7 22.1 %copy-start.2 = (s32[3]{0:T(128)S(1)}, s32[3]{0:T(128)}, u32[]{:S(2)}) copy-start(s32[3]{0:T(128)} %get-tuple-element.17.place_smem) | copy-start | bytes 40
  57.7 4.7 %collective-permute-start.4 = (bf16[64,1024]{1,0:T(8,128)(2,1)}, bf16[64,1024]{1,0:T(8,128)(2,1)S(1)}, u32[]{:S(2)}, u32[]{:S(2)}) collective-permute-start(bf16[64,1024]{1,0:T(8,128)(2,1)} %get-tuple-element.20), channel_id=1, source_target_pairs={{0,1},{1,0},{2,3},{3,2},{4,5},{5,4},{6,7},{7,6},{8,9},{9,8},{10,11... | collective-permute-start | bytes 393224 | tf_op jit(solution)/shard_map/ppermute | solution.py:398
  58.4 6.8 %collective-permute-start.5 = (bf16[64,1024]{1,0:T(8,128)(2,1)}, bf16[64,1024]{1,0:T(8,128)(2,1)S(1)}, u32[]{:S(2)}, u32[]{:S(2)}) collective-permute-start(bf16[64,1024]{1,0:T(8,128)(2,1)} %get-tuple-element.21), channel_id=1, source_target_pairs={{1,2},{3,4},{5,6},{7,8},{9,10},{11,12},{13,14},{15,16},{17,18},{19... | collective-permute-start | bytes 393224 | tf_op jit(solution)/shard_map/ppermute | solution.py:397
  67.2 23.3 %all-to-all-start.1 = ((f32[64,16,128]{2,1,0:T(8,128)}), f32[64,16,128]{2,1,0:T(8,128)S(1)}, u32[]{:S(2)}, u32[]{:S(2)}) async-start(f32[64,16,128]{2,1,0:T(8,128)} %moved_codes.1), calls=%async_computation.1 | async-start | bytes 1048576 | tf_op jit(solution)/shard_map/all_to_all | solution.py:411

commit v4 on v3

--- a/solution.py
+++ b/solution.py
@@ -387,17 +387,13 @@
 
     theirs = jnp.stack([base, (1 - sub) * blocks, sub]).astype(jnp.int32)
     mine = jnp.stack([base, sub * blocks, sub]).astype(jnp.int32)
+    sums, sum_inner, sum_outer = cluster_sums(assign, mine, ids, points, counts, centroids)
+    theirs = lax.optimization_barrier((theirs, sum_inner))[0]
     rebuilt, away = quantize(assign, theirs, ids, points, centroids, inner, outer, other_book, owners, None)
     arrived = lax.ppermute(away, sub_axis, swap)
     rebuilt, kept = quantize(assign, mine, ids, points, centroids, inner, outer, codebook, owners, rebuilt)
 
     parts = lax.all_to_all(kept + arrived, rows_axis, 0, 0, tiled=True)
-    later = lax.optimization_barrier((mine, kept))[0]
-    sums, sum_inner, sum_outer = cluster_sums(assign, later, ids, points, counts, centroids)
-    sum_outer = lax.ppermute(sum_outer, MESH_AXES, across)
-    sum_inner = lax.ppermute(sum_inner, sub_axis, swap)
-    parts, sum_inner, sum_outer = lax.optimization_barrier((parts, sum_inner, sum_outer))
-
     book_rows = lax.dynamic_slice_in_dim(
         codebook.reshape(half * codes, subdim), lax.axis_index(rows_axis) * group, group, 0
     )
@@ -408,6 +404,9 @@
         compiler_params=pltpu.CompilerParams(vmem_limit_bytes=8 * 1024 * 1024),
         name="moved_codes",
     )(parts, book_rows)
+    moved, sum_inner, sum_outer = lax.optimization_barrier((moved, sum_inner, sum_outer))
+    sum_outer = lax.ppermute(sum_outer, MESH_AXES, across)
+    sum_inner = lax.ppermute(sum_inner, sub_axis, swap)
     moved = lax.all_to_all(moved, rows_axis, 0, 0, tiled=True)
 
     edge = pl.BlockSpec((RIM, width), lambda i, *_: (i * (own // RIM - 1), 0))

time: 92 us -> 87.7 us (0.953)
  the two profiles are of different devices: /device:TPU:1 before, /device:TPU:31 now
where the time goes in v4:
time: 87.7 us; the launch traced here: 87 us
  Pallas kernels  32 us (36%)
  starting transfers between devices  28.5 us (32%)
  waiting for transfers between devices  18.3 us (21%)
  local copies, waits for them, and re-layouts  4.08 us (5%)
  other arithmetic  3.39 us (4%)
    pallas_call x2, Pallas kernels, quantize(): pl.pallas_call(quant_kernel, grid_spec=pltpu.PrefetchScalarGridSpec(num_s...  21.9 us
    all_to_all x1, waiting for transfers between devices, body(): parts = lax.all_to_all(kept + arrived, rows_axis, 0, 0, tiled=True)  10.3 us
    all_to_all x1, starting transfers between devices, body(): parts = lax.all_to_all(kept + arrived, rows_axis, 0, 0, tiled=True)  10.1 us
    all_to_all x1, starting transfers between devices, body(): moved = lax.all_to_all(moved, rows_axis, 0, 0, tiled=True)  8.65 us
    ppermute x1, waiting for transfers between devices, body(): sum_outer = lax.ppermute(sum_outer, MESH_AXES, across)  7.48 us
    pallas_call x1, Pallas kernels, cluster_sums(): pl.pallas_call(sums_kernel, grid_spec=pltpu.PrefetchScalarGridSpec(num_sc...  6.61 us
    ppermute x1, starting transfers between devices, body(): outer = lax.ppermute(outer, MESH_AXES, across)  3.47 us
    ppermute x1, starting transfers between devices, body(): sum_outer = lax.ppermute(sum_outer, MESH_AXES, across)  3 us
  transfers between devices with their start and end apart: 8, of which 3 were waited for; matrix products, arithmetic and copies ran while one was open for 4% of the time, Pallas kernels for 23%

profile of v4, /device:TPU:31, one launch (start us, length us, event | category | flops | bytes accessed | tf_op | source)
XLA Modules:
  0.0 87.0 jit_solution(8767111272969624420)
XLA Ops:
  0.6 0.8 collective-permute-start.2
  1.4 1.1 %constant_dynamic-slice_fusion.1 = (f32[64,1024]{1,0:T(8,128)S(1)}, f32[64,1024]{1,0:T(8,128)S(1)}) fusion(f32[512,1024]{1,0:T(8,128)} %cent_ref.7, s32[]{:T(128)S(6)} %select_n.10, s32[]{:T(128)S(6)} %select_n.9), kind=kLoop, calls=%fused_computation.1 | loop fusion | bytes 1048584 | tf_op jit(solution)/shard_map/dynamic_slice | solution.py:380
  2.5 0.1 collective-permute-start
  2.6 3.5 %collective-permute-start.1 = (f32[64,1024]{1,0:T(8,128)S(1)}, f32[64,1024]{1,0:T(8,128)S(1)}, u32[]{:S(2)}, u32[]{:S(2)}) collective-permute-start(f32[64,1024]{1,0:T(8,128)S(1)} %get-tuple-element.25), channel_id=1, source_target_pairs={{1,2},{3,4},{5,6},{7,8},{9,10},{11,12},{13,14},{15,16},{17,18},{19... | collective-permute-start | bytes 786440 | tf_op jit(solution)/shard_map/ppermute | solution.py:382
  6.1 0.7 add_add_fusion.place_smem
  6.7 0.6 add_add_fusion.1.place_smem
  7.4 6.6 %cluster_sums.1 = (f32[512,1024]{1,0:T(8,128)}, bf16[64,1024]{1,0:T(8,128)(2,1)}, bf16[64,1024]{1,0:T(8,128)(2,1)}) custom-call(s32[2048]{0:T(1024)} %ids_smem.5, s32[3]{0:T(128)} %add_add_fusion.place_smem, s32[16,128]{1,0:T(8,128)} %bitcast.12, bf16[2048,1024]{1,0:T(8,128)(2,1)} %points_ref.5, s32[4,128]{1,0:T(4,128)} %bitcast.8, f32[512,1024]{1,0:T(8,128)} %cent_ref.7), custom_call_target="tpu_custom_call" | custom-call | flops 2000000000 | bytes 8000000 | tf_op jit(solution)/shard_map/cluster_sums/pallas_call | solution.py:341
  14.0 0.0 collective-permute-done.inner_ref
  14.0 0.0 copy-start.4
  14.0 0.5 collective-permute-done.1.outer_ref
  14.5 0.0 copy-start.5
  14.5 0.0 collective-permute-done.2.books_ref
  14.5 0.2 copy-done.4
  14.7 0.5 copy-done.5
  15.2 0.0 copy-start.3
  15.2 0.8 copy-done.3
  16.0 11.0 %quantize.2 = (bf16[2048,1024]{1,0:T(8,128)(2,1)}, f32[64,24,128]{2,1,0:T(8,128)}) custom-call(s32[2048]{0:T(1024)} %ids_smem.5, s32[3]{0:T(128)} %add_add_fusion.1.place_smem, s32[16,128]{1,0:T(8,128)} %bitcast.13, bf16[2048,1024]{1,0:T(8,128)(2,1)} %points_ref.5, f32[512,1024]{1,0:T(8,128)} %cent_ref.7, f32[64,1024]{1,0:T(8,128)} %copy-done.4, ...), custom_call_target="tpu_custom_call" | custom-call | flops 4000000000 | bytes 6000000 | tf_op jit(solution)/shard_map/quantize/pallas_call | solution.py:304
  26.9 0.0 collective-permute-start.3
  26.9 11.0 %quantize.3 = (bf16[2048,1024]{1,0:T(8,128)(2,1)}, f32[64,24,128]{2,1,0:T(8,128)}) custom-call(s32[2048]{0:T(1024)} %ids_smem.5, s32[3]{0:T(128)} %add_add_fusion.place_smem, s32[16,128]{1,0:T(8,128)} %bitcast.14, bf16[2048,1024]{1,0:T(8,128)(2,1)} %points_ref.5, f32[512,1024]{1,0:T(8,128)} %cent_ref.7, ...), custom_call_target="tpu_custom_call", output_to_operand_aliasing={{0}: (8, {})} | custom-call | flops 4000000000 | bytes 6000000 | tf_op jit(solution)/shard_map/quantize/pallas_call | solution.py:304
  37.9 0.0 collective-permute-done.3
  37.9 2.1 %add.19 = f32[64,24,128]{2,1,0:T(8,128)} add(f32[64,24,128]{2,1,0:T(8,128)} %get-tuple-element.19, f32[64,24,128]{2,1,0:T(8,128)S(1)} %collective-permute-done.3) | non-fusion elementwise | flops 196608 | bytes 2359296 | tf_op jit(solution)/shard_map/add | solution.py:396
  40.0 0.0 copy-start.7
  40.0 0.0 copy-start.6
  40.0 0.0 copy-start
  40.0 0.0 copy-start.1
  40.0 0.0 copy-start.2
  40.0 10.1 %all-to-all-start = ((f32[64,24,128]{2,1,0:T(8,128)}), f32[64,24,128]{2,1,0:T(8,128)S(1)}, u32[]{:S(2)}, u32[]{:S(2)}) async-start(f32[64,24,128]{2,1,0:T(8,128)} %add.19), calls=%async_computation | async-start | bytes 1572864 | tf_op jit(solution)/shard_map/all_to_all | solution.py:396
  50.1 0.7 constant_dynamic-slice_fusion.book_ref
  50.8 10.3 %all-to-all-done.parts_ref = f32[64,24,128]{2,1,0:T(8,128)S(1)} async-done(((f32[64,24,128]{2,1,0:T(8,128)}), f32[64,24,128]{2,1,0:T(8,128)S(1)}, u32[]{:S(2)}, u32[]{:S(2)}) %all-to-all-start) | async-done | bytes 786464 | tf_op jit(solution)/shard_map/all_to_all | solution.py:396
  61.1 1.0 %moved_codes.1 = f32[64,16,128]{2,1,0:T(8,128)} custom-call(f32[64,24,128]{2,1,0:T(8,128)S(1)} %all-to-all-done.parts_ref, f32[16,128]{1,0:T(8,128)S(1)} %constant_dynamic-slice_fusion.book_ref), custom_call_target="tpu_custom_call" | custom-call | tf_op jit(solution)/shard_map/moved_codes/pallas_call | solution.py:401
  62.1 8.6 %all-to-all-start.1 = ((f32[64,16,128]{2,1,0:T(8,128)}), f32[64,16,128]{2,1,0:T(8,128)S(1)}, u32[]{:S(2)}, u32[]{:S(2)}) async-start(f32[64,16,128]{2,1,0:T(8,128)} %moved_codes.1), calls=%async_computation.1 | async-start | bytes 1048576 | tf_op jit(solution)/shard_map/all_to_all | solution.py:410
  70.8 0.0 copy-done.7
  70.8 2.4 %collective-permute-start.4 = (bf16[64,1024]{1,0:T(8,128)(2,1)S(1)}, bf16[64,1024]{1,0:T(8,128)(2,1)S(1)}, u32[]{:S(2)}, u32[]{:S(2)}) collective-permute-start(bf16[64,1024]{1,0:T(8,128)(2,1)S(1)} %copy-done.7), channel_id=1, source_target_pairs={{0,1},{1,0},{2,3},{3,2},{4,5},{5,4},{6,7},{7,6},{8,9},{9,8},{10,11... | collective-permute-start | bytes 393224 | tf_op jit(solution)/shard_map/ppermute | solution.py:409
  73.2 0.0 copy-done.6
  73.2 3.0 %collective-permute-start.5 = (bf16[64,1024]{1,0:T(8,128)(2,1)S(1)}, bf16[64,1024]{1,0:T(8,128)(2,1)S(1)}, u32[]{:S(2)}, u32[]{:S(2)}) collective-permute-start(bf16[64,1024]{1,0:T(8,128)(2,1)S(1)} %copy-done.6), channel_id=1, source_target_pairs={{1,2},{3,4},{5,6},{7,8},{9,10},{11,12},{13,14},{15,16},{17,18},{19... | collective-permute-start | bytes 393224 | tf_op jit(solution)/shard_map/ppermute | solution.py:408
  76.2 0.0 collective-permute-done.4.inner_in
  76.3 7.5 %collective-permute-done.5.outer_in = bf16[64,1024]{1,0:T(8,128)(2,1)S(1)} collective-permute-done((bf16[64,1024]{1,0:T(8,128)(2,1)S(1)}, bf16[64,1024]{1,0:T(8,128)(2,1)S(1)}, u32[]{:S(2)}, u32[]{:S(2)}) %collective-permute-start.5) | collective-permute-done | bytes 131104 | tf_op jit(solution)/shard_map/ppermute | solution.py:408
  83.7 0.0 copy-done
  83.7 0.0 copy-done.1
  83.7 0.0 copy-done.2
  83.8 2.5 %edge_clusters.1 = f32[512,1024]{1,0:T(8,128)} custom-call(s32[3]{0:T(128)S(1)} %copy-done.2, f32[512,1024]{1,0:T(8,128)} %get-tuple-element.18.moved_in, bf16[64,1024]{1,0:T(8,128)(2,1)S(1)} %collective-permute-done.4.inner_in, bf16[64,1024]{1,0:T(8,128)(2,1)S(1)} %collective-permute-done.5.outer_in, ...), custom_call_target="tpu_custom_call", output_to_operand_aliasing={{}: (1, {})} | custom-call | tf_op jit(solution)/shard_map/edge_clusters/pallas_call | solution.py:413
  86.2 0.0 all-to-all-done.1
  86.2 0.8 copy.13
Async XLA Ops:
  0.6 13.8 %collective-permute-start.2 = (f32[4,256,128]{2,1,0:T(8,128)}, f32[4,256,128]{2,1,0:T(8,128)S(1)}, u32[]{:S(2)}, u32[]{:S(2)}) collective-permute-start(f32[4,256,128]{2,1,0:T(8,128)} %books_ref.1), channel_id=1, source_target_pairs={{0,1},{1,0},{2,3},{3,2},{4,5},{5,4},{6,7},{7,6},{8,9},{9,8},{10,11... | collective-permute-start | bytes 1572872 | tf_op jit(solution)/shard_map/ppermute | solution.py:379
  2.5 11.5 %collective-permute-start = (f32[64,1024]{1,0:T(8,128)S(1)}, f32[64,1024]{1,0:T(8,128)S(1)}, u32[]{:S(2)}, u32[]{:S(2)}) collective-permute-start(f32[64,1024]{1,0:T(8,128)S(1)} %get-tuple-element.26), channel_id=1, source_target_pairs={{0,1},{1,0},{2,3},{3,2},{4,5},{5,4},{6,7},{7,6},{8,9},{9,8},{10,11... | collective-permute-start | bytes 786440 | tf_op jit(solution)/shard_map/ppermute | solution.py:383
  2.6 11.9 %collective-permute-start.1 = (f32[64,1024]{1,0:T(8,128)S(1)}, f32[64,1024]{1,0:T(8,128)S(1)}, u32[]{:S(2)}, u32[]{:S(2)}) collective-permute-start(f32[64,1024]{1,0:T(8,128)S(1)} %get-tuple-element.25), channel_id=1, source_target_pairs={{1,2},{3,4},{5,6},{7,8},{9,10},{11,12},{13,14},{15,16},{17,18},{19... | collective-permute-start | bytes 786440 | tf_op jit(solution)/shard_map/ppermute | solution.py:382
  14.0 0.7 copy-start.4
  14.5 0.7 copy-start.5
  15.2 0.8 copy-start.3
  26.9 11.0 %collective-permute-start.3 = (f32[64,24,128]{2,1,0:T(8,128)}, f32[64,24,128]{2,1,0:T(8,128)S(1)}, u32[]{:S(2)}, u32[]{:S(2)}) collective-permute-start(f32[64,24,128]{2,1,0:T(8,128)} %get-tuple-element.20), channel_id=1, source_target_pairs={{0,1},{1,0},{2,3},{3,2},{4,5},{5,4},{6,7},{7,6},{8,9},{9,8},{10,11... | collective-permute-start | bytes 2359304 | tf_op jit(solution)/shard_map/ppermute | solution.py:393
  40.0 30.8 %copy-start.7 = (bf16[64,1024]{1,0:T(8,128)(2,1)S(1)}, bf16[64,1024]{1,0:T(8,128)(2,1)}, u32[]{:S(2)}) copy-start(bf16[64,1024]{1,0:T(8,128)(2,1)} %get-tuple-element.22) | copy-start | bytes 393220
  40.0 33.3 %copy-start.6 = (bf16[64,1024]{1,0:T(8,128)(2,1)S(1)}, bf16[64,1024]{1,0:T(8,128)(2,1)}, u32[]{:S(2)}) copy-start(bf16[64,1024]{1,0:T(8,128)(2,1)} %get-tuple-element.23) | copy-start | bytes 393220
  40.0 43.7 %copy-start = (f32[512,1024]{1,0:T(8,128)S(1)}, f32[512,1024]{1,0:T(8,128)}, u32[]{:S(2)}) copy-start(f32[512,1024]{1,0:T(8,128)} %cent_ref.7) | copy-start | bytes 6291460
  40.0 43.7 %copy-start.1 = (s32[512]{0:T(512)S(1)}, s32[512]{0:T(512)}, u32[]{:S(2)}) copy-start(s32[512]{0:T(512)} %param.7) | copy-start | bytes 6148
  40.0 43.7 %copy-start.2 = (s32[3]{0:T(128)S(1)}, s32[3]{0:T(128)}, u32[]{:S(2)}) copy-start(s32[3]{0:T(128)} %add_add_fusion.place_smem) | copy-start | bytes 40
  40.0 21.1 %all-to-all-start = ((f32[64,24,128]{2,1,0:T(8,128)}), f32[64,24,128]{2,1,0:T(8,128)S(1)}, u32[]{:S(2)}, u32[]{:S(2)}) async-start(f32[64,24,128]{2,1,0:T(8,128)} %add.19), calls=%async_computation | async-start | bytes 1572864 | tf_op jit(solution)/shard_map/all_to_all | solution.py:396
  62.1 24.1 %all-to-all-start.1 = ((f32[64,16,128]{2,1,0:T(8,128)}), f32[64,16,128]{2,1,0:T(8,128)S(1)}, u32[]{:S(2)}, u32[]{:S(2)}) async-start(f32[64,16,128]{2,1,0:T(8,128)} %moved_codes.1), calls=%async_computation.1 | async-start | bytes 1048576 | tf_op jit(solution)/shard_map/all_to_all | solution.py:410
  70.8 5.4 %collective-permute-start.4 = (bf16[64,1024]{1,0:T(8,128)(2,1)S(1)}, bf16[64,1024]{1,0:T(8,128)(2,1)S(1)}, u32[]{:S(2)}, u32[]{:S(2)}) collective-permute-start(bf16[64,1024]{1,0:T(8,128)(2,1)S(1)} %copy-done.7), channel_id=1, source_target_pairs={{0,1},{1,0},{2,3},{3,2},{4,5},{5,4},{6,7},{7,6},{8,9},{9,8},{10,11... | collective-permute-start | bytes 393224 | tf_op jit(solution)/shard_map/ppermute | solution.py:409
  73.2 10.5 %collective-permute-start.5 = (bf16[64,1024]{1,0:T(8,128)(2,1)S(1)}, bf16[64,1024]{1,0:T(8,128)(2,1)S(1)}, u32[]{:S(2)}, u32[]{:S(2)}) collective-permute-start(bf16[64,1024]{1,0:T(8,128)(2,1)S(1)} %copy-done.6), channel_id=1, source_target_pairs={{1,2},{3,4},{5,6},{7,8},{9,10},{11,12},{13,14},{15,16},{17,18},{19... | collective-permute-start | bytes 393224 | tf_op jit(solution)/shard_map/ppermute | solution.py:408

commit v5 on v4

--- a/solution.py
+++ b/solution.py
@@ -9,9 +9,11 @@
 from jax.sharding import PartitionSpec as P
 
 RIM = 64
+SPILL = 512
 TILE = 256
 CHUNK = 512
 COLS = 256
+WIDE = 512
 SPAN = 80
 PIECES = 3
 DEPTH = 256
@@ -28,12 +30,12 @@
     return pl.multiple_of(head, 16), pl.multiple_of(tail, 16), last
 
 
-def note_gaps(ids_smem, ids_ref, base, slots, gaps):
+def note_gaps(ids_smem, ids_ref, base, first, tiles, slots, gaps):
     per = TILE // 128
     missed = jnp.zeros((per, 128), jnp.float32)
-    for tile in range(ids_ref.shape[0] // per):
-        head, tail, _ = window_starts(ids_smem, base, tile, slots)
-        ids = ids_ref[tile * per : tile * per + per, :] - base
+    for tile in range(tiles):
+        head, tail, _ = window_starts(ids_smem, base, first + tile, slots)
+        ids = ids_ref[pl.ds((first + tile) * per, per), :] - base
         missed = jnp.where((ids >= head + SPAN) & (ids < tail), 1.0, missed)
     gaps[0] = jnp.max(missed).astype(jnp.int32)
 
@@ -67,7 +69,7 @@
 
     @pl.when(pl.program_id(0) == 0)
     def _():
-        note_gaps(ids_smem, ids_ref, base, slots, gaps)
+        note_gaps(ids_smem, ids_ref, base, 0, tiles, slots, gaps)
         for tile in range(tiles):
             head, tail, _ = window_starts(ids_smem, base, tile, slots)
             picks[tile, :SPAN] = pick_slots(tile, head, head, head + SPAN)
@@ -97,7 +99,7 @@
 
     down = acc[:RIM].astype(jnp.bfloat16)
     up = acc[RIM + own :].astype(jnp.bfloat16)
-    first = place_smem[2] == 0
+    first = place_smem[1] == 0
     inner_ref[...] = jnp.where(first, up, down)
     outer_ref[...] = jnp.where(first, down, up)
     for part in range(own // 128):
@@ -121,7 +123,7 @@
     count = jnp.broadcast_to(counts_ref[pl.ds(row, 1), :], (128, 128)).astype(jnp.float32)
     inverse = (1.0 / (count + 2.0)).T
     inverse = jnp.where(which == 0, inverse[:RIM], inverse[RIM:])
-    outer = which == place_smem[2]
+    outer = which == place_smem[1]
     spread = jnp.where(outer, outer_in[...].astype(jnp.float32), inner_in[...].astype(jnp.float32))
     for col in range(cent_ref.shape[1] // 128):
         cols = slice(col * 128, col * 128 + 128)
@@ -129,7 +131,7 @@
 
 
 def quant_kernel(
-    ids_smem, place_smem, ids_ref, points_ref, cent_ref, inner_ref, outer_ref, books_ref, *refs
+    first_at, extend, ids_smem, place_smem, ids_ref, points_ref, cent_ref, inner_ref, outer_ref, books_ref, *refs
 ):
     rebuilt_ref, payload_ref, hi_win, mid_win, lo_win, picks, ids_col, resid, books_low, norms, totals, mass, gaps = refs[-13:]
     base = place_smem[0]
@@ -139,6 +141,7 @@
     slots = own + 2 * RIM
     rows = points_ref.shape[0]
     tiles = rows // TILE
+    first_tile = 0 if first_at is None else place_smem[first_at]
     lane = lax.broadcasted_iota(jnp.int32, (1, DEPTH), 1)
     pattern = jnp.where(lane < PIECES * SPAN, lax.rem(lane, SPAN), -1)
 
@@ -159,15 +162,17 @@
 
     @pl.when(pl.program_id(0) == 0)
     def _():
-        note_gaps(ids_smem, ids_ref, base, slots, gaps)
+        note_gaps(ids_smem, ids_ref, base, first_tile, tiles, slots, gaps)
         for k in range(rows // 128):
-            ids_col[k * 128 : k * 128 + 128, :] = jnp.broadcast_to(ids_ref[k : k + 1, :] - base, (128, 128)).T
+            ids_col[k * 128 : k * 128 + 128, :] = jnp.broadcast_to(
+                ids_ref[pl.ds(first_tile * (TILE // 128) + k, 1), :] - base, (128, 128)
+            ).T
         for tile in range(tiles):
-            head, tail, _ = window_starts(ids_smem, base, tile, slots)
+            head, tail, _ = window_starts(ids_smem, base, first_tile + tile, slots)
             picks[tile, :, :DEPTH] = pick_rows(tile, head, head, head + SPAN)
             picks[tile, :, DEPTH:] = pick_rows(tile, tail, jnp.maximum(tail, head + SPAN), tail + SPAN)
 
-    first = place_smem[2] == 0
+    first = place_smem[1] == 0
     split(jnp.where(first, outer_ref[...], inner_ref[...]), 0)
     split(cent_ref[...], RIM)
     split(jnp.where(first, inner_ref[...], outer_ref[...]), RIM + own)
@@ -178,12 +183,12 @@
 
     def window(start):
         at = pl.ds(pl.multiple_of(start, 16), SPAN)
-        rest = jnp.zeros((DEPTH - PIECES * SPAN, COLS), jnp.bfloat16)
+        rest = jnp.zeros((DEPTH - PIECES * SPAN, WIDE), jnp.bfloat16)
         return [hi_win[at, :], mid_win[at, :], lo_win[at, :], rest]
 
     def subtract(tile):
         at = slice(tile * TILE, tile * TILE + TILE)
-        head, tail, _ = window_starts(ids_smem, base, tile, slots)
+        head, tail, _ = window_starts(ids_smem, base, first_tile + tile, slots)
         both = jnp.concatenate(window(head) + window(tail), axis=0)
         got = jnp.dot(picks[tile], both, preferred_element_type=jnp.float32)
         resid[at, :] = (points_ref[at, :].astype(jnp.float32) - got).astype(jnp.bfloat16)
@@ -202,12 +207,12 @@
                 fresh = points_ref[at, :].astype(jnp.float32) - got
                 ids = ids_col[at, :]
                 new = (ids >= low) & (ids < high)
-                for k in range(COLS // 128):
+                for k in range(WIDE // 128):
                     cols = slice(k * 128, k * 128 + 128)
                     kept = resid[at, cols].astype(jnp.float32)
                     resid[at, cols] = jnp.where(new, fresh[:, cols], kept).astype(jnp.bfloat16)
 
-            middle_windows(ids_smem, base, tile, slots, redo)
+            middle_windows(ids_smem, base, first_tile + tile, slots, redo)
 
     units = [(j, c) for j in range(subs) for c in range(rows // CHUNK)]
 
@@ -253,10 +258,15 @@
         for g in range(codes // group):
             at = slice(g * group, g * group + group)
             slot = j * (codes // group) + g
-            payload_ref[slot, :group, :] = totals[j, at, :]
+            total = totals[j, at, :]
             part = mass[j, at, :]
             part = part + pltpu.roll(part, 64, 1)
-            payload_ref[slot, group:, :] = jnp.where(left, part[:8], part[8:])
+            part = jnp.where(left, part[:8], part[8:])
+            if extend:
+                total = total + refs[0][slot, :group, :]
+                part = part + refs[0][slot, group:, :]
+            payload_ref[slot, :group, :] = total
+            payload_ref[slot, group:, :] = part
 
 
 def reduce_kernel(prior, parts_ref, book_ref, out_ref):
@@ -279,40 +289,54 @@
     return pl.BlockSpec(shape, lambda *_: (0,) * len(shape))
 
 
-def quantize(assign, place, ids, points, centroids, inner, outer, books, owners, rebuilt):
-    rows_here, width = points.shape
+def quantize(assign, place, half_at, first_at, rows, ids, points, centroids, inner, outer, books, owners, payload, rebuilt):
+    width = points.shape[1]
     half, codes, subdim = books.shape
     own = centroids.shape[0]
-    subs = COLS // subdim
+    subs = WIDE // subdim
     steps = half // subs
     group = half * codes // owners
     slots = own + 2 * RIM
 
     def columns(count):
-        return pl.BlockSpec((count, COLS), lambda i, ids, place: (0, place[1] + i))
-
+        return pl.BlockSpec((count, WIDE), lambda i, ids, place: (0, place[half_at] + i))
+
+    if first_at is None:
+        block = columns(rows)
+    else:
+        block = pl.BlockSpec(
+            (pl.Element(rows), pl.Element(WIDE)),
+            lambda i, ids, place: (
+                pl.multiple_of(place[first_at] * TILE, TILE),
+                pl.multiple_of((place[half_at] + i) * WIDE, WIDE),
+            ),
+        )
+    sums = pl.BlockSpec((owners // steps, group + 8, subdim), lambda i, *_: (i, 0, 0))
     in_specs = [
-        whole(ids.shape), columns(rows_here), columns(own), columns(RIM), columns(RIM),
+        whole(ids.shape), block, columns(own), columns(RIM), columns(RIM),
         pl.BlockSpec((subs, codes, subdim), lambda i, *_: (i, 0, 0)),
     ]
     inputs = [assign, place, ids, points, centroids, inner, outer, books]
     aliases = {}
+    if payload is not None:
+        in_specs.append(sums)
+        inputs.append(payload)
     if rebuilt is not None:
         aliases = {len(inputs): 0}
         in_specs.append(pl.BlockSpec(memory_space=pl.ANY))
         inputs.append(rebuilt)
     return pl.pallas_call(
-        quant_kernel,
+        functools.partial(quant_kernel, first_at, payload is not None),
         grid_spec=pltpu.PrefetchScalarGridSpec(
             num_scalar_prefetch=2,
             grid=(steps,),
             in_specs=in_specs,
-            out_specs=[columns(rows_here), pl.BlockSpec((owners // steps, group + 8, subdim), lambda i, *_: (i, 0, 0))],
-            scratch_shapes=[pltpu.VMEM((slots, COLS), jnp.bfloat16)] * 3
+            out_specs=[block, sums],
+            scratch_shapes=[pltpu.VMEM((slots, WIDE), jnp.bfloat16)] * 3
             + [
-                pltpu.VMEM((rows_here // TILE, TILE, 2 * DEPTH), jnp.bfloat16),
-                pltpu.VMEM((rows_here, 128), jnp.int32),
-                pltpu.VMEM((rows_here, COLS), jnp.bfloat16),
+                pltpu.VMEM((rows // TILE, TILE, 2 * DEPTH), jnp.bfloat16),
+                pltpu.VMEM((rows, 128), jnp.int32),
+                pltpu.VMEM((rows, WIDE), jnp.bfloat16),
                 pltpu.VMEM((subs, codes, subdim), jnp.bfloat16),
                 pltpu.VMEM((subs, codes, 128), jnp.float32),
                 pltpu.VMEM((subs, codes, subdim), jnp.float32),
@@ -321,12 +345,12 @@
             ],
         ),
         out_shape=[
-            jax.ShapeDtypeStruct(points.shape, jnp.bfloat16),
+            jax.ShapeDtypeStruct((points.shape[0], width), jnp.bfloat16),
             jax.ShapeDtypeStruct((owners, group + 8, subdim), jnp.float32),
         ],
         input_output_aliases=aliases,
         compiler_params=pltpu.CompilerParams(vmem_limit_bytes=58 * 1024 * 1024),
-        cost_estimate=pl.CostEstimate(flops=4 * 10**9, bytes_accessed=6 * 10**6, transcendentals=2 * 10**6),
+        cost_estimate=pl.CostEstimate(flops=2 * 10**6 * rows, bytes_accessed=3000 * rows, transcendentals=1000 * rows),
         name="quantize",
     )(*inputs)
 
@@ -372,7 +396,7 @@
     sub = lax.axis_index(sub_axis)
     position = lax.axis_index(rows_axis) * lax.axis_size(sub_axis) + sub
     base = position * own - RIM
-    blocks = half * subdim // COLS
+    blocks = half * subdim // WIDE
     swap = [(0, 1), (1, 0)]
     pairs = [(i, i + 1) for i in range(1, places - 1, 2)]
     across = pairs + [(j, i) for i, j in pairs]
@@ -385,18 +409,28 @@
     counts = cluster_counts.reshape(own // 128, 128)
     group = half * codes // owners
 
-    theirs = jnp.stack([base, (1 - sub) * blocks, sub]).astype(jnp.int32)
-    mine = jnp.stack([base, sub * blocks, sub]).astype(jnp.int32)
-    sums, sum_inner, sum_outer = cluster_sums(assign, mine, ids, points, counts, centroids)
-    theirs = lax.optimization_barrier((theirs, sum_inner))[0]
-    rebuilt, away = quantize(assign, theirs, ids, points, centroids, inner, outer, other_book, owners, None)
+    near = rows_here - SPILL
+    place = jnp.stack(
+        [base, sub, sub * blocks, (1 - sub) * blocks, (1 - sub) * (SPILL // TILE), sub * (near // TILE)]
+    ).astype(jnp.int32)
+    rebuilt, away = quantize(
+        assign, place, 3, 4, near, ids, points, centroids, inner, inner, other_book, owners, None, None
+    )
+    rebuilt, away = quantize(
+        assign, place, 3, 5, SPILL, ids, points, centroids, inner, outer, other_book, owners, away, rebuilt
+    )
     arrived = lax.ppermute(away, sub_axis, swap)
-    rebuilt, kept = quantize(assign, mine, ids, points, centroids, inner, outer, codebook, owners, rebuilt)
-
-    parts = lax.all_to_all(kept + arrived, rows_axis, 0, 0, tiled=True)
+    rebuilt, kept = quantize(
+        assign, place, 2, None, rows_here, ids, points, centroids, inner, outer, codebook, owners, None, rebuilt
+    )
+
     book_rows = lax.dynamic_slice_in_dim(
         codebook.reshape(half * codes, subdim), lax.axis_index(rows_axis) * group, group, 0
     )
+    chip, book_rows, after = lax.optimization_barrier((kept + arrived, book_rows, place))
+    parts = lax.all_to_all(chip, rows_axis, 0, 0, tiled=True)
+    sums, sum_inner, sum_outer = cluster_sums(assign, after, ids, points, counts, centroids)
+    parts, sums, sum_inner, sum_outer = lax.optimization_barrier((parts, sums, sum_inner, sum_outer))
     prior = rows_here * places / codes
     moved = pl.pallas_call(
         functools.partial(reduce_kernel, prior),
@@ -422,7 +456,7 @@
         input_output_aliases={1: 0},
         compiler_params=pltpu.CompilerParams(vmem_limit_bytes=8 * 1024 * 1024),
         name="edge_clusters",
-    )(mine, sums, sum_inner, sum_outer, counts, centroids)
+    )(place, sums, sum_inner, sum_outer, counts, centroids)
     return (rebuilt, moved_centroids, moved.reshape(codebook.shape))
 
 

time: 87.7 us -> 85.1 us (0.970)
  waiting for transfers between devices: 18.3 us -> 11.6 us
  Pallas kernels: 32 us -> 36.5 us
  other arithmetic: 3.39 us -> 2.1 us
    all_to_all x1, waiting for transfers between devices: 10.3 us -> 3.92 us  [body(): parts = lax.all_to_all(chip, rows_axis, 0, 0, tiled=True)]
    pallas_call x2 -> x3, Pallas kernels: 21.9 us -> 25.9 us  [quantize(): pl.pallas_call(functools.partial(quant_kernel, first_at, payload is not N...]
    another operation x2 -> x0, other arithmetic: 1.3 us -> none  [the longest x1 0.65 us: body(): mine = jnp.stack([base, sub * blocks, sub]).astype(jnp.int32)]
    unnamed x17 -> x13, local copies, waits for them, and re-layouts: 2.31 us -> 2.39 us
  transfers between devices with their start and end apart: 8 -> 8, of which waited for: 3 -> 2; matrix products, arithmetic and copies ran while one was open for 4% -> 3% of each run, Pallas kernels for 23% -> 35%
where the time goes in v5:
time: 85.1 us; the launch traced here: 84.5 us
  Pallas kernels  36.5 us (43%)
  starting transfers between devices  28.7 us (34%)
  waiting for transfers between devices  11.6 us (14%)
  local copies, waits for them, and re-layouts  4.84 us (6%)
  other arithmetic  2.1 us (2%)
    pallas_call x3, Pallas kernels, quantize(): pl.pallas_call(functools.partial(quant_kernel, first_at, payload is not N...  25.9 us
    all_to_all x1, starting transfers between devices, body(): parts = lax.all_to_all(chip, rows_axis, 0, 0, tiled=True)  10.3 us
    all_to_all x1, starting transfers between devices, body(): moved = lax.all_to_all(moved, rows_axis, 0, 0, tiled=True)  8.66 us
    ppermute x1, waiting for transfers between devices, body(): sum_outer = lax.ppermute(sum_outer, MESH_AXES, across)  7.7 us
    pallas_call x1, Pallas kernels, cluster_sums(): pl.pallas_call(sums_kernel, grid_spec=pltpu.PrefetchScalarGridSpec(num_sc...  7.03 us
    all_to_all x1, waiting for transfers between devices, body(): parts = lax.all_to_all(chip, rows_axis, 0, 0, tiled=True)  3.92 us
    ppermute x1, starting transfers between devices, body(): outer = lax.ppermute(outer, MESH_AXES, across)  3.47 us
    ppermute x1, starting transfers between devices, body(): sum_outer = lax.ppermute(sum_outer, MESH_AXES, across)  2.99 us
  transfers between devices with their start and end apart: 8, of which 2 were waited for; matrix products, arithmetic and copies ran while one was open for 3% of the time, Pallas kernels for 35%

profile of v5, /device:TPU:31, one launch (start us, length us, event | category | flops | bytes accessed | tf_op | source)
XLA Modules:
  0.0 84.5 jit_solution(888912325907761548)
XLA Ops:
  0.6 0.8 collective-permute-start.2
  1.4 1.1 %constant_dynamic-slice_fusion.1 = (f32[64,1024]{1,0:T(8,128)S(1)}, f32[64,1024]{1,0:T(8,128)S(1)}) fusion(f32[512,1024]{1,0:T(8,128)} %cent_ref.9, s32[]{:T(128)S(6)} %select_n.10, s32[]{:T(128)S(6)} %select_n.9), kind=kLoop, calls=%fused_computation.1 | loop fusion | bytes 1048584 | tf_op jit(solution)/shard_map/dynamic_slice | solution.py:404
  2.5 0.1 collective-permute-start
  2.6 3.5 %collective-permute-start.1 = (f32[64,1024]{1,0:T(8,128)S(1)}, f32[64,1024]{1,0:T(8,128)S(1)}, u32[]{:S(2)}, u32[]{:S(2)}) collective-permute-start(f32[64,1024]{1,0:T(8,128)S(1)} %get-tuple-element.41), channel_id=1, source_target_pairs={{1,2},{3,4},{5,6},{7,8},{9,10},{11,12},{13,14},{15,16},{17,18},{19... | collective-permute-start | bytes 786440 | tf_op jit(solution)/shard_map/ppermute | solution.py:406
  6.1 0.7 stack.24.place_smem
  6.7 0.0 collective-permute-done.inner_ref.outer_ref
  6.7 0.0 copy-start.4
  6.7 0.0 collective-permute-done.2.books_ref
  6.8 0.0 copy-start.3
  6.8 0.7 copy-done.4
  7.4 0.2 copy-done.3
  7.6 9.1 %quantize.3 = (bf16[2048,1024]{1,0:T(8,128)(2,1)}, f32[64,24,128]{2,1,0:T(8,128)}) custom-call(s32[2048]{0:T(1024)} %ids_smem.7, s32[6]{0:T(128)} %stack.24.place_smem, s32[16,128]{1,0:T(8,128)} %bitcast.12, bf16[2048,1024]{1,0:T(8,128)(2,1)} %points_ref.7, f32[512,1024]{1,0:T(8,128)} %cent_ref.9, f32[64,1024]{1,0:T(8,128)} %copy-done.4, ...), custom_call_target="tpu_custom_call" | custom-call | flops 3072000000 | bytes 4608000 | tf_op jit(solution)/shard_map/quantize/pallas_call | solution.py:328
  16.8 0.0 collective-permute-done.1.outer_ref
  16.8 0.0 copy-start.5
  16.8 0.7 copy-done.5
  17.5 6.0 %quantize.4 = (bf16[2048,1024]{1,0:T(8,128)(2,1)}, f32[64,24,128]{2,1,0:T(8,128)}) custom-call(s32[2048]{0:T(1024)} %ids_smem.7, s32[6]{0:T(128)} %stack.24.place_smem, s32[16,128]{1,0:T(8,128)} %bitcast.13, bf16[2048,1024]{1,0:T(8,128)(2,1)} %points_ref.7, f32[512,1024]{1,0:T(8,128)} %cent_ref.9, ...), custom_call_target="tpu_custom_call", output_to_operand_aliasing={{0}: (9, {})} | custom-call | flops 1024000000 | bytes 1536000 | tf_op jit(solution)/shard_map/quantize/pallas_call | solution.py:328
  23.5 0.0 collective-permute-start.3
  23.5 0.7 constant_dynamic-slice_fusion.book_ref
  24.2 10.8 %quantize.5 = (bf16[2048,1024]{1,0:T(8,128)(2,1)}, f32[64,24,128]{2,1,0:T(8,128)}) custom-call(s32[2048]{0:T(1024)} %ids_smem.7, s32[6]{0:T(128)} %stack.24.place_smem, s32[16,128]{1,0:T(8,128)} %bitcast.14, bf16[2048,1024]{1,0:T(8,128)(2,1)} %points_ref.7, f32[512,1024]{1,0:T(8,128)} %cent_ref.9, ...), custom_call_target="tpu_custom_call", output_to_operand_aliasing={{0}: (8, {})} | custom-call | flops 4096000000 | bytes 6144000 | tf_op jit(solution)/shard_map/quantize/pallas_call | solution.py:328
  35.0 0.0 collective-permute-done.3
  35.0 2.1 %add.19 = f32[64,24,128]{2,1,0:T(8,128)} add(f32[64,24,128]{2,1,0:T(8,128)} %get-tuple-element.26, f32[64,24,128]{2,1,0:T(8,128)S(1)} %collective-permute-done.3) | non-fusion elementwise | flops 196608 | bytes 2359296 | tf_op jit(solution)/shard_map/add | solution.py:430
  37.1 10.3 %all-to-all-start = ((f32[64,24,128]{2,1,0:T(8,128)}), f32[64,24,128]{2,1,0:T(8,128)S(1)}, u32[]{:S(2)}, u32[]{:S(2)}) async-start(f32[64,24,128]{2,1,0:T(8,128)} %add.19), calls=%async_computation | async-start | bytes 1572864 | tf_op jit(solution)/shard_map/all_to_all | solution.py:431
  47.4 0.0 copy-start
  47.4 0.0 copy-start.1
  47.4 0.0 copy-start.2
  47.4 7.0 %cluster_sums.1 = (f32[512,1024]{1,0:T(8,128)}, bf16[64,1024]{1,0:T(8,128)(2,1)}, bf16[64,1024]{1,0:T(8,128)(2,1)}) custom-call(s32[2048]{0:T(1024)} %ids_smem.7, s32[6]{0:T(128)} %stack.24.place_smem, s32[16,128]{1,0:T(8,128)} %bitcast.15, bf16[2048,1024]{1,0:T(8,128)(2,1)} %points_ref.7, s32[4,128]{1,0:T(4,128)} %bitcast.9, f32[512,1024]{1,0:T(8,128)} %cent_ref.9), custom_call_target="tpu_custom_call" | custom-call | flops 2000000000 | bytes 8000000 | tf_op jit(solution)/shard_map/cluster_sums/pallas_call | solution.py:365
  54.4 3.9 %all-to-all-done.parts_ref = f32[64,24,128]{2,1,0:T(8,128)S(1)} async-done(((f32[64,24,128]{2,1,0:T(8,128)}), f32[64,24,128]{2,1,0:T(8,128)S(1)}, u32[]{:S(2)}, u32[]{:S(2)}) %all-to-all-start) | async-done | bytes 786464 | tf_op jit(solution)/shard_map/all_to_all | solution.py:431
  58.3 1.0 %moved_codes.1 = f32[64,16,128]{2,1,0:T(8,128)} custom-call(f32[64,24,128]{2,1,0:T(8,128)S(1)} %all-to-all-done.parts_ref, f32[16,128]{1,0:T(8,128)S(1)} %constant_dynamic-slice_fusion.book_ref), custom_call_target="tpu_custom_call" | custom-call | tf_op jit(solution)/shard_map/moved_codes/pallas_call | solution.py:435
  59.4 8.7 %all-to-all-start.1 = ((f32[64,16,128]{2,1,0:T(8,128)}), f32[64,16,128]{2,1,0:T(8,128)S(1)}, u32[]{:S(2)}, u32[]{:S(2)}) async-start(f32[64,16,128]{2,1,0:T(8,128)} %moved_codes.1), calls=%async_computation.1 | async-start | bytes 1048576 | tf_op jit(solution)/shard_map/all_to_all | solution.py:444
  68.1 2.4 %collective-permute-start.4 = (bf16[64,1024]{1,0:T(8,128)(2,1)}, bf16[64,1024]{1,0:T(8,128)(2,1)S(1)}, u32[]{:S(2)}, u32[]{:S(2)}) collective-permute-start(bf16[64,1024]{1,0:T(8,128)(2,1)} %get-tuple-element.38), channel_id=1, source_target_pairs={{0,1},{1,0},{2,3},{3,2},{4,5},{5,4},{6,7},{7,6},{8,9},{9,8},{10,11... | collective-permute-start | bytes 393224 | tf_op jit(solution)/shard_map/ppermute | solution.py:443
  70.5 3.0 %collective-permute-start.5 = (bf16[64,1024]{1,0:T(8,128)(2,1)}, bf16[64,1024]{1,0:T(8,128)(2,1)S(1)}, u32[]{:S(2)}, u32[]{:S(2)}) collective-permute-start(bf16[64,1024]{1,0:T(8,128)(2,1)} %get-tuple-element.39), channel_id=1, source_target_pairs={{1,2},{3,4},{5,6},{7,8},{9,10},{11,12},{13,14},{15,16},{17,18},{19... | collective-permute-start | bytes 393224 | tf_op jit(solution)/shard_map/ppermute | solution.py:442
  73.5 0.0 collective-permute-done.4.inner_in
  73.5 7.7 %collective-permute-done.5.outer_in = bf16[64,1024]{1,0:T(8,128)(2,1)S(1)} collective-permute-done((bf16[64,1024]{1,0:T(8,128)(2,1)}, bf16[64,1024]{1,0:T(8,128)(2,1)S(1)}, u32[]{:S(2)}, u32[]{:S(2)}) %collective-permute-start.5) | collective-permute-done | bytes 131104 | tf_op jit(solution)/shard_map/ppermute | solution.py:442
  81.2 0.0 copy-done
  81.2 0.0 copy-done.1
  81.2 0.0 copy-done.2
  81.2 2.5 %edge_clusters.1 = f32[512,1024]{1,0:T(8,128)} custom-call(s32[6]{0:T(128)S(1)} %copy-done.1, f32[512,1024]{1,0:T(8,128)} %get-tuple-element.33.moved_in, bf16[64,1024]{1,0:T(8,128)(2,1)S(1)} %collective-permute-done.4.inner_in, bf16[64,1024]{1,0:T(8,128)(2,1)S(1)} %collective-permute-done.5.outer_in, ...), custom_call_target="tpu_custom_call", output_to_operand_aliasing={{}: (1, {})} | custom-call | tf_op jit(solution)/shard_map/edge_clusters/pallas_call | solution.py:447
  83.7 0.0 all-to-all-done.1
  83.7 0.8 copy.15
Async XLA Ops:
  0.6 6.1 %collective-permute-start.2 = (f32[4,256,128]{2,1,0:T(8,128)}, f32[4,256,128]{2,1,0:T(8,128)S(1)}, u32[]{:S(2)}, u32[]{:S(2)}) collective-permute-start(f32[4,256,128]{2,1,0:T(8,128)} %books_ref.1), channel_id=1, source_target_pairs={{0,1},{1,0},{2,3},{3,2},{4,5},{5,4},{6,7},{7,6},{8,9},{9,8},{10,11... | collective-permute-start | bytes 1572872 | tf_op jit(solution)/shard_map/ppermute | solution.py:403
  2.5 4.3 %collective-permute-start = (f32[64,1024]{1,0:T(8,128)S(1)}, f32[64,1024]{1,0:T(8,128)S(1)}, u32[]{:S(2)}, u32[]{:S(2)}) collective-permute-start(f32[64,1024]{1,0:T(8,128)S(1)} %get-tuple-element.42), channel_id=1, source_target_pairs={{0,1},{1,0},{2,3},{3,2},{4,5},{5,4},{6,7},{7,6},{8,9},{9,8},{10,11... | collective-permute-start | bytes 786440 | tf_op jit(solution)/shard_map/ppermute | solution.py:407
  2.6 14.2 %collective-permute-start.1 = (f32[64,1024]{1,0:T(8,128)S(1)}, f32[64,1024]{1,0:T(8,128)S(1)}, u32[]{:S(2)}, u32[]{:S(2)}) collective-permute-start(f32[64,1024]{1,0:T(8,128)S(1)} %get-tuple-element.41), channel_id=1, source_target_pairs={{1,2},{3,4},{5,6},{7,8},{9,10},{11,12},{13,14},{15,16},{17,18},{19... | collective-permute-start | bytes 786440 | tf_op jit(solution)/shard_map/ppermute | solution.py:406
  6.7 0.7 copy-start.4
  6.8 0.9 %copy-start.3 = (f32[4,256,128]{2,1,0:T(8,128)}, f32[4,256,128]{2,1,0:T(8,128)S(1)}, u32[]{:S(2)}) copy-start(f32[4,256,128]{2,1,0:T(8,128)S(1)} %collective-permute-done.2.books_ref) | copy-start | bytes 1572868
  16.8 0.7 copy-start.5
  23.5 11.5 %collective-permute-start.3 = (f32[64,24,128]{2,1,0:T(8,128)}, f32[64,24,128]{2,1,0:T(8,128)S(1)}, u32[]{:S(2)}, u32[]{:S(2)}) collective-permute-start(f32[64,24,128]{2,1,0:T(8,128)} %get-tuple-element.27), channel_id=1, source_target_pairs={{0,1},{1,0},{2,3},{3,2},{4,5},{5,4},{6,7},{7,6},{8,9},{9,8},{10,11... | collective-permute-start | bytes 2359304 | tf_op jit(solution)/shard_map/ppermute | solution.py:422
  37.1 21.2 %all-to-all-start = ((f32[64,24,128]{2,1,0:T(8,128)}), f32[64,24,128]{2,1,0:T(8,128)S(1)}, u32[]{:S(2)}, u32[]{:S(2)}) async-start(f32[64,24,128]{2,1,0:T(8,128)} %add.19), calls=%async_computation | async-start | bytes 1572864 | tf_op jit(solution)/shard_map/all_to_all | solution.py:431
  47.4 33.8 %copy-start = (f32[512,1024]{1,0:T(8,128)S(1)}, f32[512,1024]{1,0:T(8,128)}, u32[]{:S(2)}) copy-start(f32[512,1024]{1,0:T(8,128)} %cent_ref.9) | copy-start | bytes 6291460
  47.4 33.8 %copy-start.1 = (s32[6]{0:T(128)S(1)}, s32[6]{0:T(128)}, u32[]{:S(2)}) copy-start(s32[6]{0:T(128)} %stack.24.place_smem) | copy-start | bytes 76
  47.4 33.8 %copy-start.2 = (s32[512]{0:T(512)S(1)}, s32[512]{0:T(512)}, u32[]{:S(2)}) copy-start(s32[512]{0:T(512)} %param.7) | copy-start | bytes 6148
  59.4 24.3 %all-to-all-start.1 = ((f32[64,16,128]{2,1,0:T(8,128)}), f32[64,16,128]{2,1,0:T(8,128)S(1)}, u32[]{:S(2)}, u32[]{:S(2)}) async-start(f32[64,16,128]{2,1,0:T(8,128)} %moved_codes.1), calls=%async_computation.1 | async-start | bytes 1048576 | tf_op jit(solution)/shard_map/all_to_all | solution.py:444
  68.1 5.4 %collective-permute-start.4 = (bf16[64,1024]{1,0:T(8,128)(2,1)}, bf16[64,1024]{1,0:T(8,128)(2,1)S(1)}, u32[]{:S(2)}, u32[]{:S(2)}) collective-permute-start(bf16[64,1024]{1,0:T(8,128)(2,1)} %get-tuple-element.38), channel_id=1, source_target_pairs={{0,1},{1,0},{2,3},{3,2},{4,5},{5,4},{6,7},{7,6},{8,9},{9,8},{10,11... | collective-permute-start | bytes 393224 | tf_op jit(solution)/shard_map/ppermute | solution.py:443
  70.5 10.7 %collective-permute-start.5 = (bf16[64,1024]{1,0:T(8,128)(2,1)}, bf16[64,1024]{1,0:T(8,128)(2,1)S(1)}, u32[]{:S(2)}, u32[]{:S(2)}) collective-permute-start(bf16[64,1024]{1,0:T(8,128)(2,1)} %get-tuple-element.39), channel_id=1, source_target_pairs={{1,2},{3,4},{5,6},{7,8},{9,10},{11,12},{13,14},{15,16},{17,18},{19... | collective-permute-start | bytes 393224 | tf_op jit(solution)/shard_map/ppermute | solution.py:442

commit v6 on v5

--- a/solution.py
+++ b/solution.py
@@ -349,7 +349,7 @@
             jax.ShapeDtypeStruct((owners, group + 8, subdim), jnp.float32),
         ],
         input_output_aliases=aliases,
-        compiler_params=pltpu.CompilerParams(vmem_limit_bytes=58 * 1024 * 1024),
+        compiler_params=pltpu.CompilerParams(vmem_limit_bytes=52 * 1024 * 1024),
         cost_estimate=pl.CostEstimate(flops=2 * 10**6 * rows, bytes_accessed=3000 * rows, transcendentals=1000 * rows),
         name="quantize",
     )(*inputs)

time: 85.1 us -> 82 us (0.964)
  Pallas kernels: 36.5 us -> 34.7 us
  local copies, waits for them, and re-layouts: 4.84 us -> 3.54 us
    pallas_call x3, Pallas kernels: 25.9 us -> 24.2 us  [quantize(): pl.pallas_call(functools.partial(quant_kernel, first_at, payload is not N...]
    unnamed x13 -> x17, local copies, waits for them, and re-layouts: 2.39 us -> 2.39 us
  transfers between devices with their start and end apart: 8 -> 8, of which waited for: 2 -> 2; matrix products, arithmetic and copies ran while one was open for 3% -> 1% of each run, Pallas kernels for 35% -> 35%
where the time goes in v6:
time: 82 us; the launch traced here: 81.4 us
  Pallas kernels  34.7 us (42%)
  starting transfers between devices  28.7 us (35%)
  waiting for transfers between devices  11.6 us (14%)
  local copies, waits for them, and re-layouts  3.54 us (4%)
  other arithmetic  2.11 us (3%)
    pallas_call x3, Pallas kernels, quantize(): pl.pallas_call(functools.partial(quant_kernel, first_at, payload is not N...  24.2 us
    all_to_all x1, starting transfers between devices, body(): parts = lax.all_to_all(chip, rows_axis, 0, 0, tiled=True)  10.2 us
    all_to_all x1, starting transfers between devices, body(): moved = lax.all_to_all(moved, rows_axis, 0, 0, tiled=True)  8.66 us
    ppermute x1, waiting for transfers between devices, body(): sum_outer = lax.ppermute(sum_outer, MESH_AXES, across)  7.7 us
    pallas_call x1, Pallas kernels, cluster_sums(): pl.pallas_call(sums_kernel, grid_spec=pltpu.PrefetchScalarGridSpec(num_sc...  7.03 us
    all_to_all x1, waiting for transfers between devices, body(): parts = lax.all_to_all(chip, rows_axis, 0, 0, tiled=True)  3.92 us
    ppermute x1, starting transfers between devices, body(): outer = lax.ppermute(outer, MESH_AXES, across)  3.47 us
    ppermute x1, starting transfers between devices, body(): sum_outer = lax.ppermute(sum_outer, MESH_AXES, across)  2.99 us
  transfers between devices with their start and end apart: 8, of which 2 were waited for; matrix products, arithmetic and copies ran while one was open for 1% of the time, Pallas kernels for 35%

profile of v6, /device:TPU:31, one launch (start us, length us, event | category | flops | bytes accessed | tf_op | source)
XLA Modules:
  0.0 81.4 jit_solution(16487658900416444011)
XLA Ops:
  0.6 0.8 collective-permute-start.2
  1.4 1.1 %constant_dynamic-slice_fusion.1 = (f32[64,1024]{1,0:T(8,128)S(1)}, f32[64,1024]{1,0:T(8,128)S(1)}) fusion(f32[512,1024]{1,0:T(8,128)} %cent_ref.9, s32[]{:T(128)S(6)} %select_n.10, s32[]{:T(128)S(6)} %select_n.9), kind=kLoop, calls=%fused_computation.1 | loop fusion | bytes 1048584 | tf_op jit(solution)/shard_map/dynamic_slice | solution.py:404
  2.5 0.1 collective-permute-start
  2.6 3.5 %collective-permute-start.1 = (f32[64,1024]{1,0:T(8,128)S(1)}, f32[64,1024]{1,0:T(8,128)S(1)}, u32[]{:S(2)}, u32[]{:S(2)}) collective-permute-start(f32[64,1024]{1,0:T(8,128)S(1)} %get-tuple-element.41), channel_id=1, source_target_pairs={{1,2},{3,4},{5,6},{7,8},{9,10},{11,12},{13,14},{15,16},{17,18},{19... | collective-permute-start | bytes 786440 | tf_op jit(solution)/shard_map/ppermute | solution.py:406
  6.1 0.1 stack.24.place_smem
  6.1 0.0 copy-start.4
  6.1 0.0 collective-permute-done.inner_ref.outer_ref
  6.1 0.0 collective-permute-done.2.books_ref
  6.2 0.0 copy-start.2
  6.2 0.7 copy-done.2
  6.9 8.5 %quantize.3 = (bf16[2048,1024]{1,0:T(8,128)(2,1)}, f32[64,24,128]{2,1,0:T(8,128)S(1)}) custom-call(s32[2048]{0:T(1024)S(1)} %copy-done.2, s32[6]{0:T(128)S(1)} %stack.24.place_smem, s32[16,128]{1,0:T(8,128)S(1)} %bitcast.10, bf16[2048,1024]{1,0:T(8,128)(2,1)} %points_ref.7, f32[512,1024]{1,0:T(8,128)} %cent_ref.9, ...), custom_call_target="tpu_custom_call" | custom-call | flops 3072000000 | bytes 4608000 | tf_op jit(solution)/shard_map/quantize/pallas_call | solution.py:328
  15.4 0.0 copy-start.1
  15.4 0.9 %copy-done.1 = f32[64,24,128]{2,1,0:T(8,128)} copy-done((f32[64,24,128]{2,1,0:T(8,128)}, f32[64,24,128]{2,1,0:T(8,128)S(1)}, u32[]{:S(2)}) %copy-start.1) | copy-done | bytes 786456
  16.3 0.0 collective-permute-done.1.outer_ref
  16.3 0.0 copy-start.7
  16.3 0.0 copy-start.3
  16.3 5.5 %quantize.4 = (bf16[2048,1024]{1,0:T(8,128)(2,1)}, f32[64,24,128]{2,1,0:T(8,128)S(1)}) custom-call(s32[2048]{0:T(1024)S(1)} %copy-done.2, s32[6]{0:T(128)S(1)} %stack.24.place_smem, s32[16,128]{1,0:T(8,128)S(1)} %bitcast.11, bf16[2048,1024]{1,0:T(8,128)(2,1)} %points_ref.7, f32[512,1024]{1,0:T(8,128)} %cent_ref.9, ...), custom_call_target="tpu_custom_call", output_to_operand_aliasing={{0}: (9, {})} | custom-call | flops 1024000000 | bytes 1536000 | tf_op jit(solution)/shard_map/quantize/pallas_call | solution.py:328
  21.8 0.0 collective-permute-start.3
  21.8 0.0 copy-done.7
  21.8 0.0 copy-done.4
  21.8 0.0 copy-done.3
  21.8 10.2 %quantize.5 = (bf16[2048,1024]{1,0:T(8,128)(2,1)}, f32[64,24,128]{2,1,0:T(8,128)S(1)}) custom-call(s32[2048]{0:T(1024)S(1)} %copy-done.3, s32[6]{0:T(128)S(1)} %stack.24.place_smem, s32[16,128]{1,0:T(8,128)S(1)} %bitcast.12, bf16[2048,1024]{1,0:T(8,128)(2,1)} %points_ref.7, f32[512,1024]{1,0:T(8,128)} %cent_ref.9, ...), custom_call_target="tpu_custom_call", output_to_operand_aliasing={{0}: (8, {})} | custom-call | flops 4096000000 | bytes 6144000 | tf_op jit(solution)/shard_map/quantize/pallas_call | solution.py:328
  31.9 0.0 collective-permute-done.3
  31.9 2.1 %add.19 = f32[64,24,128]{2,1,0:T(8,128)} add(f32[64,24,128]{2,1,0:T(8,128)S(1)} %get-tuple-element.26, f32[64,24,128]{2,1,0:T(8,128)} %collective-permute-done.3) | non-fusion elementwise | flops 196608 | bytes 2359296 | tf_op jit(solution)/shard_map/add | solution.py:430
  34.1 10.2 %all-to-all-start = ((f32[64,24,128]{2,1,0:T(8,128)}), f32[64,24,128]{2,1,0:T(8,128)S(1)}, u32[]{:S(2)}, u32[]{:S(2)}) async-start(f32[64,24,128]{2,1,0:T(8,128)} %add.19), calls=%async_computation | async-start | bytes 1572864 | tf_op jit(solution)/shard_map/all_to_all | solution.py:431
  44.3 0.0 copy-start
  44.3 0.0 copy-start.5
  44.3 0.0 copy-start.6
  44.3 7.0 %cluster_sums.1 = (f32[512,1024]{1,0:T(8,128)}, bf16[64,1024]{1,0:T(8,128)(2,1)}, bf16[64,1024]{1,0:T(8,128)(2,1)}) custom-call(s32[2048]{0:T(1024)} %ids_smem.7, s32[6]{0:T(128)} %copy-done.4, s32[16,128]{1,0:T(8,128)} %bitcast.9, bf16[2048,1024]{1,0:T(8,128)(2,1)} %points_ref.7, s32[4,128]{1,0:T(4,128)} %bitcast.13, f32[512,1024]{1,0:T(8,128)} %cent_ref.9), custom_call_target="tpu_custom_call" | custom-call | flops 2000000000 | bytes 8000000 | tf_op jit(solution)/shard_map/cluster_sums/pallas_call | solution.py:365
  51.4 3.9 %all-to-all-done.parts_ref = f32[64,24,128]{2,1,0:T(8,128)S(1)} async-done(((f32[64,24,128]{2,1,0:T(8,128)}), f32[64,24,128]{2,1,0:T(8,128)S(1)}, u32[]{:S(2)}, u32[]{:S(2)}) %all-to-all-start) | async-done | bytes 786464 | tf_op jit(solution)/shard_map/all_to_all | solution.py:431
  55.3 1.0 %moved_codes.1 = f32[64,16,128]{2,1,0:T(8,128)} custom-call(f32[64,24,128]{2,1,0:T(8,128)S(1)} %all-to-all-done.parts_ref, f32[16,128]{1,0:T(8,128)S(1)} %constant_dynamic-slice_fusion.book_ref), custom_call_target="tpu_custom_call" | custom-call | tf_op jit(solution)/shard_map/moved_codes/pallas_call | solution.py:435
  56.3 8.7 %all-to-all-start.1 = ((f32[64,16,128]{2,1,0:T(8,128)}), f32[64,16,128]{2,1,0:T(8,128)S(1)}, u32[]{:S(2)}, u32[]{:S(2)}) async-start(f32[64,16,128]{2,1,0:T(8,128)} %moved_codes.1), calls=%async_computation.1 | async-start | bytes 1048576 | tf_op jit(solution)/shard_map/all_to_all | solution.py:444
  65.0 2.4 %collective-permute-start.4 = (bf16[64,1024]{1,0:T(8,128)(2,1)}, bf16[64,1024]{1,0:T(8,128)(2,1)S(1)}, u32[]{:S(2)}, u32[]{:S(2)}) collective-permute-start(bf16[64,1024]{1,0:T(8,128)(2,1)} %get-tuple-element.38), channel_id=1, source_target_pairs={{0,1},{1,0},{2,3},{3,2},{4,5},{5,4},{6,7},{7,6},{8,9},{9,8},{10,11... | collective-permute-start | bytes 393224 | tf_op jit(solution)/shard_map/ppermute | solution.py:443
  67.4 3.0 %collective-permute-start.5 = (bf16[64,1024]{1,0:T(8,128)(2,1)}, bf16[64,1024]{1,0:T(8,128)(2,1)S(1)}, u32[]{:S(2)}, u32[]{:S(2)}) collective-permute-start(bf16[64,1024]{1,0:T(8,128)(2,1)} %get-tuple-element.39), channel_id=1, source_target_pairs={{1,2},{3,4},{5,6},{7,8},{9,10},{11,12},{13,14},{15,16},{17,18},{19... | collective-permute-start | bytes 393224 | tf_op jit(solution)/shard_map/ppermute | solution.py:442
  70.4 0.0 collective-permute-done.4.inner_in
  70.4 7.7 %collective-permute-done.5.outer_in = bf16[64,1024]{1,0:T(8,128)(2,1)S(1)} collective-permute-done((bf16[64,1024]{1,0:T(8,128)(2,1)}, bf16[64,1024]{1,0:T(8,128)(2,1)S(1)}, u32[]{:S(2)}, u32[]{:S(2)}) %collective-permute-start.5) | collective-permute-done | bytes 131104 | tf_op jit(solution)/shard_map/ppermute | solution.py:442
  78.1 0.0 copy-done
  78.1 0.0 copy-done.5
  78.2 0.0 copy-done.6
  78.2 2.5 %edge_clusters.1 = f32[512,1024]{1,0:T(8,128)} custom-call(s32[6]{0:T(128)S(1)} %copy-done.5, f32[512,1024]{1,0:T(8,128)} %get-tuple-element.33.moved_in, bf16[64,1024]{1,0:T(8,128)(2,1)S(1)} %collective-permute-done.4.inner_in, bf16[64,1024]{1,0:T(8,128)(2,1)S(1)} %collective-permute-done.5.outer_in, ...), custom_call_target="tpu_custom_call", output_to_operand_aliasing={{}: (1, {})} | custom-call | tf_op jit(solution)/shard_map/edge_clusters/pallas_call | solution.py:447
  80.6 0.0 all-to-all-done.1
  80.6 0.8 copy.15
  (1 shorter events, 0.0 us)
Async XLA Ops:
  0.6 5.5 %collective-permute-start.2 = (f32[4,256,128]{2,1,0:T(8,128)}, f32[4,256,128]{2,1,0:T(8,128)S(1)}, u32[]{:S(2)}, u32[]{:S(2)}) collective-permute-start(f32[4,256,128]{2,1,0:T(8,128)} %books_ref.1), channel_id=1, source_target_pairs={{0,1},{1,0},{2,3},{3,2},{4,5},{5,4},{6,7},{7,6},{8,9},{9,8},{10,11... | collective-permute-start | bytes 1572872 | tf_op jit(solution)/shard_map/ppermute | solution.py:403
  2.5 3.7 %collective-permute-start = (f32[64,1024]{1,0:T(8,128)S(1)}, f32[64,1024]{1,0:T(8,128)S(1)}, u32[]{:S(2)}, u32[]{:S(2)}) collective-permute-start(f32[64,1024]{1,0:T(8,128)S(1)} %get-tuple-element.42), channel_id=1, source_target_pairs={{0,1},{1,0},{2,3},{3,2},{4,5},{5,4},{6,7},{7,6},{8,9},{9,8},{10,11... | collective-permute-start | bytes 786440 | tf_op jit(solution)/shard_map/ppermute | solution.py:407
  2.6 13.7 %collective-permute-start.1 = (f32[64,1024]{1,0:T(8,128)S(1)}, f32[64,1024]{1,0:T(8,128)S(1)}, u32[]{:S(2)}, u32[]{:S(2)}) collective-permute-start(f32[64,1024]{1,0:T(8,128)S(1)} %get-tuple-element.41), channel_id=1, source_target_pairs={{1,2},{3,4},{5,6},{7,8},{9,10},{11,12},{13,14},{15,16},{17,18},{19... | collective-permute-start | bytes 786440 | tf_op jit(solution)/shard_map/ppermute | solution.py:406
  6.1 15.6 %copy-start.4 = (s32[6]{0:T(128)}, s32[6]{0:T(128)S(1)}, u32[]{:S(2)}) copy-start(s32[6]{0:T(128)S(1)} %stack.24.place_smem) | copy-start | bytes 76
  6.2 0.7 copy-start.2
  15.4 0.9 %copy-start.1 = (f32[64,24,128]{2,1,0:T(8,128)}, f32[64,24,128]{2,1,0:T(8,128)S(1)}, u32[]{:S(2)}) copy-start(f32[64,24,128]{2,1,0:T(8,128)S(1)} %get-tuple-element.22.refs_0_) | copy-start | bytes 2359300
  16.3 5.5 %copy-start.7 = (f32[4,256,128]{2,1,0:T(8,128)S(1)}, f32[4,256,128]{2,1,0:T(8,128)}, u32[]{:S(2)}) copy-start(f32[4,256,128]{2,1,0:T(8,128)} %books_ref.1) | copy-start | bytes 1572868
  16.3 5.5 %copy-start.3 = (s32[2048]{0:T(1024)S(1)}, s32[2048]{0:T(1024)}, u32[]{:S(2)}) copy-start(s32[2048]{0:T(1024)} %ids_smem.7) | copy-start | bytes 24580
  21.8 10.2 %collective-permute-start.3 = (f32[64,24,128]{2,1,0:T(8,128)S(1)}, f32[64,24,128]{2,1,0:T(8,128)}, u32[]{:S(2)}, u32[]{:S(2)}) collective-permute-start(f32[64,24,128]{2,1,0:T(8,128)S(1)} %get-tuple-element.27), channel_id=1, source_target_pairs={{0,1},{1,0},{2,3},{3,2},{4,5},{5,4},{6,7},{7,6},{8,9},{9,8},{10,11... | collective-permute-start | bytes 2359304 | tf_op jit(solution)/shard_map/ppermute | solution.py:422
  34.1 21.2 %all-to-all-start = ((f32[64,24,128]{2,1,0:T(8,128)}), f32[64,24,128]{2,1,0:T(8,128)S(1)}, u32[]{:S(2)}, u32[]{:S(2)}) async-start(f32[64,24,128]{2,1,0:T(8,128)} %add.19), calls=%async_computation | async-start | bytes 1572864 | tf_op jit(solution)/shard_map/all_to_all | solution.py:431
  44.3 33.8 %copy-start = (f32[512,1024]{1,0:T(8,128)S(1)}, f32[512,1024]{1,0:T(8,128)}, u32[]{:S(2)}) copy-start(f32[512,1024]{1,0:T(8,128)} %cent_ref.9) | copy-start | bytes 6291460
  44.3 33.8 %copy-start.5 = (s32[6]{0:T(128)S(1)}, s32[6]{0:T(128)}, u32[]{:S(2)}) copy-start(s32[6]{0:T(128)} %copy-done.4) | copy-start | bytes 76
  44.3 33.8 %copy-start.6 = (s32[512]{0:T(512)S(1)}, s32[512]{0:T(512)}, u32[]{:S(2)}) copy-start(s32[512]{0:T(512)} %param.7) | copy-start | bytes 6148
  56.3 24.3 %all-to-all-start.1 = ((f32[64,16,128]{2,1,0:T(8,128)}), f32[64,16,128]{2,1,0:T(8,128)S(1)}, u32[]{:S(2)}, u32[]{:S(2)}) async-start(f32[64,16,128]{2,1,0:T(8,128)} %moved_codes.1), calls=%async_computation.1 | async-start | bytes 1048576 | tf_op jit(solution)/shard_map/all_to_all | solution.py:444
  65.0 5.4 %collective-permute-start.4 = (bf16[64,1024]{1,0:T(8,128)(2,1)}, bf16[64,1024]{1,0:T(8,128)(2,1)S(1)}, u32[]{:S(2)}, u32[]{:S(2)}) collective-permute-start(bf16[64,1024]{1,0:T(8,128)(2,1)} %get-tuple-element.38), channel_id=1, source_target_pairs={{0,1},{1,0},{2,3},{3,2},{4,5},{5,4},{6,7},{7,6},{8,9},{9,8},{10,11... | collective-permute-start | bytes 393224 | tf_op jit(solution)/shard_map/ppermute | solution.py:443
  67.4 10.7 %collective-permute-start.5 = (bf16[64,1024]{1,0:T(8,128)(2,1)}, bf16[64,1024]{1,0:T(8,128)(2,1)S(1)}, u32[]{:S(2)}, u32[]{:S(2)}) collective-permute-start(bf16[64,1024]{1,0:T(8,128)(2,1)} %get-tuple-element.39), channel_id=1, source_target_pairs={{1,2},{3,4},{5,6},{7,8},{9,10},{11,12},{13,14},{15,16},{17,18},{19... | collective-permute-start | bytes 393224 | tf_op jit(solution)/shard_map/ppermute | solution.py:442

commit v7 on v6

--- a/solution.py
+++ b/solution.py
@@ -349,7 +349,7 @@
             jax.ShapeDtypeStruct((owners, group + 8, subdim), jnp.float32),
         ],
         input_output_aliases=aliases,
-        compiler_params=pltpu.CompilerParams(vmem_limit_bytes=52 * 1024 * 1024),
+        compiler_params=pltpu.CompilerParams(vmem_limit_bytes=51 * 1024 * 1024),
         cost_estimate=pl.CostEstimate(flops=2 * 10**6 * rows, bytes_accessed=3000 * rows, transcendentals=1000 * rows),
         name="quantize",
     )(*inputs)

time: 82 us -> 80.9 us (0.987)
  local copies, waits for them, and re-layouts: 3.54 us -> 2.66 us
    unnamed x17 -> x15, local copies, waits for them, and re-layouts: 2.39 us -> 1.51 us
where the time goes in v7:
time: 80.9 us; the launch traced here: 80.3 us
  Pallas kernels  34.5 us (43%)
  starting transfers between devices  28.7 us (35%)
  waiting for transfers between devices  11.6 us (14%)
  local copies, waits for them, and re-layouts  2.66 us (3%)
  other arithmetic  2.09 us (3%)
    pallas_call x3, Pallas kernels, quantize(): pl.pallas_call(functools.partial(quant_kernel, first_at, payload is not N...  23.9 us
    all_to_all x1, starting transfers between devices, body(): parts = lax.all_to_all(chip, rows_axis, 0, 0, tiled=True)  10.2 us
    all_to_all x1, starting transfers between devices, body(): moved = lax.all_to_all(moved, rows_axis, 0, 0, tiled=True)  8.66 us
    ppermute x1, waiting for transfers between devices, body(): sum_outer = lax.ppermute(sum_outer, MESH_AXES, across)  7.7 us
    pallas_call x1, Pallas kernels, cluster_sums(): pl.pallas_call(sums_kernel, grid_spec=pltpu.PrefetchScalarGridSpec(num_sc...  7.03 us
    all_to_all x1, waiting for transfers between devices, body(): parts = lax.all_to_all(chip, rows_axis, 0, 0, tiled=True)  3.92 us
    ppermute x1, starting transfers between devices, body(): outer = lax.ppermute(outer, MESH_AXES, across)  3.47 us
    ppermute x1, starting transfers between devices, body(): sum_outer = lax.ppermute(sum_outer, MESH_AXES, across)  2.99 us
  transfers between devices with their start and end apart: 8, of which 2 were waited for; matrix products, arithmetic and copies ran while one was open for 1% of the time, Pallas kernels for 35%

profile of v7, /device:TPU:31, one launch (start us, length us, event | category | flops | bytes accessed | tf_op | source)
XLA Modules:
  0.0 80.3 jit_solution(6200127963309412045)
XLA Ops:
  0.6 0.8 collective-permute-start.2
  1.4 1.1 %constant_dynamic-slice_fusion.1 = (f32[64,1024]{1,0:T(8,128)S(1)}, f32[64,1024]{1,0:T(8,128)S(1)}) fusion(f32[512,1024]{1,0:T(8,128)} %cent_ref.9, s32[]{:T(128)S(6)} %select_n.10, s32[]{:T(128)S(6)} %select_n.9), kind=kLoop, calls=%fused_computation.1 | loop fusion | bytes 1048584 | tf_op jit(solution)/shard_map/dynamic_slice | solution.py:404
  2.5 0.1 collective-permute-start
  2.6 3.5 %collective-permute-start.1 = (f32[64,1024]{1,0:T(8,128)S(1)}, f32[64,1024]{1,0:T(8,128)S(1)}, u32[]{:S(2)}, u32[]{:S(2)}) collective-permute-start(f32[64,1024]{1,0:T(8,128)S(1)} %get-tuple-element.41), channel_id=1, source_target_pairs={{1,2},{3,4},{5,6},{7,8},{9,10},{11,12},{13,14},{15,16},{17,18},{19... | collective-permute-start | bytes 786440 | tf_op jit(solution)/shard_map/ppermute | solution.py:406
  6.1 0.1 stack.24.place_smem
  6.1 0.0 copy-start.3
  6.1 0.0 collective-permute-done.inner_ref.outer_ref
  6.1 0.0 collective-permute-done.2.books_ref
  6.2 0.0 copy-start.1
  6.2 0.7 copy-done.1
  6.9 8.5 %quantize.3 = (bf16[2048,1024]{1,0:T(8,128)(2,1)}, f32[64,24,128]{2,1,0:T(8,128)S(1)}) custom-call(s32[2048]{0:T(1024)S(1)} %copy-done.1, s32[6]{0:T(128)S(1)} %stack.24.place_smem, s32[16,128]{1,0:T(8,128)S(1)} %bitcast.10, bf16[2048,1024]{1,0:T(8,128)(2,1)} %points_ref.7, f32[512,1024]{1,0:T(8,128)} %cent_ref.9, ...), custom_call_target="tpu_custom_call" | custom-call | flops 3072000000 | bytes 4608000 | tf_op jit(solution)/shard_map/quantize/pallas_call | solution.py:328
  15.4 0.0 collective-permute-done.1.outer_ref
  15.4 0.0 copy-start.6
  15.4 0.0 copy-start.2
  15.4 5.2 %quantize.4 = (bf16[2048,1024]{1,0:T(8,128)(2,1)}, f32[64,24,128]{2,1,0:T(8,128)S(1)}) custom-call(s32[2048]{0:T(1024)S(1)} %copy-done.1, s32[6]{0:T(128)S(1)} %stack.24.place_smem, s32[16,128]{1,0:T(8,128)S(1)} %bitcast.11, bf16[2048,1024]{1,0:T(8,128)(2,1)} %points_ref.7, f32[512,1024]{1,0:T(8,128)} %cent_ref.9, ...), custom_call_target="tpu_custom_call", output_to_operand_aliasing={{0}: (9, {})} | custom-call | flops 1024000000 | bytes 1536000 | tf_op jit(solution)/shard_map/quantize/pallas_call | solution.py:328
  20.7 0.0 collective-permute-start.3
  20.7 0.0 copy-done.6
  20.7 0.0 copy-done.3
  20.7 0.0 copy-done.2
  20.7 10.2 %quantize.5 = (bf16[2048,1024]{1,0:T(8,128)(2,1)}, f32[64,24,128]{2,1,0:T(8,128)S(1)}) custom-call(s32[2048]{0:T(1024)S(1)} %copy-done.2, s32[6]{0:T(128)S(1)} %stack.24.place_smem, s32[16,128]{1,0:T(8,128)S(1)} %bitcast.12, bf16[2048,1024]{1,0:T(8,128)(2,1)} %points_ref.7, f32[512,1024]{1,0:T(8,128)} %cent_ref.9, ...), custom_call_target="tpu_custom_call", output_to_operand_aliasing={{0}: (8, {})} | custom-call | flops 4096000000 | bytes 6144000 | tf_op jit(solution)/shard_map/quantize/pallas_call | solution.py:328
  30.8 0.0 collective-permute-done.3
  30.8 2.1 %add.19 = f32[64,24,128]{2,1,0:T(8,128)} add(f32[64,24,128]{2,1,0:T(8,128)S(1)} %get-tuple-element.26, f32[64,24,128]{2,1,0:T(8,128)} %collective-permute-done.3) | non-fusion elementwise | flops 196608 | bytes 2359296 | tf_op jit(solution)/shard_map/add | solution.py:430
  32.9 10.2 %all-to-all-start = ((f32[64,24,128]{2,1,0:T(8,128)}), f32[64,24,128]{2,1,0:T(8,128)S(1)}, u32[]{:S(2)}, u32[]{:S(2)}) async-start(f32[64,24,128]{2,1,0:T(8,128)} %add.19), calls=%async_computation | async-start | bytes 1572864 | tf_op jit(solution)/shard_map/all_to_all | solution.py:431
  43.2 0.0 copy-start
  43.2 0.0 copy-start.4
  43.2 0.0 copy-start.5
  43.2 7.0 %cluster_sums.1 = (f32[512,1024]{1,0:T(8,128)}, bf16[64,1024]{1,0:T(8,128)(2,1)}, bf16[64,1024]{1,0:T(8,128)(2,1)}) custom-call(s32[2048]{0:T(1024)} %ids_smem.7, s32[6]{0:T(128)} %copy-done.3, s32[16,128]{1,0:T(8,128)} %bitcast.9, bf16[2048,1024]{1,0:T(8,128)(2,1)} %points_ref.7, s32[4,128]{1,0:T(4,128)} %bitcast.13, f32[512,1024]{1,0:T(8,128)} %cent_ref.9), custom_call_target="tpu_custom_call" | custom-call | flops 2000000000 | bytes 8000000 | tf_op jit(solution)/shard_map/cluster_sums/pallas_call | solution.py:365
  50.3 3.9 %all-to-all-done.parts_ref = f32[64,24,128]{2,1,0:T(8,128)S(1)} async-done(((f32[64,24,128]{2,1,0:T(8,128)}), f32[64,24,128]{2,1,0:T(8,128)S(1)}, u32[]{:S(2)}, u32[]{:S(2)}) %all-to-all-start) | async-done | bytes 786464 | tf_op jit(solution)/shard_map/all_to_all | solution.py:431
  54.2 1.0 %moved_codes.1 = f32[64,16,128]{2,1,0:T(8,128)} custom-call(f32[64,24,128]{2,1,0:T(8,128)S(1)} %all-to-all-done.parts_ref, f32[16,128]{1,0:T(8,128)S(1)} %constant_dynamic-slice_fusion.book_ref), custom_call_target="tpu_custom_call" | custom-call | tf_op jit(solution)/shard_map/moved_codes/pallas_call | solution.py:435
  55.2 8.7 %all-to-all-start.1 = ((f32[64,16,128]{2,1,0:T(8,128)}), f32[64,16,128]{2,1,0:T(8,128)S(1)}, u32[]{:S(2)}, u32[]{:S(2)}) async-start(f32[64,16,128]{2,1,0:T(8,128)} %moved_codes.1), calls=%async_computation.1 | async-start | bytes 1048576 | tf_op jit(solution)/shard_map/all_to_all | solution.py:444
  63.9 2.4 %collective-permute-start.4 = (bf16[64,1024]{1,0:T(8,128)(2,1)}, bf16[64,1024]{1,0:T(8,128)(2,1)S(1)}, u32[]{:S(2)}, u32[]{:S(2)}) collective-permute-start(bf16[64,1024]{1,0:T(8,128)(2,1)} %get-tuple-element.38), channel_id=1, source_target_pairs={{0,1},{1,0},{2,3},{3,2},{4,5},{5,4},{6,7},{7,6},{8,9},{9,8},{10,11... | collective-permute-start | bytes 393224 | tf_op jit(solution)/shard_map/ppermute | solution.py:443
  66.3 3.0 %collective-permute-start.5 = (bf16[64,1024]{1,0:T(8,128)(2,1)}, bf16[64,1024]{1,0:T(8,128)(2,1)S(1)}, u32[]{:S(2)}, u32[]{:S(2)}) collective-permute-start(bf16[64,1024]{1,0:T(8,128)(2,1)} %get-tuple-element.39), channel_id=1, source_target_pairs={{1,2},{3,4},{5,6},{7,8},{9,10},{11,12},{13,14},{15,16},{17,18},{19... | collective-permute-start | bytes 393224 | tf_op jit(solution)/shard_map/ppermute | solution.py:442
  69.3 0.0 collective-permute-done.4.inner_in
  69.3 7.7 %collective-permute-done.5.outer_in = bf16[64,1024]{1,0:T(8,128)(2,1)S(1)} collective-permute-done((bf16[64,1024]{1,0:T(8,128)(2,1)}, bf16[64,1024]{1,0:T(8,128)(2,1)S(1)}, u32[]{:S(2)}, u32[]{:S(2)}) %collective-permute-start.5) | collective-permute-done | bytes 131104 | tf_op jit(solution)/shard_map/ppermute | solution.py:442
  77.0 0.0 copy-done
  77.0 0.0 copy-done.4
  77.0 0.0 copy-done.5
  77.0 2.5 %edge_clusters.1 = f32[512,1024]{1,0:T(8,128)} custom-call(s32[6]{0:T(128)S(1)} %copy-done.4, f32[512,1024]{1,0:T(8,128)} %get-tuple-element.33.moved_in, bf16[64,1024]{1,0:T(8,128)(2,1)S(1)} %collective-permute-done.4.inner_in, bf16[64,1024]{1,0:T(8,128)(2,1)S(1)} %collective-permute-done.5.outer_in, ...), custom_call_target="tpu_custom_call", output_to_operand_aliasing={{}: (1, {})} | custom-call | tf_op jit(solution)/shard_map/edge_clusters/pallas_call | solution.py:447
  79.5 0.0 all-to-all-done.1
  79.5 0.8 copy.15
  (1 shorter events, 0.0 us)
Async XLA Ops:
  0.6 5.5 %collective-permute-start.2 = (f32[4,256,128]{2,1,0:T(8,128)}, f32[4,256,128]{2,1,0:T(8,128)S(1)}, u32[]{:S(2)}, u32[]{:S(2)}) collective-permute-start(f32[4,256,128]{2,1,0:T(8,128)} %books_ref.1), channel_id=1, source_target_pairs={{0,1},{1,0},{2,3},{3,2},{4,5},{5,4},{6,7},{7,6},{8,9},{9,8},{10,11... | collective-permute-start | bytes 1572872 | tf_op jit(solution)/shard_map/ppermute | solution.py:403
  2.5 3.7 %collective-permute-start = (f32[64,1024]{1,0:T(8,128)S(1)}, f32[64,1024]{1,0:T(8,128)S(1)}, u32[]{:S(2)}, u32[]{:S(2)}) collective-permute-start(f32[64,1024]{1,0:T(8,128)S(1)} %get-tuple-element.42), channel_id=1, source_target_pairs={{0,1},{1,0},{2,3},{3,2},{4,5},{5,4},{6,7},{7,6},{8,9},{9,8},{10,11... | collective-permute-start | bytes 786440 | tf_op jit(solution)/shard_map/ppermute | solution.py:407
  2.6 12.8 %collective-permute-start.1 = (f32[64,1024]{1,0:T(8,128)S(1)}, f32[64,1024]{1,0:T(8,128)S(1)}, u32[]{:S(2)}, u32[]{:S(2)}) collective-permute-start(f32[64,1024]{1,0:T(8,128)S(1)} %get-tuple-element.41), channel_id=1, source_target_pairs={{1,2},{3,4},{5,6},{7,8},{9,10},{11,12},{13,14},{15,16},{17,18},{19... | collective-permute-start | bytes 786440 | tf_op jit(solution)/shard_map/ppermute | solution.py:406
  6.1 14.5 %copy-start.3 = (s32[6]{0:T(128)}, s32[6]{0:T(128)S(1)}, u32[]{:S(2)}) copy-start(s32[6]{0:T(128)S(1)} %stack.24.place_smem) | copy-start | bytes 76
  6.2 0.7 copy-start.1
  15.4 5.3 %copy-start.6 = (f32[4,256,128]{2,1,0:T(8,128)S(1)}, f32[4,256,128]{2,1,0:T(8,128)}, u32[]{:S(2)}) copy-start(f32[4,256,128]{2,1,0:T(8,128)} %books_ref.1) | copy-start | bytes 1572868
  15.4 5.3 %copy-start.2 = (s32[2048]{0:T(1024)S(1)}, s32[2048]{0:T(1024)}, u32[]{:S(2)}) copy-start(s32[2048]{0:T(1024)} %ids_smem.7) | copy-start | bytes 24580
  20.7 10.2 %collective-permute-start.3 = (f32[64,24,128]{2,1,0:T(8,128)S(1)}, f32[64,24,128]{2,1,0:T(8,128)}, u32[]{:S(2)}, u32[]{:S(2)}) collective-permute-start(f32[64,24,128]{2,1,0:T(8,128)S(1)} %get-tuple-element.27), channel_id=1, source_target_pairs={{0,1},{1,0},{2,3},{3,2},{4,5},{5,4},{6,7},{7,6},{8,9},{9,8},{10,11... | collective-permute-start | bytes 2359304 | tf_op jit(solution)/shard_map/ppermute | solution.py:422
  32.9 21.2 %all-to-all-start = ((f32[64,24,128]{2,1,0:T(8,128)}), f32[64,24,128]{2,1,0:T(8,128)S(1)}, u32[]{:S(2)}, u32[]{:S(2)}) async-start(f32[64,24,128]{2,1,0:T(8,128)} %add.19), calls=%async_computation | async-start | bytes 1572864 | tf_op jit(solution)/shard_map/all_to_all | solution.py:431
  43.2 33.8 %copy-start = (f32[512,1024]{1,0:T(8,128)S(1)}, f32[512,1024]{1,0:T(8,128)}, u32[]{:S(2)}) copy-start(f32[512,1024]{1,0:T(8,128)} %cent_ref.9) | copy-start | bytes 6291460
  43.2 33.8 %copy-start.4 = (s32[6]{0:T(128)S(1)}, s32[6]{0:T(128)}, u32[]{:S(2)}) copy-start(s32[6]{0:T(128)} %copy-done.3) | copy-start | bytes 76
  43.2 33.8 %copy-start.5 = (s32[512]{0:T(512)S(1)}, s32[512]{0:T(512)}, u32[]{:S(2)}) copy-start(s32[512]{0:T(512)} %param.7) | copy-start | bytes 6148
  55.2 24.3 %all-to-all-start.1 = ((f32[64,16,128]{2,1,0:T(8,128)}), f32[64,16,128]{2,1,0:T(8,128)S(1)}, u32[]{:S(2)}, u32[]{:S(2)}) async-start(f32[64,16,128]{2,1,0:T(8,128)} %moved_codes.1), calls=%async_computation.1 | async-start | bytes 1048576 | tf_op jit(solution)/shard_map/all_to_all | solution.py:444
  63.9 5.4 %collective-permute-start.4 = (bf16[64,1024]{1,0:T(8,128)(2,1)}, bf16[64,1024]{1,0:T(8,128)(2,1)S(1)}, u32[]{:S(2)}, u32[]{:S(2)}) collective-permute-start(bf16[64,1024]{1,0:T(8,128)(2,1)} %get-tuple-element.38), channel_id=1, source_target_pairs={{0,1},{1,0},{2,3},{3,2},{4,5},{5,4},{6,7},{7,6},{8,9},{9,8},{10,11... | collective-permute-start | bytes 393224 | tf_op jit(solution)/shard_map/ppermute | solution.py:443
  66.3 10.7 %collective-permute-start.5 = (bf16[64,1024]{1,0:T(8,128)(2,1)}, bf16[64,1024]{1,0:T(8,128)(2,1)S(1)}, u32[]{:S(2)}, u32[]{:S(2)}) collective-permute-start(bf16[64,1024]{1,0:T(8,128)(2,1)} %get-tuple-element.39), channel_id=1, source_target_pairs={{1,2},{3,4},{5,6},{7,8},{9,10},{11,12},{13,14},{15,16},{17,18},{19... | collective-permute-start | bytes 393224 | tf_op jit(solution)/shard_map/ppermute | solution.py:442
